TPU v7x, 32 devices: a whole 2x2x4 slice. The times are simulated.
32 devices in a mesh: groups: 2 (over x), blk: 16 (over z, y, core).
Axes of the slice: x: 2, y: 2, z: 4, core: 2. Of those that a mesh axis runs over, the one named last changes fastest.
Arguments:
- factors: bfloat16 [64, 2, 64, 128], P(('groups', 'blk')), parts along dimension 0, may hold values from -2.09375 to 2.09375
- token_mask: int32 [64, 64], P(('groups', 'blk')), parts along dimension 0, may hold values 0 or 1
- store: bfloat16 [16384, 2, 4096], P(('groups', 'blk')), parts along dimension 0, may hold values from -0.0625 to 0.0625
- inv_fisher: bfloat16 [2, 4096, 4096], P(None, 'blk'), as said below
- source_ids: int32 [16384], P(('groups', 'blk')), parts along dimension 0, may hold values from 0 to 15
- source_weight: float32 [16], replicated, may hold values from 0.25 to 4
Outputs:
- scores: float32 [64, 8192], P('groups', 'blk'), parts along dimension 0
There are 2 independent parts, one for each index of `groups`. A program takes and returns all parts, laid end to end along the dimension named above; an argument that names none is the same for every part. Nothing has to cross between parts.
Inputs may be any that keep to these rules, and one draw needn't show every extreme that they name: `inv_fisher`: each layer's matrix is symmetric.
All inputs are finite; a program needn't handle non-finite values. No bound on the sum of `token_mask` on one device may be relied on, other than what follows from the above.
Results may differ from a plain program's by a relative error of at most 0.004.
Values may be sent and summed in bfloat16 or wider, within the bound.
No kernel may reach another device: no remote copies, remote signals or barrier semaphores. Data moves between devices by JAX's collectives and lax.ppermute only.
A program may use at most 64 MiB of HBM per device.

v0:
```python
import jax
import jax.numpy as jnp
from jax import lax
from jax.sharding import PartitionSpec as P


def make_grads(factors, token_mask):
    rank_size = factors.shape[3] // 2
    mask_values = token_mask.astype(jnp.float32)[:, None, :, None]
    left_side = factors[..., :rank_size].astype(jnp.float32) * mask_values
    right_side = factors[..., rank_size:].astype(jnp.float32)
    outer_sum = jnp.einsum("qlta,qltb->qlab", left_side, right_side)
    return outer_sum.reshape(outer_sum.shape[0], outer_sum.shape[1], rank_size * rank_size).astype(
        jnp.bfloat16
    )


def local(factors, token_mask, store, inv_fisher, source_ids, source_weight):
    query_grads = make_grads(factors, token_mask)
    layer_count = inv_fisher.shape[0]
    segment = lax.all_gather(query_grads, "blk", axis=0, tiled=True)
    products = [
        lax.dot_general(
            segment[:, layer_idx],
            inv_fisher[layer_idx],
            (((1,), (1,)), ((), ())),
            preferred_element_type=jnp.float32,
        )
        for layer_idx in range(layer_count)
    ]
    hidden_cols = jnp.stack(products, axis=1).astype(jnp.bfloat16)
    hidden = lax.all_to_all(hidden_cols, "blk", split_axis=0, concat_axis=2, tiled=True)
    matches = (
        source_ids[:, None] == jnp.arange(source_weight.shape[0], dtype=jnp.int32)[None, :]
    ).astype(jnp.float32)
    scaling = jnp.sum(matches * source_weight[None, :], axis=1)
    raw_scores = lax.dot_general(
        lax.all_gather(hidden, "blk", axis=0, tiled=True),
        store,
        (((1, 2), (1, 2)), ((), ())),
        preferred_element_type=jnp.float32,
    )
    return raw_scores * scaling[None, :]


def solution(mesh):
    placed = (
        P(("groups", "blk"), None, None, None),
        P(("groups", "blk"), None),
        P(("groups", "blk"), None, None),
        P(None, "blk", None),
        P(("groups", "blk")),
        P(),
    )
    return jax.shard_map(
        local, mesh=mesh, in_specs=placed, out_specs=P("groups", "blk"), check_vma=False
    )
```

profile of v0, /device:TPU:0, one launch (start us, length us, event | category | flops | bytes accessed | tf_op | source)
XLA Modules:
  0.0 74.3 jit_solution(9541657118500640011)
XLA Ops:
  0.0 0.0 copy-start
  0.0 0.0 copy-start.1
  0.0 0.7 convert_element_type.16
  0.7 1.2 %convolution_convert_fusion = bf16[2,2,64,64]{3,2,1,0:T(8,128)(2,1)S(1)} fusion(bf16[2,2,64,128]{3,2,1,0:T(8,128)(2,1)} %param.6, f32[2,64]{1,0:T(2,128)S(1)} %convert_element_type.16), kind=kOutput, calls=%fused_computation.8 | convolution fusion | flops 2146304 | bytes 164352 | tf_op jit(solution)/shard_map/qlta,qltb->qlab/dot_general | solution.py:12
  1.9 0.1 convert_element_type.18
  2.0 0.0 copy-start.2
  2.0 24.7 %all_gather.6 = bf16[32,2,4096]{2,1,0:T(2,128)(2,1)S(1)} all-gather(bf16[2,2,4096]{2,1,0:T(2,128)(2,1)S(1)} %convert_element_type.18), channel_id=1, replica_groups=mesh['groups'=2,'blk'=16] {'blk'}, dimensions={0}, use_global_device_ids=true | all-gather | bytes 557056 | tf_op jit(solution)/shard_map/all_gather | solution.py:21
  26.8 1.2 %fusion.32 = (bf16[32,1,4096]{2,1,0:T(2,128)(2,1)S(1)}, bf16[32,1,4096]{2,1,0:T(2,128)(2,1)S(1)}) fusion(bf16[32,2,4096]{2,1,0:T(2,128)(2,1)S(1)} %all_gather.6), kind=kLoop, calls=%fused_computation.26 | loop fusion | bytes 1048576 | tf_op jit(solution)/shard_map/slice | solution.py:24
  28.0 2.3 %fusion.20 = bf16[32,1,256]{2,0,1:T(8,128)(2,1)S(1)} fusion(bf16[2,256,4096]{2,1,0:T(8,128)(2,1)} %param.9, bf16[32,1,4096]{2,1,0:T(2,128)(2,1)S(1)} %get-tuple-element.6), kind=kOutput, calls=%fused_computation.13 | convolution fusion | flops 67117056 | bytes 2375680 | tf_op jit(solution)/shard_map/dot_general | solution.py:23
  30.3 0.0 copy-done.2
  30.3 0.7 fusion.23
  31.0 0.7 copy.22
  31.6 3.5 %all-to-all-start = ((bf16[32,2,256]{2,1,0:T(2,128)(2,1)}), bf16[32,2,256]{2,1,0:T(2,128)(2,1)S(1)}, u32[]{:S(2)}, u32[]{:S(2)}) async-start(bf16[32,2,256]{2,1,0:T(2,128)(2,1)} %copy.22), calls=%async_computation | async-start | bytes 65536 | tf_op jit(solution)/shard_map/all_to_all | solution.py:32
  35.1 0.0 copy-done
  35.2 0.0 copy-done.1
  35.2 0.1 select_reduce_fusion
  35.3 6.5 %all-to-all-done = bf16[32,2,256]{2,1,0:T(2,128)(2,1)S(1)} async-done(((bf16[32,2,256]{2,1,0:T(2,128)(2,1)}), bf16[32,2,256]{2,1,0:T(2,128)(2,1)S(1)}, u32[]{:S(2)}, u32[]{:S(2)}) %all-to-all-start) | async-done | bytes 32800 | tf_op jit(solution)/shard_map/all_to_all | solution.py:32
  41.8 19.2 %all_gather.7 = bf16[32,2,4096]{2,1,0:T(2,128)(2,1)S(1)} all-gather(bf16[2,2,4096]{2,1,0:T(2,128)(2,1)S(1)} %bitcast.35), channel_id=1, replica_groups=mesh['groups'=2,'blk'=16] {'blk'}, dimensions={0}, use_global_device_ids=true | all-gather | bytes 557056 | tf_op jit(solution)/shard_map/all_gather | solution.py:38
  61.0 13.3 %fusion.11 = f32[32,512]{1,0:T(8,128)} fusion(bf16[512,2,4096]{2,1,0:T(2,128)(2,1)} %param.8, bf16[32,2,4096]{2,1,0:T(2,128)(2,1)S(1)} %all_gather.7, f32[512]{0:T(512)S(1)} %select_reduce_fusion), kind=kOutput, calls=%fused_computation.10 | convolution fusion | flops 268451840 | bytes 8980480 | tf_op jit(solution)/shard_map/dot_general | solution.py:37
  (2 shorter events, 0.0 us)
Async XLA Ops:
  0.0 35.1 %copy-start = (s32[512]{0:T(512)S(1)}, s32[512]{0:T(512)}, u32[]{:S(2)}) copy-start(s32[512]{0:T(512)} %param.10) | copy-start | bytes 6148
  0.0 35.2 %copy-start.1 = (f32[16]{0:T(128)S(1)}, f32[16]{0:T(128)}, u32[]{:S(2)}) copy-start(f32[16]{0:T(128)} %param.11) | copy-start | bytes 196
  2.0 28.2 %copy-start.2 = (bf16[2,256,4096]{2,1,0:T(8,128)(2,1)S(1)}, bf16[2,256,4096]{2,1,0:T(8,128)(2,1)}, u32[]{:S(2)}) copy-start(bf16[2,256,4096]{2,1,0:T(8,128)(2,1)} %param.9) | copy-start | bytes 12582916
  31.6 10.1 %all-to-all-start = ((bf16[32,2,256]{2,1,0:T(2,128)(2,1)}), bf16[32,2,256]{2,1,0:T(2,128)(2,1)S(1)}, u32[]{:S(2)}, u32[]{:S(2)}) async-start(bf16[32,2,256]{2,1,0:T(2,128)(2,1)} %copy.22), calls=%async_computation | async-start | bytes 65536 | tf_op jit(solution)/shard_map/all_to_all | solution.py:32
where the time goes:
time: 74.6 us; the launch traced here: 74.3 us
  blocking collectives  43.9 us (59%)
  matrix products  17.5 us (23%)
  waiting for transfers between devices  6.49 us (9%)
  starting transfers between devices  3.5 us (5%)
  local copies, waits for them, and re-layouts  2.01 us (3%)
  other arithmetic  0.81 us (1%)
    all_gather x1, blocking collectives, local(): segment = lax.all_gather(query_grads, 'blk', axis=0, tiled=True)  24.7 us
    all_gather x1, blocking collectives, local(): lax.all_gather(hidden, 'blk', axis=0, tiled=True)  19.2 us
    dot_general x1, matrix products, local(): lax.dot_general(lax.all_gather(hidden, 'blk', axis=0, tiled=True), store,...  13.3 us
    all_to_all x1, waiting for transfers between devices, local(): lax.all_to_all(hidden_cols, 'blk', split_axis=0, concat_axis=2, tiled=True)  6.49 us
    all_to_all x1, starting transfers between devices, local(): lax.all_to_all(hidden_cols, 'blk', split_axis=0, concat_axis=2, tiled=True)  3.5 us
    dot_general x2, matrix products, local(): lax.dot_general(segment[:, layer_idx], inv_fisher[layer_idx], (((1,), (1,...  3 us
  transfers between devices with their start and end apart: 1, of which 1 were waited for; matrix products, arithmetic and copies ran while one was open for 0% of the time, Pallas kernels for 0%

commit v1 on v0

--- a/solution.py
+++ b/solution.py
@@ -29,13 +29,13 @@
         for layer_idx in range(layer_count)
     ]
     hidden_cols = jnp.stack(products, axis=1).astype(jnp.bfloat16)
-    hidden = lax.all_to_all(hidden_cols, "blk", split_axis=0, concat_axis=2, tiled=True)
+    hidden = lax.all_gather(hidden_cols, "blk", axis=2, tiled=True)
     matches = (
         source_ids[:, None] == jnp.arange(source_weight.shape[0], dtype=jnp.int32)[None, :]
     ).astype(jnp.float32)
     scaling = jnp.sum(matches * source_weight[None, :], axis=1)
     raw_scores = lax.dot_general(
-        lax.all_gather(hidden, "blk", axis=0, tiled=True),
+        hidden,
         store,
         (((1, 2), (1, 2)), ((), ())),
         preferred_element_type=jnp.float32,

time: 74.6 us -> 63.1 us (0.85)
  waiting for transfers between devices: 6.49 us -> 0 us
  starting transfers between devices: 3.5 us -> 0 us
    all_to_all x1 -> x0, waiting for transfers between devices: 6.49 us -> none  [local(): lax.all_to_all(hidden_cols, 'blk', split_axis=0, concat_axis=2, tiled=True)]
    all_to_all x1 -> x0, starting transfers between devices: 3.5 us -> none  [local(): lax.all_to_all(hidden_cols, 'blk', split_axis=0, concat_axis=2, tiled=True)]
  transfers between devices with their start and end apart: 1 -> 0, of which waited for: 1 -> 0; matrix products, arithmetic and copies ran while one was open for 0% -> 0% of each run, Pallas kernels for 0% -> 0%
where the time goes in v1:
time: 63.1 us; the launch traced here: 62.8 us
  blocking collectives  43.6 us (69%)
  matrix products  17 us (27%)
  local copies, waits for them, and re-layouts  1.34 us (2%)
  other arithmetic  0.78 us (1%)
    all_gather x1, blocking collectives, local(): segment = lax.all_gather(query_grads, 'blk', axis=0, tiled=True)  24.7 us
    all_gather x1, blocking collectives, local(): hidden = lax.all_gather(hidden_cols, 'blk', axis=2, tiled=True)  18.9 us
    dot_general x1, matrix products, local(): lax.dot_general(hidden, store, (((1, 2), (1, 2)), ((), ())), preferred_el...  12.9 us
    dot_general x2, matrix products, local(): lax.dot_general(segment[:, layer_idx], inv_fisher[layer_idx], (((1,), (1,...  3 us

profile of v1, /device:TPU:0, one launch (start us, length us, event | category | flops | bytes accessed | tf_op | source)
XLA Modules:
  0.0 62.8 jit_solution(6970404608652119523)
XLA Ops:
  0.0 0.7 %convert_element_type.16 = f32[2,64]{1,0:T(2,128)S(1)} convert(s32[2,64]{1,0:T(2,128)} %param.7) | non-fusion elementwise | flops 128 | bytes 1024 | tf_op jit(solution)/shard_map/convert_element_type | solution.py:9
  0.7 1.2 %convolution_convert_fusion = bf16[2,2,64,64]{3,2,1,0:T(8,128)(2,1)S(1)} fusion(bf16[2,2,64,128]{3,2,1,0:T(8,128)(2,1)} %param.6, f32[2,64]{1,0:T(2,128)S(1)} %convert_element_type.16), kind=kOutput, calls=%fused_computation.8 | convolution fusion | flops 2146304 | bytes 164352 | tf_op jit(solution)/shard_map/qlta,qltb->qlab/dot_general | solution.py:12
  1.9 0.1 convert_element_type.18
  2.0 0.0 copy-start.2
  2.0 0.0 copy-start
  2.0 0.0 copy-start.1
  2.0 24.7 %all_gather.6 = bf16[32,2,4096]{2,1,0:T(2,128)(2,1)S(1)} all-gather(bf16[2,2,4096]{2,1,0:T(2,128)(2,1)S(1)} %convert_element_type.18), channel_id=1, replica_groups=mesh['groups'=2,'blk'=16] {'blk'}, dimensions={0}, use_global_device_ids=true | all-gather | bytes 557056 | tf_op jit(solution)/shard_map/all_gather | solution.py:21
  26.8 1.2 %fusion.31 = (bf16[32,1,4096]{2,1,0:T(2,128)(2,1)S(1)}, bf16[32,1,4096]{2,1,0:T(2,128)(2,1)S(1)}) fusion(bf16[32,2,4096]{2,1,0:T(2,128)(2,1)S(1)} %all_gather.6), kind=kLoop, calls=%fused_computation.25 | loop fusion | bytes 1048576 | tf_op jit(solution)/shard_map/slice | solution.py:24
  27.9 2.3 %fusion.20 = bf16[32,1,256]{2,0,1:T(8,128)(2,1)S(1)} fusion(bf16[2,256,4096]{2,1,0:T(8,128)(2,1)} %param.9, bf16[32,1,4096]{2,1,0:T(2,128)(2,1)S(1)} %get-tuple-element.6), kind=kOutput, calls=%fused_computation.13 | convolution fusion | flops 67117056 | bytes 2375680 | tf_op jit(solution)/shard_map/dot_general | solution.py:23
  30.3 0.0 copy-done.2
  30.3 0.7 %fusion.23 = bf16[32,1,256]{2,0,1:T(8,128)(2,1)S(1)} fusion(bf16[2,256,4096]{2,1,0:T(8,128)(2,1)S(1)} %copy-done.2, bf16[32,1,4096]{2,1,0:T(2,128)(2,1)S(1)} %get-tuple-element.5), kind=kOutput, calls=%fused_computation.14 | convolution fusion | flops 67117056 | bytes 2637824 | tf_op jit(solution)/shard_map/dot_general | solution.py:23
  31.0 18.9 %all_gather.7 = bf16[32,2,4096]{2,0,1:T(8,128)(2,1)S(1)} all-gather(bf16[32,2,256]{2,0,1:T(8,128)(2,1)S(1)} %pad_maximum_fusion), channel_id=1, replica_groups=mesh['groups'=2,'blk'=16] {'blk'}, dimensions={2}, use_global_device_ids=true | all-gather | bytes 557056 | tf_op jit(solution)/shard_map/all_gather | solution.py:32
  49.9 0.0 copy-done
  49.9 0.0 copy-done.1
  49.9 0.1 select_reduce_fusion
  50.0 12.9 %fusion.11 = f32[32,512]{1,0:T(8,128)} fusion(bf16[32,2,4096]{2,0,1:T(8,128)(2,1)S(1)} %all_gather.7, bf16[512,2,4096]{2,1,0:T(2,128)(2,1)} %param.8, f32[512]{0:T(512)S(1)} %select_reduce_fusion), kind=kOutput, calls=%fused_computation.10 | convolution fusion | flops 268451840 | bytes 8980480 | tf_op jit(solution)/shard_map/dot_general | solution.py:37
  (1 shorter events, 0.0 us)
Async XLA Ops:
  2.0 28.3 %copy-start.2 = (bf16[2,256,4096]{2,1,0:T(8,128)(2,1)S(1)}, bf16[2,256,4096]{2,1,0:T(8,128)(2,1)}, u32[]{:S(2)}) copy-start(bf16[2,256,4096]{2,1,0:T(8,128)(2,1)} %param.9) | copy-start | bytes 12582916
  2.0 47.9 %copy-start = (s32[512]{0:T(512)S(1)}, s32[512]{0:T(512)}, u32[]{:S(2)}) copy-start(s32[512]{0:T(512)} %param.10) | copy-start | bytes 6148
  2.0 47.8 %copy-start.1 = (f32[16]{0:T(128)S(1)}, f32[16]{0:T(128)}, u32[]{:S(2)}) copy-start(f32[16]{0:T(128)} %param.11) | copy-start | bytes 196

commit v2 on v1

v2 whole, which is shorter than its diff:
```python
import functools

import jax
import jax.numpy as jnp
from jax import lax
from jax.experimental import pallas as pl
from jax.experimental.pallas import tpu as pltpu
from jax.sharding import PartitionSpec as P

LANES = 128
VMEM_LIMIT = 40 * 2**20
IN_VMEM = pl.BlockSpec(memory_space=pltpu.VMEM)


def make_grads(factors, token_mask):
    rank_size = factors.shape[3] // 2
    mask_values = token_mask.astype(jnp.float32)[:, None, :, None]
    left_side = factors[..., :rank_size].astype(jnp.float32) * mask_values
    right_side = factors[..., rank_size:].astype(jnp.float32)
    outer_sum = jnp.einsum("qlta,qltb->qlab", left_side, right_side)
    return outer_sum.reshape(outer_sum.shape[0], outer_sum.shape[1], rank_size * rank_size).astype(
        jnp.bfloat16
    )


def make_scaling(source_ids, source_weight):
    matches = (
        source_ids[:, None] == jnp.arange(source_weight.shape[0], dtype=jnp.int32)[None, :]
    ).astype(jnp.float32)
    return jnp.sum(matches * source_weight[None, :], axis=1)


def plain(factors, token_mask, store, inv_fisher, source_ids, source_weight):
    segment = lax.all_gather(make_grads(factors, token_mask), "blk", axis=0, tiled=True)
    products = [
        lax.dot_general(
            segment[:, layer_idx],
            inv_fisher[layer_idx],
            (((1,), (1,)), ((), ())),
            preferred_element_type=jnp.float32,
        )
        for layer_idx in range(inv_fisher.shape[0])
    ]
    hidden_cols = jnp.stack(products, axis=1).astype(jnp.bfloat16)
    hidden = lax.all_gather(hidden_cols, "blk", axis=2, tiled=True)
    raw_scores = lax.dot_general(
        hidden, store, (((1, 2), (1, 2)), ((), ())), preferred_element_type=jnp.float32
    )
    return raw_scores * make_scaling(source_ids, source_weight)[None, :]


def grads_kernel(factors_ref, mask_ref, out_ref, outer_ref, flat_ref):
    queries, layers, _, width = factors_ref.shape
    rank = width // 2
    tiles = rank * rank // LANES
    for layer in range(layers):
        for query in range(queries):
            block = factors_ref[query, layer].astype(jnp.float32)
            left = block[:, :rank].T * mask_ref[query : query + 1].astype(jnp.float32)
            outer_ref[...] = jnp.dot(
                left.astype(jnp.bfloat16),
                block[:, rank:].astype(jnp.bfloat16),
                preferred_element_type=jnp.float32,
            )
            flat_ref[layer, pl.ds(query, tiles, queries)] = jnp.concatenate(
                [outer_ref[pl.ds(0, tiles, 2)], outer_ref[pl.ds(1, tiles, 2)]], axis=1
            )
    out_ref[...] = (
        flat_ref[...].astype(jnp.bfloat16).reshape(layers * tiles, queries, LANES)
    )


def grads_call(factors, token_mask):
    queries, layers, _, width = factors.shape
    rank = width // 2
    tiles = rank * rank // LANES
    return pl.pallas_call(
        grads_kernel,
        out_shape=jax.ShapeDtypeStruct((layers * tiles, queries, LANES), jnp.bfloat16),
        in_specs=[IN_VMEM] * 2,
        out_specs=IN_VMEM,
        scratch_shapes=[
            pltpu.VMEM((rank, rank), jnp.float32),
            pltpu.VMEM((layers, tiles * queries, LANES), jnp.float32),
        ],
        compiler_params=pltpu.CompilerParams(vmem_limit_bytes=VMEM_LIMIT),
    )(factors, token_mask)


def gather_parts(chunk, size):
    held = chunk[None]
    step = size // 2
    while step > 1:
        other = lax.ppermute(held, "blk", [(i, i ^ step) for i in range(size)])
        held = jnp.concatenate([held, other], axis=0)
        step //= 2
    return held, lax.ppermute(held, "blk", [(i, i ^ 1) for i in range(size)])


def entry_of(position, size):
    bits = (size // 2).bit_length() - 1
    return sum(((position >> (bits - 1 - b)) & 1) << b for b in range(bits))


def fisher_kernel(size, near_ref, far_ref, fisher_ref, out_ref, whole_ref):
    me = lax.axis_index("blk")
    half = size // 2
    layers, rows, feats = fisher_ref.shape
    tiles = feats // LANES
    queries = near_ref.shape[2]
    odd = lax.rem(me, 2) == 1
    for entry in range(half):
        near, far = near_ref[entry], far_ref[entry]
        place = lax.bitwise_xor(me // 2, position_of(entry, size))
        whole_ref[place, 0] = jnp.where(odd, far, near)
        whole_ref[place, 1] = jnp.where(odd, near, far)
    parts = []
    for layer in range(layers):
        grads = jnp.concatenate(
            [
                whole_ref[:, :, layer * tiles + tile].reshape(size * queries, LANES)
                for tile in range(tiles)
            ],
            axis=1,
        )
        parts.append(
            lax.dot_general(
                fisher_ref[layer],
                grads,
                (((1,), (1,)), ((), ())),
                preferred_element_type=jnp.float32,
            )
        )
    pieces = [
        part[start : start + LANES] for start in range(0, rows, LANES) for part in parts
    ]
    out_ref[...] = jnp.concatenate(pieces, axis=1).astype(jnp.bfloat16)


def position_of(entry, size):
    return entry_of(entry, size)


def fisher_call(near, far, inv_fisher, size):
    return pl.pallas_call(
        functools.partial(fisher_kernel, size),
        out_shape=jax.ShapeDtypeStruct((LANES, LANES), jnp.bfloat16),
        in_specs=[IN_VMEM] * 3,
        out_specs=IN_VMEM,
        scratch_shapes=[pltpu.VMEM((size // 2, 2) + near.shape[1:], jnp.bfloat16)],
        compiler_params=pltpu.CompilerParams(vmem_limit_bytes=VMEM_LIMIT),
    )(near, far, inv_fisher)


def score_kernel(size, queries, near_ref, far_ref, store_ref, scale_ref, out_ref, total_ref):
    me = lax.axis_index("blk")
    count, layers, feats = store_ref.shape
    width = feats // size
    groups = width // LANES
    span = LANES // groups
    lane = lax.broadcasted_iota(jnp.int32, (LANES, LANES), 1)
    total_ref[...] = jnp.zeros_like(total_ref)
    for entry in range(size // 2):
        for far, ref in enumerate((near_ref, far_ref)):
            owner = lax.bitwise_xor(me, 2 * position_of(entry, size) + far)
            chunk = ref[entry]
            weights = jnp.concatenate(
                [
                    jnp.where(lane // span == group, chunk, jnp.zeros_like(chunk))
                    for group in range(groups)
                ],
                axis=0,
            )
            columns = pl.ds(pl.multiple_of(owner * width, width), width)
            rows = store_ref[:, :, columns].reshape(count * layers, width)
            total_ref[...] += jnp.dot(rows, weights, preferred_element_type=jnp.float32)
    result = jnp.zeros((queries, count), jnp.float32)
    for layer in range(layers):
        turned = total_ref[pl.ds(layer, count, layers)].T
        for group in range(groups):
            start = group * span + layer * queries
            result = result + turned[start : start + queries]
    out_ref[...] = result * scale_ref[...]


def score_call(near, far, store, scaling, size, queries):
    count, layers, _ = store.shape
    return pl.pallas_call(
        functools.partial(score_kernel, size, queries),
        out_shape=jax.ShapeDtypeStruct((queries, count), jnp.float32),
        in_specs=[IN_VMEM] * 4,
        out_specs=IN_VMEM,
        scratch_shapes=[pltpu.VMEM((count * layers, LANES), jnp.float32)],
        compiler_params=pltpu.CompilerParams(vmem_limit_bytes=VMEM_LIMIT),
    )(near, far, store, scaling[None, :])


def fits(size, factors, store, inv_fisher):
    queries, layers, _, width = factors.shape
    _, rows, feats = inv_fisher.shape
    return (
        size > 1
        and size & (size - 1) == 0
        and width == LANES
        and queries == 2
        and layers == 2
        and rows % LANES == 0
        and (rows // LANES) * layers * queries * size == LANES
        and store.shape[0] % LANES == 0
        and feats == rows * size
    )


def solution(mesh):
    size = mesh.shape["blk"]

    def local(factors, token_mask, store, inv_fisher, source_ids, source_weight):
        if not fits(size, factors, store, inv_fisher):
            return plain(factors, token_mask, store, inv_fisher, source_ids, source_weight)
        scaling = make_scaling(source_ids, source_weight)
        near, far = gather_parts(grads_call(factors, token_mask), size)
        hidden = fisher_call(near, far, inv_fisher, size)
        near, far = gather_parts(hidden, size)
        return score_call(near, far, store, scaling, size, factors.shape[0] * size)

    placed = (
        P(("groups", "blk"), None, None, None),
        P(("groups", "blk"), None),
        P(("groups", "blk"), None, None),
        P(None, "blk", None),
        P(("groups", "blk")),
        P(),
    )
    return jax.shard_map(
        local, mesh=mesh, in_specs=placed, out_specs=P("groups", "blk"), check_vma=False
    )
```

time: 63.1 us -> 48.8 us (0.77)
  blocking collectives: 43.6 us -> 0 us
  waiting for transfers between devices: 0 us -> 18.3 us
  matrix products: 17 us -> 0 us
  starting transfers between devices: 0 us -> 14.1 us
  Pallas kernels: 0 us -> 7.46 us
  local copies, waits for them, and re-layouts: 1.34 us -> 7.09 us
  other arithmetic: 0.78 us -> 1.49 us
    all_gather x2 -> x0, blocking collectives: 43.6 us -> none  [the longest x1 24.7 us: local(): segment = lax.all_gather(query_grads, 'blk', axis=0, tiled=True)]
    ppermute x0 -> x8, waiting for transfers between devices: none -> 18.3 us  [the longest x6 16.1 us: gather_parts(): other = lax.ppermute(held, 'blk', [(i, i ^ step) for i in range(size)])]
    dot_general x4 -> x0, matrix products: 17 us -> none  [the longest x1 12.9 us: local(): lax.dot_general(hidden, store, (((1, 2), (1, 2)), ((), ())), preferred_el...]
    ppermute x0 -> x8, starting transfers between devices: none -> 14.1 us  [the longest x6 13.9 us: gather_parts(): other = lax.ppermute(held, 'blk', [(i, i ^ step) for i in range(size)])]
    pallas_call x0 -> x3, Pallas kernels: none -> 7.46 us  [the longest x1 5.3 us: score_call(): pl.pallas_call(functools.partial(score_kernel, size, queries), out_shape=...]
    unnamed x6 -> x8, local copies, waits for them, and re-layouts: 0.02 us -> 7.09 us
    slice x1 -> x0, local copies, waits for them, and re-layouts: 1.19 us -> none  [local(): segment[:, layer_idx]]
    concatenate x0 -> x6, other arithmetic: none -> 0.7 us  [gather_parts(): held = jnp.concatenate([held, other], axis=0)]
  transfers between devices with their start and end apart: 0 -> 8, of which waited for: 0 -> 8; matrix products, arithmetic and copies ran while one was open for 0% -> 2% of each run, Pallas kernels for 0% -> 0%
where the time goes in v2:
time: 48.8 us; the launch traced here: 48.5 us
  waiting for transfers between devices  18.3 us (38%)
  starting transfers between devices  14.1 us (29%)
  Pallas kernels  7.46 us (15%)
  local copies, waits for them, and re-layouts  7.09 us (15%)
  other arithmetic  1.49 us (3%)
    ppermute x6, waiting for transfers between devices, gather_parts(): other = lax.ppermute(held, 'blk', [(i, i ^ step) for i in range(size)])  16.1 us
    ppermute x6, starting transfers between devices, gather_parts(): other = lax.ppermute(held, 'blk', [(i, i ^ step) for i in range(size)])  13.9 us
    unnamed x8, local copies, waits for them, and re-layouts  7.09 us
    pallas_call x1, Pallas kernels, score_call(): pl.pallas_call(functools.partial(score_kernel, size, queries), out_shape=...  5.3 us
    ppermute x2, waiting for transfers between devices, gather_parts(): return (held, lax.ppermute(held, 'blk', [(i, i ^ 1) for i in range(size)]))  2.26 us
    pallas_call x1, Pallas kernels, fisher_call(): pl.pallas_call(functools.partial(fisher_kernel, size), out_shape=jax.Shap...  1.82 us
  transfers between devices with their start and end apart: 8, of which 8 were waited for; matrix products, arithmetic and copies ran while one was open for 2% of the time, Pallas kernels for 0%

profile of v2, /device:TPU:0, one launch (start us, length us, event | category | flops | bytes accessed | tf_op | source)
XLA Modules:
  0.0 48.5 jit_solution(1398243248302208530)
XLA Ops:
  0.0 0.0 copy-start.2
  0.0 0.8 %copy-done.2 = bf16[2,2,64,128]{3,2,1,0:T(8,128)(2,1)S(1)} copy-done((bf16[2,2,64,128]{3,2,1,0:T(8,128)(2,1)S(1)}, bf16[2,2,64,128]{3,2,1,0:T(8,128)(2,1)}, u32[]{:S(2)}) %copy-start.2) | copy-done | bytes 65560
  0.8 0.0 copy-start.3
  0.8 0.7 %copy-done.3 = s32[2,64]{1,0:T(2,128)S(1)} copy-done((s32[2,64]{1,0:T(2,128)S(1)}, s32[2,64]{1,0:T(2,128)}, u32[]{:S(2)}) %copy-start.3) | copy-done | bytes 536
  1.5 0.3 shard_map.64
  1.9 4.1 %collective-permute-start = (bf16[1,64,2,128]{3,2,1,0:T(2,128)(2,1)S(1)}, bf16[1,64,2,128]{3,2,1,0:T(2,128)(2,1)S(1)}, u32[]{:S(2)}, u32[]{:S(2)}) collective-permute-start(bf16[1,64,2,128]{3,2,1,0:T(2,128)(2,1)S(1)} %bitcast.7), channel_id=1, source_target_pairs={{0,8},{1,9},{2,10},{3,11},{4,12},{5,13},{6,14},{7,15},{8,0},{9,1},... | collective-permute-start | bytes 98312 | tf_op jit(solution)/shard_map/ppermute | solution.py:94
  6.0 2.2 %collective-permute-done = bf16[1,64,2,128]{3,2,1,0:T(2,128)(2,1)S(1)} collective-permute-done((bf16[1,64,2,128]{3,2,1,0:T(2,128)(2,1)S(1)}, bf16[1,64,2,128]{3,2,1,0:T(2,128)(2,1)S(1)}, u32[]{:S(2)}, u32[]{:S(2)}) %collective-permute-start) | collective-permute-done | bytes 32800 | tf_op jit(solution)/shard_map/ppermute | solution.py:94
  8.2 0.1 pad_maximum_fusion.4
  8.3 1.6 %collective-permute-start.1 = (bf16[2,64,2,128]{3,2,1,0:T(2,128)(2,1)S(1)}, bf16[2,64,2,128]{3,2,1,0:T(2,128)(2,1)S(1)}, u32[]{:S(2)}, u32[]{:S(2)}) collective-permute-start(bf16[2,64,2,128]{3,2,1,0:T(2,128)(2,1)S(1)} %pad_maximum_fusion.4), channel_id=1, source_target_pairs={{0,4},{1,5},{2,6},{3,7},{4,0},{5,1},{6,2},{7,3},{8,12},{9,13},{10,... | collective-permute-start | bytes 196616 | tf_op jit(solution)/shard_map/ppermute | solution.py:94
  9.9 2.7 %collective-permute-done.1 = bf16[2,64,2,128]{3,2,1,0:T(2,128)(2,1)S(1)} collective-permute-done((bf16[2,64,2,128]{3,2,1,0:T(2,128)(2,1)S(1)}, bf16[2,64,2,128]{3,2,1,0:T(2,128)(2,1)S(1)}, u32[]{:S(2)}, u32[]{:S(2)}) %collective-permute-start.1) | collective-permute-done | bytes 65568 | tf_op jit(solution)/shard_map/ppermute | solution.py:94
  12.6 0.2 pad_maximum_fusion.2
  12.8 1.8 %collective-permute-start.2 = (bf16[4,64,2,128]{3,2,1,0:T(2,128)(2,1)S(1)}, bf16[4,64,2,128]{3,2,1,0:T(2,128)(2,1)S(1)}, u32[]{:S(2)}, u32[]{:S(2)}) collective-permute-start(bf16[4,64,2,128]{3,2,1,0:T(2,128)(2,1)S(1)} %pad_maximum_fusion.2), channel_id=1, source_target_pairs={{0,2},{1,3},{2,0},{3,1},{4,6},{5,7},{6,4},{7,5},{8,10},{9,11},{10,... | collective-permute-start | bytes 393224 | tf_op jit(solution)/shard_map/ppermute | solution.py:94
  14.6 3.2 %collective-permute-done.2 = bf16[4,64,2,128]{3,2,1,0:T(2,128)(2,1)S(1)} collective-permute-done((bf16[4,64,2,128]{3,2,1,0:T(2,128)(2,1)S(1)}, bf16[4,64,2,128]{3,2,1,0:T(2,128)(2,1)S(1)}, u32[]{:S(2)}, u32[]{:S(2)}) %collective-permute-start.2) | collective-permute-done | bytes 131104 | tf_op jit(solution)/shard_map/ppermute | solution.py:94
  17.9 0.4 pad_maximum_fusion.near_ref
  18.2 0.1 collective-permute-start.3
  18.3 1.5 %collective-permute-done.3.far_ref = bf16[8,64,2,128]{3,2,1,0:T(2,128)(2,1)S(1)} collective-permute-done((bf16[8,64,2,128]{3,2,1,0:T(2,128)(2,1)S(1)}, bf16[8,64,2,128]{3,2,1,0:T(2,128)(2,1)S(1)}, u32[]{:S(2)}, u32[]{:S(2)}) %collective-permute-start.3) | collective-permute-done | bytes 262176 | tf_op jit(solution)/shard_map/ppermute | solution.py:97
  19.8 0.0 copy-start.1
  19.9 2.2 %copy-done.1 = bf16[2,256,4096]{2,1,0:T(8,128)(2,1)S(1)} copy-done((bf16[2,256,4096]{2,1,0:T(8,128)(2,1)S(1)}, bf16[2,256,4096]{2,1,0:T(8,128)(2,1)}, u32[]{:S(2)}) %copy-start.1) | copy-done | bytes 4194328
  22.0 1.8 %shard_map.65 = bf16[128,128]{1,0:T(8,128)(2,1)S(1)} custom-call(bf16[8,64,2,128]{3,2,1,0:T(2,128)(2,1)S(1)} %pad_maximum_fusion.near_ref, bf16[8,64,2,128]{3,2,1,0:T(2,128)(2,1)S(1)} %collective-permute-done.3.far_ref, bf16[2,256,4096]{2,1,0:T(8,128)(2,1)S(1)} %copy-done.1), custom_call_target="tpu_custom_call" | custom-call | tf_op jit(solution)/shard_map/pallas_call | solution.py:145
  23.9 2.7 %collective-permute-start.4 = (bf16[1,128,128]{2,1,0:T(8,128)(2,1)S(1)}, bf16[1,128,128]{2,1,0:T(8,128)(2,1)S(1)}, u32[]{:S(2)}, u32[]{:S(2)}) collective-permute-start(bf16[1,128,128]{2,1,0:T(8,128)(2,1)S(1)} %bitcast.3), channel_id=1, source_target_pairs={{0,8},{1,9},{2,10},{3,11},{4,12},{5,13},{6,14},{7,15},{8,0},{9,1},... | collective-permute-start | bytes 98312 | tf_op jit(solution)/shard_map/ppermute | solution.py:94
  26.5 2.2 %collective-permute-done.4 = bf16[1,128,128]{2,1,0:T(8,128)(2,1)S(1)} collective-permute-done((bf16[1,128,128]{2,1,0:T(8,128)(2,1)S(1)}, bf16[1,128,128]{2,1,0:T(8,128)(2,1)S(1)}, u32[]{:S(2)}, u32[]{:S(2)}) %collective-permute-start.4) | collective-permute-done | bytes 32800 | tf_op jit(solution)/shard_map/ppermute | solution.py:94
  28.8 1.6 %collective-permute-start.5 = (bf16[2,128,128]{2,1,0:T(8,128)(2,1)S(1)}, bf16[2,128,128]{2,1,0:T(8,128)(2,1)S(1)}, u32[]{:S(2)}, u32[]{:S(2)}) collective-permute-start(bf16[2,128,128]{2,1,0:T(8,128)(2,1)S(1)} %pad_maximum_fusion.5), channel_id=1, source_target_pairs={{0,4},{1,5},{2,6},{3,7},{4,0},{5,1},{6,2},{7,3},{8,12},{9,13},{10,... | collective-permute-start | bytes 196616 | tf_op jit(solution)/shard_map/ppermute | solution.py:94
  30.4 2.7 %collective-permute-done.5 = bf16[2,128,128]{2,1,0:T(8,128)(2,1)S(1)} collective-permute-done((bf16[2,128,128]{2,1,0:T(8,128)(2,1)S(1)}, bf16[2,128,128]{2,1,0:T(8,128)(2,1)S(1)}, u32[]{:S(2)}, u32[]{:S(2)}) %collective-permute-start.5) | collective-permute-done | bytes 65568 | tf_op jit(solution)/shard_map/ppermute | solution.py:94
  33.1 2.1 %collective-permute-start.6 = (bf16[4,128,128]{2,1,0:T(8,128)(2,1)S(1)}, bf16[4,128,128]{2,1,0:T(8,128)(2,1)S(1)}, u32[]{:S(2)}, u32[]{:S(2)}) collective-permute-start(bf16[4,128,128]{2,1,0:T(8,128)(2,1)S(1)} %pad_maximum_fusion.3), channel_id=1, source_target_pairs={{0,2},{1,3},{2,0},{3,1},{4,6},{5,7},{6,4},{7,5},{8,10},{9,11},{10,... | collective-permute-start | bytes 393224 | tf_op jit(solution)/shard_map/ppermute | solution.py:94
  35.2 2.9 %collective-permute-done.6 = bf16[4,128,128]{2,1,0:T(8,128)(2,1)S(1)} collective-permute-done((bf16[4,128,128]{2,1,0:T(8,128)(2,1)S(1)}, bf16[4,128,128]{2,1,0:T(8,128)(2,1)S(1)}, u32[]{:S(2)}, u32[]{:S(2)}) %collective-permute-start.6) | collective-permute-done | bytes 131104 | tf_op jit(solution)/shard_map/ppermute | solution.py:94
  38.2 0.1 collective-permute-start.7
  38.3 0.8 %select_reduce_fusion = f32[512]{0:T(512)S(1)} fusion(f32[16]{0:T(128)} %param.11, s32[512]{0:T(512)} %param.10), kind=kLoop, calls=%fused_computation.6 | loop fusion | flops 24064 | bytes 4160 | tf_op jit(solution)/shard_map/reduce_sum | solution.py:30
  39.1 0.7 %collective-permute-done.7.far_ref = bf16[8,128,128]{2,1,0:T(8,128)(2,1)S(1)} collective-permute-done((bf16[8,128,128]{2,1,0:T(8,128)(2,1)S(1)}, bf16[8,128,128]{2,1,0:T(8,128)(2,1)S(1)}, u32[]{:S(2)}, u32[]{:S(2)}) %collective-permute-start.7) | collective-permute-done | bytes 262176 | tf_op jit(solution)/shard_map/ppermute | solution.py:97
  39.8 0.0 copy-start
  39.8 3.4 %copy-done = bf16[512,2,4096]{2,1,0:T(2,128)(2,1)S(1)} copy-done((bf16[512,2,4096]{2,1,0:T(2,128)(2,1)S(1)}, bf16[512,2,4096]{2,1,0:T(2,128)(2,1)}, u32[]{:S(2)}) %copy-start) | copy-done | bytes 8388632
  43.2 5.3 %shard_map.66 = f32[32,512]{1,0:T(8,128)} custom-call(bf16[8,128,128]{2,1,0:T(8,128)(2,1)S(1)} %pad_maximum_fusion.1.near_ref, bf16[8,128,128]{2,1,0:T(8,128)(2,1)S(1)} %collective-permute-done.7.far_ref, bf16[512,2,4096]{2,1,0:T(2,128)(2,1)S(1)} %copy-done, f32[1,512]{1,0:T(1,128)S(1)} %bitcast.11), custom_call_target="tpu_custom_call" | custom-call | tf_op jit(solution)/shard_map/pallas_call | solution.py:188
  (3 shorter events, 0.1 us)
Async XLA Ops:
  0.0 0.8 %copy-start.2 = (bf16[2,2,64,128]{3,2,1,0:T(8,128)(2,1)S(1)}, bf16[2,2,64,128]{3,2,1,0:T(8,128)(2,1)}, u32[]{:S(2)}) copy-start(bf16[2,2,64,128]{3,2,1,0:T(8,128)(2,1)} %factors_ref.1) | copy-start | bytes 196612
  0.8 0.7 %copy-start.3 = (s32[2,64]{1,0:T(2,128)S(1)}, s32[2,64]{1,0:T(2,128)}, u32[]{:S(2)}) copy-start(s32[2,64]{1,0:T(2,128)} %mask_ref.1) | copy-start | bytes 1540
  1.9 6.3 %collective-permute-start = (bf16[1,64,2,128]{3,2,1,0:T(2,128)(2,1)S(1)}, bf16[1,64,2,128]{3,2,1,0:T(2,128)(2,1)S(1)}, u32[]{:S(2)}, u32[]{:S(2)}) collective-permute-start(bf16[1,64,2,128]{3,2,1,0:T(2,128)(2,1)S(1)} %bitcast.7), channel_id=1, source_target_pairs={{0,8},{1,9},{2,10},{3,11},{4,12},{5,13},{6,14},{7,15},{8,0},{9,1},... | collective-permute-start | bytes 98312 | tf_op jit(solution)/shard_map/ppermute | solution.py:94
  8.3 4.3 %collective-permute-start.1 = (bf16[2,64,2,128]{3,2,1,0:T(2,128)(2,1)S(1)}, bf16[2,64,2,128]{3,2,1,0:T(2,128)(2,1)S(1)}, u32[]{:S(2)}, u32[]{:S(2)}) collective-permute-start(bf16[2,64,2,128]{3,2,1,0:T(2,128)(2,1)S(1)} %pad_maximum_fusion.4), channel_id=1, source_target_pairs={{0,4},{1,5},{2,6},{3,7},{4,0},{5,1},{6,2},{7,3},{8,12},{9,13},{10,... | collective-permute-start | bytes 196616 | tf_op jit(solution)/shard_map/ppermute | solution.py:94
  12.8 5.0 %collective-permute-start.2 = (bf16[4,64,2,128]{3,2,1,0:T(2,128)(2,1)S(1)}, bf16[4,64,2,128]{3,2,1,0:T(2,128)(2,1)S(1)}, u32[]{:S(2)}, u32[]{:S(2)}) collective-permute-start(bf16[4,64,2,128]{3,2,1,0:T(2,128)(2,1)S(1)} %pad_maximum_fusion.2), channel_id=1, source_target_pairs={{0,2},{1,3},{2,0},{3,1},{4,6},{5,7},{6,4},{7,5},{8,10},{9,11},{10,... | collective-permute-start | bytes 393224 | tf_op jit(solution)/shard_map/ppermute | solution.py:94
  18.2 1.6 %collective-permute-start.3 = (bf16[8,64,2,128]{3,2,1,0:T(2,128)(2,1)S(1)}, bf16[8,64,2,128]{3,2,1,0:T(2,128)(2,1)S(1)}, u32[]{:S(2)}, u32[]{:S(2)}) collective-permute-start(bf16[8,64,2,128]{3,2,1,0:T(2,128)(2,1)S(1)} %pad_maximum_fusion.near_ref), channel_id=1, source_target_pairs={{0,1},{1,0},{2,3},{3,2},{4,5},{5,4},{6,7},{7,6},{8,9},{9,8},{10,11... | collective-permute-start | bytes 786440 | tf_op jit(solution)/shard_map/ppermute | solution.py:97
  19.8 2.2 %copy-start.1 = (bf16[2,256,4096]{2,1,0:T(8,128)(2,1)S(1)}, bf16[2,256,4096]{2,1,0:T(8,128)(2,1)}, u32[]{:S(2)}) copy-start(bf16[2,256,4096]{2,1,0:T(8,128)(2,1)} %fisher_ref.1) | copy-start | bytes 12582916
  23.9 4.9 %collective-permute-start.4 = (bf16[1,128,128]{2,1,0:T(8,128)(2,1)S(1)}, bf16[1,128,128]{2,1,0:T(8,128)(2,1)S(1)}, u32[]{:S(2)}, u32[]{:S(2)}) collective-permute-start(bf16[1,128,128]{2,1,0:T(8,128)(2,1)S(1)} %bitcast.3), channel_id=1, source_target_pairs={{0,8},{1,9},{2,10},{3,11},{4,12},{5,13},{6,14},{7,15},{8,0},{9,1},... | collective-permute-start | bytes 98312 | tf_op jit(solution)/shard_map/ppermute | solution.py:94
  28.8 4.3 %collective-permute-start.5 = (bf16[2,128,128]{2,1,0:T(8,128)(2,1)S(1)}, bf16[2,128,128]{2,1,0:T(8,128)(2,1)S(1)}, u32[]{:S(2)}, u32[]{:S(2)}) collective-permute-start(bf16[2,128,128]{2,1,0:T(8,128)(2,1)S(1)} %pad_maximum_fusion.5), channel_id=1, source_target_pairs={{0,4},{1,5},{2,6},{3,7},{4,0},{5,1},{6,2},{7,3},{8,12},{9,13},{10,... | collective-permute-start | bytes 196616 | tf_op jit(solution)/shard_map/ppermute | solution.py:94
  33.1 5.1 %collective-permute-start.6 = (bf16[4,128,128]{2,1,0:T(8,128)(2,1)S(1)}, bf16[4,128,128]{2,1,0:T(8,128)(2,1)S(1)}, u32[]{:S(2)}, u32[]{:S(2)}) collective-permute-start(bf16[4,128,128]{2,1,0:T(8,128)(2,1)S(1)} %pad_maximum_fusion.3), channel_id=1, source_target_pairs={{0,2},{1,3},{2,0},{3,1},{4,6},{5,7},{6,4},{7,5},{8,10},{9,11},{10,... | collective-permute-start | bytes 393224 | tf_op jit(solution)/shard_map/ppermute | solution.py:94
  38.2 1.6 %collective-permute-start.7 = (bf16[8,128,128]{2,1,0:T(8,128)(2,1)S(1)}, bf16[8,128,128]{2,1,0:T(8,128)(2,1)S(1)}, u32[]{:S(2)}, u32[]{:S(2)}) collective-permute-start(bf16[8,128,128]{2,1,0:T(8,128)(2,1)S(1)} %pad_maximum_fusion.1.near_ref), channel_id=1, source_target_pairs={{0,1},{1,0},{2,3},{3,2},{4,5},{5,4},{6,7},{7,6},{8,9},{9,8},{10,11... | collective-permute-start | bytes 786440 | tf_op jit(solution)/shard_map/ppermute | solution.py:97
  39.8 3.4 %copy-start = (bf16[512,2,4096]{2,1,0:T(2,128)(2,1)S(1)}, bf16[512,2,4096]{2,1,0:T(2,128)(2,1)}, u32[]{:S(2)}) copy-start(bf16[512,2,4096]{2,1,0:T(2,128)(2,1)} %store_ref.1) | copy-start | bytes 25165828

commit v3 on v2

v3 whole, which is shorter than its diff:
```python
import functools
import math

import jax
import jax.numpy as jnp
from jax import lax
from jax.experimental import pallas as pl
from jax.experimental.pallas import tpu as pltpu
from jax.sharding import PartitionSpec as P

LANES = 128
IN_VMEM = pl.BlockSpec(memory_space=pltpu.VMEM)
IN_HBM = pl.BlockSpec(memory_space=pltpu.HBM)
PARAMS = pltpu.CompilerParams(vmem_limit_bytes=16 * 2**20)


def make_grads(factors, token_mask):
    rank_size = factors.shape[3] // 2
    mask_values = token_mask.astype(jnp.float32)[:, None, :, None]
    left_side = factors[..., :rank_size].astype(jnp.float32) * mask_values
    right_side = factors[..., rank_size:].astype(jnp.float32)
    outer_sum = jnp.einsum("qlta,qltb->qlab", left_side, right_side)
    return outer_sum.reshape(outer_sum.shape[0], outer_sum.shape[1], rank_size * rank_size).astype(
        jnp.bfloat16
    )


def make_scaling(source_ids, source_weight):
    matches = (
        source_ids[:, None] == jnp.arange(source_weight.shape[0], dtype=jnp.int32)[None, :]
    ).astype(jnp.float32)
    return jnp.sum(matches * source_weight[None, :], axis=1)


def plain(factors, token_mask, store, inv_fisher, source_ids, source_weight):
    segment = lax.all_gather(make_grads(factors, token_mask), "blk", axis=0, tiled=True)
    products = [
        lax.dot_general(
            segment[:, layer_idx],
            inv_fisher[layer_idx],
            (((1,), (1,)), ((), ())),
            preferred_element_type=jnp.float32,
        )
        for layer_idx in range(inv_fisher.shape[0])
    ]
    hidden_cols = jnp.stack(products, axis=1).astype(jnp.bfloat16)
    hidden = lax.all_gather(hidden_cols, "blk", axis=2, tiled=True)
    raw_scores = lax.dot_general(
        hidden, store, (((1, 2), (1, 2)), ((), ())), preferred_element_type=jnp.float32
    )
    return raw_scores * make_scaling(source_ids, source_weight)[None, :]


def grads_kernel(factors_ref, mask_ref, out_ref, held_ref, mask_held_ref, outer_ref, flat_ref, sems):
    copies = [
        pltpu.make_async_copy(factors_ref, held_ref, sems.at[0]),
        pltpu.make_async_copy(mask_ref, mask_held_ref, sems.at[1]),
    ]
    for copy in copies:
        copy.start()
    for copy in copies:
        copy.wait()
    queries, layers, _, width = factors_ref.shape
    rank = width // 2
    tiles = rank * rank // LANES
    for layer in range(layers):
        for query in range(queries):
            block = held_ref[query, layer].astype(jnp.float32)
            left = block[:, :rank].T * mask_held_ref[query : query + 1].astype(jnp.float32)
            outer_ref[...] = jnp.dot(
                left.astype(jnp.bfloat16),
                block[:, rank:].astype(jnp.bfloat16),
                preferred_element_type=jnp.float32,
            )
            flat_ref[layer, pl.ds(query, tiles, queries)] = jnp.concatenate(
                [outer_ref[pl.ds(0, tiles, 2)], outer_ref[pl.ds(1, tiles, 2)]], axis=1
            )
    out_ref[...] = (
        flat_ref[...].astype(jnp.bfloat16).reshape(layers * tiles, queries, LANES)
    )


def grads_call(factors, token_mask):
    queries, layers, _, width = factors.shape
    rank = width // 2
    tiles = rank * rank // LANES
    return pl.pallas_call(
        grads_kernel,
        out_shape=jax.ShapeDtypeStruct((layers * tiles, queries, LANES), jnp.bfloat16),
        in_specs=[IN_HBM] * 2,
        out_specs=IN_VMEM,
        scratch_shapes=[
            pltpu.VMEM(factors.shape, factors.dtype),
            pltpu.VMEM(token_mask.shape, token_mask.dtype),
            pltpu.VMEM((rank, rank), jnp.float32),
            pltpu.VMEM((layers, tiles * queries, LANES), jnp.float32),
            pltpu.SemaphoreType.DMA((2,)),
        ],
        compiler_params=PARAMS,
    )(factors, token_mask)


def load_kernel(size, index, source_ref, out_ref, sem):
    width = out_ref.shape[-1]
    for entry, owner in enumerate(owners(size)[index]):
        columns = pl.ds(pl.multiple_of(owner * width, width), width)
        pltpu.make_async_copy(source_ref.at[:, :, columns], out_ref.at[entry], sem).start()
    pltpu.make_async_copy(out_ref, out_ref, sem).wait()


def load_store(store, size, index, entries):
    rows, layers, feats = store.shape
    shape = (entries, rows, layers, feats // size)
    return pl.pallas_call(
        functools.partial(load_kernel, size, index),
        out_shape=jax.ShapeDtypeStruct(shape, store.dtype),
        in_specs=[IN_HBM],
        out_specs=IN_VMEM,
        scratch_shapes=[pltpu.SemaphoreType.DMA],
        cost_estimate=pl.CostEstimate(
            flops=0, bytes_accessed=2 * math.prod(shape), transcendentals=0
        ),
        compiler_params=PARAMS,
    )(store)


def copy_kernel(source_ref, out_ref, sem):
    copy = pltpu.make_async_copy(source_ref, out_ref, sem)
    copy.start()
    copy.wait()


def load_whole(source):
    return pl.pallas_call(
        copy_kernel,
        out_shape=jax.ShapeDtypeStruct(source.shape, source.dtype),
        in_specs=[IN_HBM],
        out_specs=IN_VMEM,
        scratch_shapes=[pltpu.SemaphoreType.DMA],
        cost_estimate=pl.CostEstimate(
            flops=0, bytes_accessed=2 * source.size, transcendentals=0
        ),
        compiler_params=PARAMS,
    )(source)


def together(first, *others):
    return lax.optimization_barrier((first, *others))


def send(value, even, odd, size):
    pairs = [(i, i ^ (odd if i % 2 else even)) for i in range(size)]
    return lax.ppermute(value, "blk", pairs)


def gather_parts(chunk, size, meanwhile):
    own = chunk[None]
    done = []
    step = size // 2
    while step > 4:
        other = send(own, step, step, size)
        if not done:
            work = meanwhile[0](own)
            other, work = together(other, work)
            done.append(work)
        own = jnp.concatenate([own, other], axis=0)
        step //= 2
    own_and_core = jnp.concatenate([own, send(own, 1, 1, size)], axis=0)
    side = send(own, 4, 4, size)
    corner = send(own_and_core, 6, 2, size)
    work = meanwhile[1](own_and_core)
    corner, work = together(corner, work)
    done.append(work)
    rest = jnp.concatenate([side, corner], axis=0)
    return (own_and_core, rest, send(rest, 1, 1, size)), done


def owners(size):
    me = lax.axis_index("blk")
    corner = jnp.where(lax.rem(me, 2) == 1, 2, 6)
    other = me ^ 1
    other_corner = jnp.where(lax.rem(me, 2) == 1, 6, 2)
    own = [0]
    step = size // 2
    while step > 4:
        own = own + [step ^ entry for entry in own]
        step //= 2
    both = own + [entry ^ 1 for entry in own]
    return (
        [me ^ entry for entry in both],
        [me ^ 4 ^ entry for entry in own] + [me ^ corner ^ entry for entry in both],
        [other ^ 4 ^ entry for entry in own] + [other ^ other_corner ^ entry for entry in both],
    )


def fisher_kernel(size, *refs):
    part_refs, (fisher_ref, out_ref, whole_ref) = refs[:3], refs[3:]
    layers, rows, feats = fisher_ref.shape
    tiles = feats // LANES
    queries = whole_ref.shape[2]
    for ref, places in zip(part_refs, owners(size)):
        for entry, place in enumerate(places):
            whole_ref[place] = ref[entry]
    parts = []
    for layer in range(layers):
        grads = jnp.concatenate(
            [
                whole_ref[:, layer * tiles + tile].reshape(size * queries, LANES)
                for tile in range(tiles)
            ],
            axis=1,
        )
        parts.append(
            lax.dot_general(
                fisher_ref[layer],
                grads,
                (((1,), (1,)), ((), ())),
                preferred_element_type=jnp.float32,
            )
        )
    pieces = [
        part[start : start + LANES] for start in range(0, rows, LANES) for part in parts
    ]
    out_ref[...] = jnp.concatenate(pieces, axis=1).astype(jnp.bfloat16)


def fisher_call(parts, inv_fisher, size):
    return pl.pallas_call(
        functools.partial(fisher_kernel, size),
        out_shape=jax.ShapeDtypeStruct((LANES, LANES), jnp.bfloat16),
        in_specs=[IN_VMEM] * 4,
        out_specs=IN_VMEM,
        scratch_shapes=[pltpu.VMEM((size,) + parts[0].shape[1:], jnp.bfloat16)],
        compiler_params=PARAMS,
    )(*parts, inv_fisher)


def add_products(chunk_ref, store_ref, total_ref, fresh):
    _, count, layers, width = store_ref.shape
    groups = width // LANES
    span = LANES // groups
    lane = lax.broadcasted_iota(jnp.int32, (LANES, LANES), 1)
    for entry in range(chunk_ref.shape[0]):
        chunk = chunk_ref[entry]
        weights = jnp.concatenate(
            [
                jnp.where(lane // span == group, chunk, jnp.zeros_like(chunk))
                for group in range(groups)
            ],
            axis=0,
        )
        rows = store_ref[entry].reshape(count * layers, width)
        product = jnp.dot(rows, weights, preferred_element_type=jnp.float32)
        if fresh and entry == 0:
            total_ref[...] = product
        else:
            total_ref[...] += product


def partial_kernel(chunk_ref, store_ref, *refs):
    add_products(chunk_ref, store_ref, refs[-1], fresh=len(refs) == 1)


def partial_call(chunks, store, total=None):
    _, count, layers, width = store.shape
    flops = 2 * chunks.shape[0] * count * layers * width * LANES
    return pl.pallas_call(
        partial_kernel,
        out_shape=jax.ShapeDtypeStruct((count * layers, LANES), jnp.float32),
        in_specs=[IN_VMEM] * (2 if total is None else 3),
        out_specs=IN_VMEM,
        input_output_aliases={} if total is None else {2: 0},
        cost_estimate=pl.CostEstimate(flops=flops, bytes_accessed=0, transcendentals=0),
        compiler_params=PARAMS,
    )(*([chunks, store] if total is None else [chunks, store, total]))


def score_kernel(queries, chunk_ref, store_ref, before_ref, scale_ref, out_ref, total_ref):
    _, count, layers, width = store_ref.shape
    groups = width // LANES
    span = LANES // groups
    total_ref[...] = before_ref[...]
    add_products(chunk_ref, store_ref, total_ref, fresh=False)
    lane = lax.broadcasted_iota(jnp.int32, (count, LANES), 1)
    mixed = total_ref[pl.ds(0, count, layers)]
    for layer in range(1, layers):
        rows = total_ref[pl.ds(layer, count, layers)]
        mixed = jnp.where(lane % span // queries == layer, rows, mixed)
    turned = mixed.T
    result = turned[:queries]
    for start in range(queries, LANES, queries):
        result = result + turned[start : start + queries]
    out_ref[...] = result * scale_ref[...]


def score_call(chunks, store, total, scaling, queries):
    _, count, layers, _ = store.shape
    return pl.pallas_call(
        functools.partial(score_kernel, queries),
        out_shape=jax.ShapeDtypeStruct((queries, count), jnp.float32),
        in_specs=[IN_VMEM] * 4,
        out_specs=IN_VMEM,
        scratch_shapes=[pltpu.VMEM(total.shape, jnp.float32)],
        compiler_params=PARAMS,
    )(chunks, store, total, scaling[None, :])


def fits(size, factors, store, inv_fisher):
    queries, layers, _, width = factors.shape
    _, rows, feats = inv_fisher.shape
    return (
        size >= 8
        and size & (size - 1) == 0
        and width == LANES
        and queries == 2
        and layers == 2
        and rows % LANES == 0
        and (rows // LANES) * layers * queries * size == LANES
        and store.shape[0] % LANES == 0
        and feats == rows * size
    )


def solution(mesh):
    size = mesh.shape["blk"]

    def local(factors, token_mask, store, inv_fisher, source_ids, source_weight):
        if not fits(size, factors, store, inv_fisher):
            return plain(factors, token_mask, store, inv_fisher, source_ids, source_weight)
        scaling = make_scaling(source_ids, source_weight)
        grads = grads_call(factors, token_mask)
        counts = [size // 4, size * 3 // 8, size * 3 // 8]

        def first_stores(after):
            return [load_store(together(store, after)[0], size, k, counts[k]) for k in (0, 1)]

        def last_store(after):
            return load_store(together(store, after)[0], size, 2, counts[2])

        parts, (fisher, stores) = gather_parts(
            grads, size, [lambda after: load_whole(together(inv_fisher, after)[0]), first_stores]
        )
        hidden = fisher_call(parts, fisher, size)
        parts, (last, total) = gather_parts(
            hidden, size, [last_store, lambda chunks: partial_call(chunks, stores[0])]
        )
        total = partial_call(parts[1], stores[1], total)
        return score_call(parts[2], last, total, scaling, factors.shape[0] * size)

    placed = (
        P(("groups", "blk"), None, None, None),
        P(("groups", "blk"), None),
        P(("groups", "blk"), None, None),
        P(None, "blk", None),
        P(("groups", "blk")),
        P(),
    )
    return jax.shard_map(
        local, mesh=mesh, in_specs=placed, out_specs=P("groups", "blk"), check_vma=False
    )
```

time: 48.8 us -> 35.4 us (0.73)
  waiting for transfers between devices: 18.3 us -> 6.44 us
  local copies, waits for them, and re-layouts: 7.09 us -> 3.9 us
  Pallas kernels: 7.46 us -> 10.3 us
  other arithmetic: 1.49 us -> 0.39 us
    ppermute x8 -> x10, waiting for transfers between devices: 18.3 us -> 6.44 us  [send(): return lax.ppermute(value, 'blk', pairs)]
    unnamed x8 -> x14, local copies, waits for them, and re-layouts: 7.09 us -> 3.78 us
    pallas_call x1 -> x7, Pallas kernels: 5.3 us -> 8.51 us  [the longest x3 4.4 us: load_store(): pl.pallas_call(functools.partial(load_kernel, size, index), out_shape=jax...]
    reduce_sum x1, other arithmetic: 0.79 us -> 0.09 us  [make_scaling(): return jnp.sum(matches * source_weight[None, :], axis=1)]
    ppermute x8 -> x10, starting transfers between devices: 14.1 us -> 14 us  [send(): return lax.ppermute(value, 'blk', pairs)]
  transfers between devices with their start and end apart: 8 -> 10, of which waited for: 8 -> 7; matrix products, arithmetic and copies ran while one was open for 2% -> 1% of each run, Pallas kernels for 0% -> 19%
where the time goes in v3:
time: 35.4 us; the launch traced here: 35.2 us
  starting transfers between devices  14 us (40%)
  Pallas kernels  10.3 us (29%)
  waiting for transfers between devices  6.44 us (18%)
  local copies, waits for them, and re-layouts  3.9 us (11%)
  other arithmetic  0.39 us (1%)
    ppermute x10, starting transfers between devices, send(): return lax.ppermute(value, 'blk', pairs)  14 us
    ppermute x10, waiting for transfers between devices, send(): return lax.ppermute(value, 'blk', pairs)  6.44 us
    pallas_call x3, Pallas kernels, load_store(): pl.pallas_call(functools.partial(load_kernel, size, index), out_shape=jax...  4.4 us
    unnamed x14, local copies, waits for them, and re-layouts  3.78 us
    pallas_call x2, Pallas kernels, partial_call(): pl.pallas_call(partial_kernel, out_shape=jax.ShapeDtypeStruct((count * la...  1.93 us
    pallas_call x1, Pallas kernels, score_call(): pl.pallas_call(functools.partial(score_kernel, queries), out_shape=jax.Sh...  1.89 us
    pallas_call x1, Pallas kernels, fisher_call(): pl.pallas_call(functools.partial(fisher_kernel, size), out_shape=jax.Shap...  1.36 us
  transfers between devices with their start and end apart: 10, of which 7 were waited for; matrix products, arithmetic and copies ran while one was open for 1% of the time, Pallas kernels for 19%

profile of v3, /device:TPU:0, one launch (start us, length us, event | category | flops | bytes accessed | tf_op | source)
XLA Modules:
  0.0 35.2 jit_solution(16537882623426594795)
XLA Ops:
  0.0 0.8 %copy-done.2 = bf16[2,2,64,128]{3,2,1,0:T(8,128)(2,1)S(1)} copy-done((bf16[2,2,64,128]{3,2,1,0:T(8,128)(2,1)S(1)}, bf16[2,2,64,128]{3,2,1,0:T(8,128)(2,1)}, u32[]{:S(2)}) %copy-start.2) | copy-done | bytes 65560
  0.8 0.7 %copy-done.3 = s32[2,64]{1,0:T(2,128)S(1)} copy-done((s32[2,64]{1,0:T(2,128)S(1)}, s32[2,64]{1,0:T(2,128)}, u32[]{:S(2)}) %copy-start.3) | copy-done | bytes 536
  1.5 0.4 %shard_map.64 = bf16[64,2,128]{2,1,0:T(2,128)(2,1)S(1)} custom-call(bf16[2,2,64,128]{3,2,1,0:T(8,128)(2,1)S(1)} %copy-done.2, s32[2,64]{1,0:T(2,128)S(1)} %copy-done.3), custom_call_target="tpu_custom_call" | custom-call | tf_op jit(solution)/shard_map/pallas_call | solution.py:87
  2.0 4.1 %collective-permute-start = (bf16[1,64,2,128]{3,2,1,0:T(2,128)(2,1)S(1)}, bf16[1,64,2,128]{3,2,1,0:T(2,128)(2,1)S(1)}, u32[]{:S(2)}, u32[]{:S(2)}) collective-permute-start(bf16[1,64,2,128]{3,2,1,0:T(2,128)(2,1)S(1)} %bitcast.6), channel_id=1, source_target_pairs={{0,8},{1,9},{2,10},{3,11},{4,12},{5,13},{6,14},{7,15},{8,0},{9,1},... | collective-permute-start | bytes 98312 | tf_op jit(solution)/shard_map/ppermute | solution.py:153
  6.1 2.2 %copy-done.1 = bf16[2,256,4096]{2,1,0:T(8,128)(2,1)S(1)} copy-done((bf16[2,256,4096]{2,1,0:T(8,128)(2,1)S(1)}, bf16[2,256,4096]{2,1,0:T(8,128)(2,1)}, u32[]{:S(2)}) %copy-start.1) | copy-done | bytes 4194328
  8.2 0.3 shard_map.65.refs_3_
  8.6 0.1 pad_maximum_fusion.2
  8.7 0.1 collective-permute-start.1
  8.7 1.6 %collective-permute-start.2 = (bf16[2,64,2,128]{3,2,1,0:T(2,128)(2,1)S(1)}, bf16[2,64,2,128]{3,2,1,0:T(2,128)(2,1)S(1)}, u32[]{:S(2)}, u32[]{:S(2)}) collective-permute-start(bf16[2,64,2,128]{3,2,1,0:T(2,128)(2,1)S(1)} %pad_maximum_fusion.2), channel_id=1, source_target_pairs={{0,4},{1,5},{2,6},{3,7},{4,0},{5,1},{6,2},{7,3},{8,12},{9,13},{10,... | collective-permute-start | bytes 196616 | tf_op jit(solution)/shard_map/ppermute | solution.py:153
  10.4 0.2 pad_maximum_fusion.refs_0_
  10.6 2.2 %collective-permute-start.3 = (bf16[4,64,2,128]{3,2,1,0:T(2,128)(2,1)S(1)}, bf16[4,64,2,128]{3,2,1,0:T(2,128)(2,1)S(1)}, u32[]{:S(2)}, u32[]{:S(2)}) collective-permute-start(bf16[4,64,2,128]{3,2,1,0:T(2,128)(2,1)S(1)} %pad_maximum_fusion.refs_0_), channel_id=1, source_target_pairs={{0,6},{1,3},{2,4},{3,1},{4,2},{5,7},{6,0},{7,5},{8,14},{9,11},{10,... | collective-permute-start | bytes 393224 | tf_op jit(solution)/shard_map/ppermute | solution.py:153
  12.8 1.7 %shard_map.67.store_ref = bf16[6,512,2,256]{3,2,1,0:T(2,128)(2,1)S(1)} custom-call(bf16[512,2,4096]{2,1,0:T(2,128)(2,1)S(1)} %copy-done), custom_call_target="tpu_custom_call" | custom-call | bytes 3145728 | tf_op jit(solution)/shard_map/pallas_call | solution.py:114
  14.4 1.1 %shard_map.66.store_ref = bf16[4,512,2,256]{3,2,1,0:T(2,128)(2,1)S(1)} custom-call(bf16[512,2,4096]{2,1,0:T(2,128)(2,1)S(1)} %copy-done), custom_call_target="tpu_custom_call" | custom-call | bytes 2097152 | tf_op jit(solution)/shard_map/pallas_call | solution.py:114
  15.6 0.9 %collective-permute-done.3 = bf16[4,64,2,128]{3,2,1,0:T(2,128)(2,1)S(1)} collective-permute-done((bf16[4,64,2,128]{3,2,1,0:T(2,128)(2,1)S(1)}, bf16[4,64,2,128]{3,2,1,0:T(2,128)(2,1)S(1)}, u32[]{:S(2)}, u32[]{:S(2)}) %collective-permute-start.3) | collective-permute-done | bytes 131104 | tf_op jit(solution)/shard_map/ppermute | solution.py:153
  16.5 0.1 constant_dynamic-update-slice_fusion.refs_1_
  16.7 1.4 %collective-permute-done.4.refs_2_ = bf16[6,64,2,128]{3,2,1,0:T(2,128)(2,1)S(1)} collective-permute-done((bf16[6,64,2,128]{3,2,1,0:T(2,128)(2,1)S(1)}, bf16[6,64,2,128]{3,2,1,0:T(2,128)(2,1)S(1)}, u32[]{:S(2)}, u32[]{:S(2)}) %collective-permute-start.4) | collective-permute-done | bytes 196640 | tf_op jit(solution)/shard_map/ppermute | solution.py:153
  18.1 1.4 %shard_map.68 = bf16[128,128]{1,0:T(8,128)(2,1)S(1)} custom-call(bf16[4,64,2,128]{3,2,1,0:T(2,128)(2,1)S(1)} %pad_maximum_fusion.refs_0_, bf16[6,64,2,128]{3,2,1,0:T(2,128)(2,1)S(1)} %constant_dynamic-update-slice_fusion.refs_1_, bf16[6,64,2,128]{3,2,1,0:T(2,128)(2,1)S(1)} %collective-permute-done.4.refs_2_, bf16[2,256,4096]{2,1,0:T(8,128)(2,1)S(1)} %shard_map.65.refs_3_), custom_call_target="tpu_custom_call" | custom-call | tf_op jit(solution)/shard_map/pallas_call | solution.py:228
  19.5 2.6 %collective-permute-start.5 = (bf16[1,128,128]{2,1,0:T(8,128)(2,1)S(1)}, bf16[1,128,128]{2,1,0:T(8,128)(2,1)S(1)}, u32[]{:S(2)}, u32[]{:S(2)}) collective-permute-start(bf16[1,128,128]{2,1,0:T(8,128)(2,1)S(1)} %bitcast.3), channel_id=1, source_target_pairs={{0,8},{1,9},{2,10},{3,11},{4,12},{5,13},{6,14},{7,15},{8,0},{9,1},... | collective-permute-start | bytes 98312 | tf_op jit(solution)/shard_map/ppermute | solution.py:153
  22.1 1.6 %shard_map.69.store_ref = bf16[6,512,2,256]{3,2,1,0:T(2,128)(2,1)S(1)} custom-call(bf16[512,2,4096]{2,1,0:T(2,128)(2,1)S(1)} %copy-done), custom_call_target="tpu_custom_call" | custom-call | bytes 3145728 | tf_op jit(solution)/shard_map/pallas_call | solution.py:114
  23.8 0.7 %collective-permute-done.5 = bf16[1,128,128]{2,1,0:T(8,128)(2,1)S(1)} collective-permute-done((bf16[1,128,128]{2,1,0:T(8,128)(2,1)S(1)}, bf16[1,128,128]{2,1,0:T(8,128)(2,1)S(1)}, u32[]{:S(2)}, u32[]{:S(2)}) %collective-permute-start.5) | collective-permute-done | bytes 32800 | tf_op jit(solution)/shard_map/ppermute | solution.py:153
  24.5 0.1 collective-permute-start.7
  24.6 1.1 %collective-permute-start.6 = (bf16[2,128,128]{2,1,0:T(8,128)(2,1)S(1)}, bf16[2,128,128]{2,1,0:T(8,128)(2,1)S(1)}, u32[]{:S(2)}, u32[]{:S(2)}) collective-permute-start(bf16[2,128,128]{2,1,0:T(8,128)(2,1)S(1)} %pad_maximum_fusion.3), channel_id=1, source_target_pairs={{0,4},{1,5},{2,6},{3,7},{4,0},{5,1},{6,2},{7,3},{8,12},{9,13},{10,... | collective-permute-start | bytes 196616 | tf_op jit(solution)/shard_map/ppermute | solution.py:153
  25.7 0.1 collective-permute-done.7
  25.9 2.1 %collective-permute-start.8 = (bf16[4,128,128]{2,1,0:T(8,128)(2,1)S(1)}, bf16[4,128,128]{2,1,0:T(8,128)(2,1)S(1)}, u32[]{:S(2)}, u32[]{:S(2)}) collective-permute-start(bf16[4,128,128]{2,1,0:T(8,128)(2,1)S(1)} %pad_maximum_fusion.1.chunk_ref), channel_id=1, source_target_pairs={{0,6},{1,3},{2,4},{3,1},{4,2},{5,7},{6,0},{7,5},{8,14},{9,11},{10,... | collective-permute-start | bytes 393224 | tf_op jit(solution)/shard_map/ppermute | solution.py:153
  27.9 0.8 %shard_map.70.refs_0_ = f32[1024,128]{1,0:T(8,128)S(1)} custom-call(bf16[4,128,128]{2,1,0:T(8,128)(2,1)S(1)} %pad_maximum_fusion.1.chunk_ref, bf16[4,512,2,256]{3,2,1,0:T(2,128)(2,1)S(1)} %shard_map.66.store_ref), custom_call_target="tpu_custom_call" | custom-call | flops 268435456 | tf_op jit(solution)/shard_map/pallas_call | solution.py:267
  28.7 0.4 %collective-permute-done.6 = bf16[2,128,128]{2,1,0:T(8,128)(2,1)S(1)} collective-permute-done((bf16[2,128,128]{2,1,0:T(8,128)(2,1)S(1)}, bf16[2,128,128]{2,1,0:T(8,128)(2,1)S(1)}, u32[]{:S(2)}, u32[]{:S(2)}) %collective-permute-start.6) | collective-permute-done | bytes 65568 | tf_op jit(solution)/shard_map/ppermute | solution.py:153
  29.1 2.7 %collective-permute-done.8 = bf16[4,128,128]{2,1,0:T(8,128)(2,1)S(1)} collective-permute-done((bf16[4,128,128]{2,1,0:T(8,128)(2,1)S(1)}, bf16[4,128,128]{2,1,0:T(8,128)(2,1)S(1)}, u32[]{:S(2)}, u32[]{:S(2)}) %collective-permute-start.8) | collective-permute-done | bytes 131104 | tf_op jit(solution)/shard_map/ppermute | solution.py:153
  31.8 0.1 collective-permute-start.9
  31.9 0.1 select_reduce_fusion
  32.0 1.1 %shard_map.71.before_ref = f32[1024,128]{1,0:T(8,128)S(1)} custom-call(bf16[6,128,128]{2,1,0:T(8,128)(2,1)S(1)} %constant_dynamic-update-slice_fusion.2.chunk_ref, bf16[6,512,2,256]{3,2,1,0:T(2,128)(2,1)S(1)} %shard_map.67.store_ref, f32[1024,128]{1,0:T(8,128)S(1)} %shard_map.70.refs_0_), custom_call_target="tpu_custom_call", output_to_operand_aliasing={{}: (2, {})} | custom-call | flops 402653184 | tf_op jit(solution)/shard_map/pallas_call | solution.py:267
  33.1 0.2 collective-permute-done.9.chunk_ref
  33.3 1.9 %shard_map.72 = f32[32,512]{1,0:T(8,128)} custom-call(bf16[6,128,128]{2,1,0:T(8,128)(2,1)S(1)} %collective-permute-done.9.chunk_ref, bf16[6,512,2,256]{3,2,1,0:T(2,128)(2,1)S(1)} %shard_map.69.store_ref, f32[1024,128]{1,0:T(8,128)S(1)} %shard_map.71.before_ref, f32[1,512]{1,0:T(1,128)S(1)} %bitcast.9), custom_call_target="tpu_custom_call" | custom-call | tf_op jit(solution)/shard_map/pallas_call | solution.py:298
  (18 shorter events, 0.2 us)
Async XLA Ops:
  0.0 0.8 %copy-start.2 = (bf16[2,2,64,128]{3,2,1,0:T(8,128)(2,1)S(1)}, bf16[2,2,64,128]{3,2,1,0:T(8,128)(2,1)}, u32[]{:S(2)}) copy-start(bf16[2,2,64,128]{3,2,1,0:T(8,128)(2,1)} %factors_ref.1) | copy-start | bytes 196612
  0.8 0.7 %copy-start.3 = (s32[2,64]{1,0:T(2,128)S(1)}, s32[2,64]{1,0:T(2,128)}, u32[]{:S(2)}) copy-start(s32[2,64]{1,0:T(2,128)} %mask_ref.1) | copy-start | bytes 1540
  1.9 10.8 %copy-start = (bf16[512,2,4096]{2,1,0:T(2,128)(2,1)S(1)}, bf16[512,2,4096]{2,1,0:T(2,128)(2,1)}, u32[]{:S(2)}) copy-start(bf16[512,2,4096]{2,1,0:T(2,128)(2,1)} %source_ref.3) | copy-start | bytes 25165828
  2.0 6.6 %collective-permute-start = (bf16[1,64,2,128]{3,2,1,0:T(2,128)(2,1)S(1)}, bf16[1,64,2,128]{3,2,1,0:T(2,128)(2,1)S(1)}, u32[]{:S(2)}, u32[]{:S(2)}) collective-permute-start(bf16[1,64,2,128]{3,2,1,0:T(2,128)(2,1)S(1)} %bitcast.6), channel_id=1, source_target_pairs={{0,8},{1,9},{2,10},{3,11},{4,12},{5,13},{6,14},{7,15},{8,0},{9,1},... | collective-permute-start | bytes 98312 | tf_op jit(solution)/shard_map/ppermute | solution.py:153
  6.1 2.2 %copy-start.1 = (bf16[2,256,4096]{2,1,0:T(8,128)(2,1)S(1)}, bf16[2,256,4096]{2,1,0:T(8,128)(2,1)}, u32[]{:S(2)}) copy-start(bf16[2,256,4096]{2,1,0:T(8,128)(2,1)} %source_ref) | copy-start | bytes 12582916
  8.7 1.7 %collective-permute-start.1 = (bf16[2,64,2,128]{3,2,1,0:T(2,128)(2,1)S(1)}, bf16[2,64,2,128]{3,2,1,0:T(2,128)(2,1)S(1)}, u32[]{:S(2)}, u32[]{:S(2)}) collective-permute-start(bf16[2,64,2,128]{3,2,1,0:T(2,128)(2,1)S(1)} %pad_maximum_fusion.2), channel_id=1, source_target_pairs={{0,1},{1,0},{2,3},{3,2},{4,5},{5,4},{6,7},{7,6},{8,9},{9,8},{10,11... | collective-permute-start | bytes 196616 | tf_op jit(solution)/shard_map/ppermute | solution.py:153
  8.7 6.8 %collective-permute-start.2 = (bf16[2,64,2,128]{3,2,1,0:T(2,128)(2,1)S(1)}, bf16[2,64,2,128]{3,2,1,0:T(2,128)(2,1)S(1)}, u32[]{:S(2)}, u32[]{:S(2)}) collective-permute-start(bf16[2,64,2,128]{3,2,1,0:T(2,128)(2,1)S(1)} %pad_maximum_fusion.2), channel_id=1, source_target_pairs={{0,4},{1,5},{2,6},{3,7},{4,0},{5,1},{6,2},{7,3},{8,12},{9,13},{10,... | collective-permute-start | bytes 196616 | tf_op jit(solution)/shard_map/ppermute | solution.py:153
  10.6 5.9 %collective-permute-start.3 = (bf16[4,64,2,128]{3,2,1,0:T(2,128)(2,1)S(1)}, bf16[4,64,2,128]{3,2,1,0:T(2,128)(2,1)S(1)}, u32[]{:S(2)}, u32[]{:S(2)}) collective-permute-start(bf16[4,64,2,128]{3,2,1,0:T(2,128)(2,1)S(1)} %pad_maximum_fusion.refs_0_), channel_id=1, source_target_pairs={{0,6},{1,3},{2,4},{3,1},{4,2},{5,7},{6,0},{7,5},{8,14},{9,11},{10,... | collective-permute-start | bytes 393224 | tf_op jit(solution)/shard_map/ppermute | solution.py:153
  16.6 1.5 %collective-permute-start.4 = (bf16[6,64,2,128]{3,2,1,0:T(2,128)(2,1)S(1)}, bf16[6,64,2,128]{3,2,1,0:T(2,128)(2,1)S(1)}, u32[]{:S(2)}, u32[]{:S(2)}) collective-permute-start(bf16[6,64,2,128]{3,2,1,0:T(2,128)(2,1)S(1)} %constant_dynamic-update-slice_fusion.refs_1_), channel_id=1, source_target_pairs={{0,1},{1,0},{2,3},{3,2},{4,5},{5,4},{6,7},{7,6},{8,9},{9,8},{10,11... | collective-permute-start | bytes 589832 | tf_op jit(solution)/shard_map/ppermute | solution.py:153
  19.5 12.4 %copy-start.4 = (s32[512]{0:T(512)S(1)}, s32[512]{0:T(512)}, u32[]{:S(2)}) copy-start(s32[512]{0:T(512)} %param.10) | copy-start | bytes 6148
  19.5 12.4 %copy-start.5 = (f32[16]{0:T(128)S(1)}, f32[16]{0:T(128)}, u32[]{:S(2)}) copy-start(f32[16]{0:T(128)} %param.11) | copy-start | bytes 196
  19.5 5.0 %collective-permute-start.5 = (bf16[1,128,128]{2,1,0:T(8,128)(2,1)S(1)}, bf16[1,128,128]{2,1,0:T(8,128)(2,1)S(1)}, u32[]{:S(2)}, u32[]{:S(2)}) collective-permute-start(bf16[1,128,128]{2,1,0:T(8,128)(2,1)S(1)} %bitcast.3), channel_id=1, source_target_pairs={{0,8},{1,9},{2,10},{3,11},{4,12},{5,13},{6,14},{7,15},{8,0},{9,1},... | collective-permute-start | bytes 98312 | tf_op jit(solution)/shard_map/ppermute | solution.py:153
  24.5 1.3 %collective-permute-start.7 = (bf16[2,128,128]{2,1,0:T(8,128)(2,1)S(1)}, bf16[2,128,128]{2,1,0:T(8,128)(2,1)S(1)}, u32[]{:S(2)}, u32[]{:S(2)}) collective-permute-start(bf16[2,128,128]{2,1,0:T(8,128)(2,1)S(1)} %pad_maximum_fusion.3), channel_id=1, source_target_pairs={{0,1},{1,0},{2,3},{3,2},{4,5},{5,4},{6,7},{7,6},{8,9},{9,8},{10,11... | collective-permute-start | bytes 196616 | tf_op jit(solution)/shard_map/ppermute | solution.py:153
  24.6 4.5 %collective-permute-start.6 = (bf16[2,128,128]{2,1,0:T(8,128)(2,1)S(1)}, bf16[2,128,128]{2,1,0:T(8,128)(2,1)S(1)}, u32[]{:S(2)}, u32[]{:S(2)}) collective-permute-start(bf16[2,128,128]{2,1,0:T(8,128)(2,1)S(1)} %pad_maximum_fusion.3), channel_id=1, source_target_pairs={{0,4},{1,5},{2,6},{3,7},{4,0},{5,1},{6,2},{7,3},{8,12},{9,13},{10,... | collective-permute-start | bytes 196616 | tf_op jit(solution)/shard_map/ppermute | solution.py:153
  25.9 5.9 %collective-permute-start.8 = (bf16[4,128,128]{2,1,0:T(8,128)(2,1)S(1)}, bf16[4,128,128]{2,1,0:T(8,128)(2,1)S(1)}, u32[]{:S(2)}, u32[]{:S(2)}) collective-permute-start(bf16[4,128,128]{2,1,0:T(8,128)(2,1)S(1)} %pad_maximum_fusion.1.chunk_ref), channel_id=1, source_target_pairs={{0,6},{1,3},{2,4},{3,1},{4,2},{5,7},{6,0},{7,5},{8,14},{9,11},{10,... | collective-permute-start | bytes 393224 | tf_op jit(solution)/shard_map/ppermute | solution.py:153
  31.8 1.5 %collective-permute-start.9 = (bf16[6,128,128]{2,1,0:T(8,128)(2,1)S(1)}, bf16[6,128,128]{2,1,0:T(8,128)(2,1)S(1)}, u32[]{:S(2)}, u32[]{:S(2)}) collective-permute-start(bf16[6,128,128]{2,1,0:T(8,128)(2,1)S(1)} %constant_dynamic-update-slice_fusion.2.chunk_ref), channel_id=1, source_target_pairs={{0,1},{1,0},{2,3},{3,2},{4,5},{5,4},{6,7},{7,6},{8,9},{9,8},{10,11... | collective-permute-start | bytes 589832 | tf_op jit(solution)/shard_map/ppermute | solution.py:153

commit v4 on v2

v4 whole, which is shorter than its diff:
```python
import functools
import math

import jax
import jax.numpy as jnp
from jax import lax
from jax.experimental import pallas as pl
from jax.experimental.pallas import tpu as pltpu
from jax.sharding import PartitionSpec as P

LANES = 128
IN_VMEM = pl.BlockSpec(memory_space=pltpu.VMEM)
IN_HBM = pl.BlockSpec(memory_space=pltpu.HBM)
PARAMS = pltpu.CompilerParams(vmem_limit_bytes=16 * 2**20)


def make_grads(factors, token_mask):
    rank_size = factors.shape[3] // 2
    mask_values = token_mask.astype(jnp.float32)[:, None, :, None]
    left_side = factors[..., :rank_size].astype(jnp.float32) * mask_values
    right_side = factors[..., rank_size:].astype(jnp.float32)
    outer_sum = jnp.einsum("qlta,qltb->qlab", left_side, right_side)
    return outer_sum.reshape(outer_sum.shape[0], outer_sum.shape[1], rank_size * rank_size).astype(
        jnp.bfloat16
    )


def make_scaling(source_ids, source_weight):
    matches = (
        source_ids[:, None] == jnp.arange(source_weight.shape[0], dtype=jnp.int32)[None, :]
    ).astype(jnp.float32)
    return jnp.sum(matches * source_weight[None, :], axis=1)


def plain(factors, token_mask, store, inv_fisher, source_ids, source_weight):
    segment = lax.all_gather(make_grads(factors, token_mask), "blk", axis=0, tiled=True)
    products = [
        lax.dot_general(
            segment[:, layer_idx],
            inv_fisher[layer_idx],
            (((1,), (1,)), ((), ())),
            preferred_element_type=jnp.float32,
        )
        for layer_idx in range(inv_fisher.shape[0])
    ]
    hidden_cols = jnp.stack(products, axis=1).astype(jnp.bfloat16)
    hidden = lax.all_gather(hidden_cols, "blk", axis=2, tiled=True)
    raw_scores = lax.dot_general(
        hidden, store, (((1, 2), (1, 2)), ((), ())), preferred_element_type=jnp.float32
    )
    return raw_scores * make_scaling(source_ids, source_weight)[None, :]


def grads_kernel(factors_ref, mask_ref, out_ref, outer_ref, flat_ref):
    queries, layers, _, width = factors_ref.shape
    rank = width // 2
    tiles = rank * rank // LANES
    for layer in range(layers):
        for query in range(queries):
            block = factors_ref[query, layer].astype(jnp.float32)
            left = block[:, :rank].T * mask_ref[query : query + 1]
            outer_ref[...] = jnp.dot(
                left.astype(jnp.bfloat16),
                block[:, rank:].astype(jnp.bfloat16),
                preferred_element_type=jnp.float32,
            )
            flat_ref[layer, pl.ds(query, tiles, queries)] = jnp.concatenate(
                [outer_ref[pl.ds(0, tiles, 2)], outer_ref[pl.ds(1, tiles, 2)]], axis=1
            )
    out_ref[...] = (
        flat_ref[...].astype(jnp.bfloat16).reshape(layers * tiles, queries, LANES)
    )


def grads_call(factors, token_mask):
    queries, layers, _, width = factors.shape
    rank = width // 2
    tiles = rank * rank // LANES
    return pl.pallas_call(
        grads_kernel,
        out_shape=jax.ShapeDtypeStruct((layers * tiles, queries, LANES), jnp.bfloat16),
        in_specs=[IN_VMEM] * 2,
        out_specs=IN_VMEM,
        scratch_shapes=[
            pltpu.VMEM((rank, rank), jnp.float32),
            pltpu.VMEM((layers, tiles * queries, LANES), jnp.float32),
        ],
        compiler_params=PARAMS,
    )(factors, token_mask.astype(jnp.float32))


def load_kernel(size, names, source_ref, out_ref, sem):
    width = out_ref.shape[-1]
    places = owners(size)
    for entry, owner in enumerate(sum([places[name] for name in names], [])):
        columns = pl.ds(pl.multiple_of(owner * width, width), width)
        pltpu.make_async_copy(source_ref.at[:, :, columns], out_ref.at[entry], sem).start()
    pltpu.make_async_copy(out_ref, out_ref, sem).wait()


def load_store(store, size, names, after):
    store, _ = lax.optimization_barrier((store, after))
    rows, layers, feats = store.shape
    entries = sum(entry_count(name, size) for name in names)
    shape = (entries, rows, layers, feats // size)
    return pl.pallas_call(
        functools.partial(load_kernel, size, names),
        out_shape=jax.ShapeDtypeStruct(shape, store.dtype),
        in_specs=[IN_HBM],
        out_specs=IN_VMEM,
        scratch_shapes=[pltpu.SemaphoreType.DMA],
        cost_estimate=pl.CostEstimate(
            flops=0, bytes_accessed=2 * math.prod(shape), transcendentals=0
        ),
        compiler_params=PARAMS,
    )(store)


def copy_kernel(source_ref, out_ref, sem):
    copy = pltpu.make_async_copy(source_ref, out_ref, sem)
    copy.start()
    copy.wait()


def load_whole(source, after):
    source, _ = lax.optimization_barrier((source, after))
    return pl.pallas_call(
        copy_kernel,
        out_shape=jax.ShapeDtypeStruct(source.shape, source.dtype),
        in_specs=[IN_HBM],
        out_specs=IN_VMEM,
        scratch_shapes=[pltpu.SemaphoreType.DMA],
        cost_estimate=pl.CostEstimate(
            flops=0, bytes_accessed=2 * source.size, transcendentals=0
        ),
        compiler_params=PARAMS,
    )(source)


def send(value, even, odd, size):
    pairs = [(i, i ^ (odd if i % 2 else even)) for i in range(size)]
    return lax.ppermute(value, "blk", pairs)


def far_steps(size):
    return [size >> k for k in range(1, size.bit_length()) if size >> k > 4]


def gather_direct(chunk, size, early, middle, late):
    share = chunk[None]
    for step in far_steps(size):
        other = send(share, step, step, size)
        if step == size // 2:
            other, *_ = lax.optimization_barrier((other, *early(share)))
        share = jnp.concatenate([share, other], axis=0)
    got = {"own": share, "core": send(share, 1, 1, size)}
    one, two, three = (send(share, even, odd, size) for even, odd in SQUARE)
    one, got["core"], *_ = lax.optimization_barrier((one, got["core"], *middle(got)))
    got.update(one=one, core_one=send(one, 1, 1, size))
    two, three, *_ = lax.optimization_barrier((two, three, got["core_one"], *late(got)))
    got.update(two=two, core_two=send(two, 1, 1, size))
    got.update(three=three, core_three=send(three, 1, 1, size))
    return got


def gather_square(chunk, size, early, middle, late):
    got = {}
    share = chunk[None]
    for step in far_steps(size):
        other = send(share, step, step, size)
        if step == size // 2:
            other, *_ = lax.optimization_barrier((other, *early(share)))
        share = jnp.concatenate([share, other], axis=0)
    core = send(share, 1, 1, size)
    near = send(share, 4, 4, size)
    got["both"] = jnp.concatenate([share, core], axis=0)
    corner = send(got["both"], 6, 2, size)
    near, *_ = lax.optimization_barrier((near, *middle(got)))
    got["near"] = near
    got["core_near"] = send(near, 1, 1, size)
    corner, *_ = lax.optimization_barrier((corner, got["core_near"], *late(got)))
    got["corner"] = corner
    got["core_corner"] = send(corner, 1, 1, size)
    return got


def owners(size):
    me = lax.axis_index("blk")
    core = me ^ 1
    is_odd = lax.rem(me, 2) == 1
    share = [0]
    for step in far_steps(size):
        share = share + [step ^ entry for entry in share]
    both = share + [1 ^ entry for entry in share]
    places = {
        "own": [me ^ entry for entry in share],
        "core": [core ^ entry for entry in share],
        "both": [me ^ entry for entry in both],
        "near": [me ^ 4 ^ entry for entry in share],
        "core_near": [core ^ 4 ^ entry for entry in share],
    }
    mine, theirs = jnp.where(is_odd, 2, 6), jnp.where(is_odd, 6, 2)
    places["corner"] = [me ^ mine ^ entry for entry in both]
    places["core_corner"] = [core ^ theirs ^ entry for entry in both]
    for name, (even, odd) in zip(("one", "two", "three"), SQUARE):
        mine, theirs = jnp.where(is_odd, odd, even), jnp.where(is_odd, even, odd)
        places[name] = [me ^ mine ^ entry for entry in share]
        places["core_" + name] = [core ^ theirs ^ entry for entry in share]
    return places


def entry_count(name, size):
    return (2 if name in TWICE else 1) << len(far_steps(size))


SQUARE = ((4, 6), (6, 2), (2, 4))
DIRECT = ("own", "core", "one", "two", "three", "core_one", "core_two", "core_three")
TWICE = ("both", "corner", "core_corner")


def fisher_kernel(size, *refs):
    part_refs, (fisher_ref, out_ref, whole_ref) = refs[:-3], refs[-3:]
    layers, rows, feats = fisher_ref.shape
    tiles = feats // LANES
    queries = whole_ref.shape[2]
    places_of = owners(size)
    for ref, name in zip(part_refs, DIRECT):
        for entry, place in enumerate(places_of[name]):
            whole_ref[place] = ref[entry]
    parts = []
    for layer in range(layers):
        grads = jnp.concatenate(
            [
                whole_ref[:, layer * tiles + tile].reshape(size * queries, LANES)
                for tile in range(tiles)
            ],
            axis=1,
        )
        parts.append(
            lax.dot_general(
                fisher_ref[layer],
                grads,
                (((1,), (1,)), ((), ())),
                preferred_element_type=jnp.float32,
            )
        )
    pieces = [
        part[start : start + LANES] for start in range(0, rows, LANES) for part in parts
    ]
    out_ref[...] = jnp.concatenate(pieces, axis=1).astype(jnp.bfloat16)


def fisher_call(got, inv_fisher, size):
    chunk_shape = got["own"].shape[1:]
    return pl.pallas_call(
        functools.partial(fisher_kernel, size),
        out_shape=jax.ShapeDtypeStruct((LANES, LANES), jnp.bfloat16),
        in_specs=[IN_VMEM] * (len(DIRECT) + 1),
        out_specs=IN_VMEM,
        scratch_shapes=[pltpu.VMEM((size,) + chunk_shape, jnp.bfloat16)],
        compiler_params=PARAMS,
    )(*[got[name] for name in DIRECT], inv_fisher)


def products(chunk_refs, store_ref, start, total):
    _, count, layers, width = store_ref.shape
    groups = width // LANES
    span = LANES // groups
    lane = lax.broadcasted_iota(jnp.int32, (LANES, LANES), 1)
    for ref in chunk_refs:
        for entry in range(ref.shape[0]):
            chunk = ref[entry]
            weights = jnp.concatenate(
                [
                    jnp.where(lane // span == group, chunk, jnp.zeros_like(chunk))
                    for group in range(groups)
                ],
                axis=0,
            )
            rows = store_ref[start].reshape(count * layers, width)
            start += 1
            product = jnp.dot(rows, weights, preferred_element_type=jnp.float32)
            total = product if total is None else total + product
    return total


def partial_kernel(starts, *refs):
    number = len(starts)
    total = refs[2 * number][...] if len(refs) == 2 * number + 2 else None
    for chunk_ref, store_ref, start in zip(refs, refs[number:], starts):
        total = products([chunk_ref], store_ref, start, total)
    refs[-1][...] = total


def partial_call(chunks, stores, starts, total=None):
    _, count, layers, width = stores[0].shape
    entries = sum(chunk.shape[0] for chunk in chunks)
    flops = 2 * entries * count * layers * width * LANES
    operands = [*chunks, *stores] + ([] if total is None else [total])
    return pl.pallas_call(
        functools.partial(partial_kernel, tuple(starts)),
        out_shape=jax.ShapeDtypeStruct((count * layers, LANES), jnp.float32),
        in_specs=[IN_VMEM] * len(operands),
        out_specs=IN_VMEM,
        cost_estimate=pl.CostEstimate(flops=0, bytes_accessed=0, transcendentals=0),
        compiler_params=PARAMS,
    )(*operands)


def score_kernel(queries, start, *refs):
    *chunk_refs, store_ref, before_ref, scale_ref, out_ref, total_ref = refs
    _, count, layers, width = store_ref.shape
    span = LANES // (width // LANES)
    total_ref[...] = products(chunk_refs, store_ref, start, before_ref[...])
    lane = lax.broadcasted_iota(jnp.int32, (count, LANES), 1)
    mixed = total_ref[pl.ds(0, count, layers)]
    for layer in range(1, layers):
        rows = total_ref[pl.ds(layer, count, layers)]
        mixed = jnp.where(lane % span // queries == layer, rows, mixed)
    turned = mixed.T
    result = turned[:queries]
    for first in range(queries, LANES, queries):
        result = result + turned[first : first + queries]
    out_ref[...] = result * scale_ref[...]


def score_call(chunks, store, start, total, scaling, queries):
    _, count, layers, _ = store.shape
    return pl.pallas_call(
        functools.partial(score_kernel, queries, start),
        out_shape=jax.ShapeDtypeStruct((queries, count), jnp.float32),
        in_specs=[IN_VMEM] * (len(chunks) + 3),
        out_specs=IN_VMEM,
        scratch_shapes=[pltpu.VMEM(total.shape, jnp.float32)],
        compiler_params=PARAMS,
    )(*chunks, store, total, scaling[None, :])


def fits(size, factors, store, inv_fisher):
    queries, layers, _, width = factors.shape
    _, rows, feats = inv_fisher.shape
    return (
        size >= 16
        and size & (size - 1) == 0
        and width == LANES
        and queries == 2
        and layers == 2
        and rows % LANES == 0
        and (rows // LANES) * layers * queries * size == LANES
        and store.shape[0] % LANES == 0
        and feats == rows * size
    )


def solution(mesh):
    size = mesh.shape["blk"]

    def local(factors, token_mask, store, inv_fisher, source_ids, source_weight):
        if not fits(size, factors, store, inv_fisher):
            return plain(factors, token_mask, store, inv_fisher, source_ids, source_weight)
        scaling = make_scaling(source_ids, source_weight)
        grads = grads_call(factors, token_mask)
        ready = {}

        def keep(name, value):
            ready[name] = value
            return value

        def load(name, parts, after):
            return keep(name, load_store(store, size, parts, after))

        homes = (("both",), ("near", "core_near"), ("corner", "core_corner"))

        def home_of(name):
            return next(k for k, home in enumerate(homes) if name in home)

        def start_of(name):
            home = homes[home_of(name)]
            return sum(entry_count(other, size) for other in home[: home.index(name)])

        got = gather_direct(
            grads,
            size,
            lambda share: [keep("fisher", load_whole(inv_fisher, share))],
            lambda got: [load(0, homes[0], got["core"])],
            lambda got: [load(1, homes[1], got["one"])],
        )
        hidden = fisher_call(got, ready["fisher"], size)

        def add(got, *names):
            total = partial_call(
                [got[name] for name in names],
                [ready[home_of(name)] for name in names],
                [start_of(name) for name in names],
                ready.get("total"),
            )
            return keep("total", total)

        got = gather_square(
            hidden,
            size,
            lambda share: [load(2, homes[2], share)],
            lambda got: [add(got, "both")],
            lambda got: [add(got, "near")],
        )
        add(got, "core_near", "corner")
        return score_call(
            [got["core_corner"]], ready[2], start_of("core_corner"),
            ready["total"], scaling, factors.shape[0] * size,
        )

    placed = (
        P(("groups", "blk"), None, None, None),
        P(("groups", "blk"), None),
        P(("groups", "blk"), None, None),
        P(None, "blk", None),
        P(("groups", "blk")),
        P(),
    )
    return jax.shard_map(
        local, mesh=mesh, in_specs=placed, out_specs=P("groups", "blk"), check_vma=False
    )
```

time: 48.8 us -> 34.7 us (0.71)
  waiting for transfers between devices: 18.3 us -> 6.28 us
  local copies, waits for them, and re-layouts: 7.09 us -> 3.05 us
  Pallas kernels: 7.46 us -> 10.4 us
  other arithmetic: 1.49 us -> 0.88 us
    ppermute x8 -> x14, waiting for transfers between devices: 18.3 us -> 6.28 us  [send(): return lax.ppermute(value, 'blk', pairs)]
    unnamed x8 -> x10, local copies, waits for them, and re-layouts: 7.09 us -> 3.05 us
    pallas_call x1 -> x8, Pallas kernels: 5.3 us -> 8.72 us  [the longest x3 4.4 us: load_store(): pl.pallas_call(functools.partial(load_kernel, size, names), out_shape=jax...]
    reduce_sum x1, other arithmetic: 0.79 us -> 0.09 us  [make_scaling(): return jnp.sum(matches * source_weight[None, :], axis=1)]
    convert_element_type x0 -> x1, other arithmetic: none -> 0.68 us  [grads_call(): token_mask.astype(jnp.float32)]
    concatenate x6 -> x3, other arithmetic: 0.7 us -> 0.11 us  [the longest x1 0.09 us: gather_direct(): share = jnp.concatenate([share, other], axis=0)]
    ppermute x8 -> x14, starting transfers between devices: 14.1 us -> 13.7 us  [send(): return lax.ppermute(value, 'blk', pairs)]
  transfers between devices with their start and end apart: 8 -> 14, of which waited for: 8 -> 10; matrix products, arithmetic and copies ran while one was open for 2% -> 0% of each run, Pallas kernels for 0% -> 21%
where the time goes in v4:
time: 34.7 us; the launch traced here: 34.5 us
  starting transfers between devices  13.7 us (39%)
  Pallas kernels  10.4 us (30%)
  waiting for transfers between devices  6.28 us (18%)
  local copies, waits for them, and re-layouts  3.05 us (9%)
  other arithmetic  0.88 us (3%)
    ppermute x14, starting transfers between devices, send(): return lax.ppermute(value, 'blk', pairs)  13.7 us
    ppermute x14, waiting for transfers between devices, send(): return lax.ppermute(value, 'blk', pairs)  6.28 us
    pallas_call x3, Pallas kernels, load_store(): pl.pallas_call(functools.partial(load_kernel, size, names), out_shape=jax...  4.4 us
    unnamed x10, local copies, waits for them, and re-layouts  3.05 us
    pallas_call x3, Pallas kernels, partial_call(): pl.pallas_call(functools.partial(partial_kernel, tuple(starts)), out_shap...  2.43 us
    pallas_call x1, Pallas kernels, score_call(): pl.pallas_call(functools.partial(score_kernel, queries, start), out_shape...  1.61 us
    pallas_call x1, Pallas kernels, fisher_call(): pl.pallas_call(functools.partial(fisher_kernel, size), out_shape=jax.Shap...  1.35 us
  transfers between devices with their start and end apart: 14, of which 10 were waited for; matrix products, arithmetic and copies ran while one was open for 0% of the time, Pallas kernels for 21%

profile of v4, /device:TPU:0, one launch (start us, length us, event | category | flops | bytes accessed | tf_op | source)
XLA Modules:
  0.0 34.5 jit_solution(1013111005319107230)
XLA Ops:
  0.0 0.7 %convert_element_type.4.mask_ref = f32[2,64]{1,0:T(2,128)S(1)} convert(s32[2,64]{1,0:T(2,128)} %param.7) | non-fusion elementwise | flops 128 | bytes 1024 | tf_op jit(solution)/shard_map/convert_element_type | solution.py:89
  0.7 0.8 %copy-done.2 = bf16[2,2,64,128]{3,2,1,0:T(8,128)(2,1)S(1)} copy-done((bf16[2,2,64,128]{3,2,1,0:T(8,128)(2,1)S(1)}, bf16[2,2,64,128]{3,2,1,0:T(8,128)(2,1)}, u32[]{:S(2)}) %copy-start.2) | copy-done | bytes 65560
  1.5 0.3 shard_map.64
  1.9 4.1 %collective-permute-start = (bf16[1,64,2,128]{3,2,1,0:T(2,128)(2,1)S(1)}, bf16[1,64,2,128]{3,2,1,0:T(2,128)(2,1)S(1)}, u32[]{:S(2)}, u32[]{:S(2)}) collective-permute-start(bf16[1,64,2,128]{3,2,1,0:T(2,128)(2,1)S(1)} %bitcast.6), channel_id=1, source_target_pairs={{0,8},{1,9},{2,10},{3,11},{4,12},{5,13},{6,14},{7,15},{8,0},{9,1},... | collective-permute-start | bytes 98312 | tf_op jit(solution)/shard_map/ppermute | solution.py:142
  6.0 2.2 %copy-done.1 = bf16[2,256,4096]{2,1,0:T(8,128)(2,1)S(1)} copy-done((bf16[2,256,4096]{2,1,0:T(8,128)(2,1)S(1)}, bf16[2,256,4096]{2,1,0:T(8,128)(2,1)}, u32[]{:S(2)}) %copy-start.1) | copy-done | bytes 4194328
  8.2 0.3 shard_map.65.refs_8_
  8.5 0.1 pad_maximum_fusion.1.refs_0_
  8.7 1.6 %collective-permute-start.1 = (bf16[2,64,2,128]{3,2,1,0:T(2,128)(2,1)S(1)}, bf16[2,64,2,128]{3,2,1,0:T(2,128)(2,1)S(1)}, u32[]{:S(2)}, u32[]{:S(2)}) collective-permute-start(bf16[2,64,2,128]{3,2,1,0:T(2,128)(2,1)S(1)} %pad_maximum_fusion.1.refs_0_), channel_id=1, source_target_pairs={{0,4},{1,7},{2,6},{3,5},{4,0},{5,3},{6,2},{7,1},{8,12},{9,15},{10,... | collective-permute-start | bytes 196616 | tf_op jit(solution)/shard_map/ppermute | solution.py:142
  10.3 1.4 %collective-permute-start.3 = (bf16[2,64,2,128]{3,2,1,0:T(2,128)(2,1)S(1)}, bf16[2,64,2,128]{3,2,1,0:T(2,128)(2,1)S(1)}, u32[]{:S(2)}, u32[]{:S(2)}) collective-permute-start(bf16[2,64,2,128]{3,2,1,0:T(2,128)(2,1)S(1)} %pad_maximum_fusion.1.refs_0_), channel_id=1, source_target_pairs={{0,6},{1,3},{2,4},{3,1},{4,2},{5,7},{6,0},{7,5},{8,14},{9,11},{10,... | collective-permute-start | bytes 196616 | tf_op jit(solution)/shard_map/ppermute | solution.py:142
  11.7 0.5 %collective-permute-start.4 = (bf16[2,64,2,128]{3,2,1,0:T(2,128)(2,1)S(1)}, bf16[2,64,2,128]{3,2,1,0:T(2,128)(2,1)S(1)}, u32[]{:S(2)}, u32[]{:S(2)}) collective-permute-start(bf16[2,64,2,128]{3,2,1,0:T(2,128)(2,1)S(1)} %pad_maximum_fusion.1.refs_0_), channel_id=1, source_target_pairs={{0,2},{1,5},{2,0},{3,7},{4,6},{5,1},{6,4},{7,3},{8,10},{9,13},{10,... | collective-permute-start | bytes 196616 | tf_op jit(solution)/shard_map/ppermute | solution.py:142
  12.2 1.1 %shard_map.66.refs_1_ = bf16[4,512,2,256]{3,2,1,0:T(2,128)(2,1)S(1)} custom-call(bf16[512,2,4096]{2,1,0:T(2,128)(2,1)S(1)} %copy-done), custom_call_target="tpu_custom_call" | custom-call | bytes 2097152 | tf_op jit(solution)/shard_map/pallas_call | solution.py:106
  13.4 1.1 %shard_map.67.refs_1_.refs_2_ = bf16[4,512,2,256]{3,2,1,0:T(2,128)(2,1)S(1)} custom-call(bf16[512,2,4096]{2,1,0:T(2,128)(2,1)S(1)} %copy-done), custom_call_target="tpu_custom_call" | custom-call | bytes 2097152 | tf_op jit(solution)/shard_map/pallas_call | solution.py:106
  14.6 1.3 %collective-permute-done.3.refs_3_ = bf16[2,64,2,128]{3,2,1,0:T(2,128)(2,1)S(1)} collective-permute-done((bf16[2,64,2,128]{3,2,1,0:T(2,128)(2,1)S(1)}, bf16[2,64,2,128]{3,2,1,0:T(2,128)(2,1)S(1)}, u32[]{:S(2)}, u32[]{:S(2)}) %collective-permute-start.3) | collective-permute-done | bytes 65568 | tf_op jit(solution)/shard_map/ppermute | solution.py:142
  15.8 0.4 %collective-permute-done.4.refs_4_ = bf16[2,64,2,128]{3,2,1,0:T(2,128)(2,1)S(1)} collective-permute-done((bf16[2,64,2,128]{3,2,1,0:T(2,128)(2,1)S(1)}, bf16[2,64,2,128]{3,2,1,0:T(2,128)(2,1)S(1)}, u32[]{:S(2)}, u32[]{:S(2)}) %collective-permute-start.4) | collective-permute-done | bytes 65568 | tf_op jit(solution)/shard_map/ppermute | solution.py:142
  16.3 0.5 %collective-permute-start.7 = (bf16[2,64,2,128]{3,2,1,0:T(2,128)(2,1)S(1)}, bf16[2,64,2,128]{3,2,1,0:T(2,128)(2,1)S(1)}, u32[]{:S(2)}, u32[]{:S(2)}) collective-permute-start(bf16[2,64,2,128]{3,2,1,0:T(2,128)(2,1)S(1)} %collective-permute-done.4.refs_4_), channel_id=1, source_target_pairs={{0,1},{1,0},{2,3},{3,2},{4,5},{5,4},{6,7},{7,6},{8,9},{9,8},{10,11... | collective-permute-start | bytes 196616 | tf_op jit(solution)/shard_map/ppermute | solution.py:142
  16.8 0.7 %collective-permute-done.6.refs_6_ = bf16[2,64,2,128]{3,2,1,0:T(2,128)(2,1)S(1)} collective-permute-done((bf16[2,64,2,128]{3,2,1,0:T(2,128)(2,1)S(1)}, bf16[2,64,2,128]{3,2,1,0:T(2,128)(2,1)S(1)}, u32[]{:S(2)}, u32[]{:S(2)}) %collective-permute-start.6) | collective-permute-done | bytes 65568 | tf_op jit(solution)/shard_map/ppermute | solution.py:142
  17.5 0.2 collective-permute-done.7.refs_7_
  17.7 1.3 %shard_map.68 = bf16[128,128]{1,0:T(8,128)(2,1)S(1)} custom-call(bf16[2,64,2,128]{3,2,1,0:T(2,128)(2,1)S(1)} %pad_maximum_fusion.1.refs_0_, bf16[2,64,2,128]{3,2,1,0:T(2,128)(2,1)S(1)} %collective-permute-done.2.refs_1_, bf16[2,64,2,128]{3,2,1,0:T(2,128)(2,1)S(1)} %collective-permute-done.1.refs_2_, ...), custom_call_target="tpu_custom_call" | custom-call | tf_op jit(solution)/shard_map/pallas_call | solution.py:255
  19.0 2.5 %collective-permute-start.8 = (bf16[1,128,128]{2,1,0:T(8,128)(2,1)S(1)}, bf16[1,128,128]{2,1,0:T(8,128)(2,1)S(1)}, u32[]{:S(2)}, u32[]{:S(2)}) collective-permute-start(bf16[1,128,128]{2,1,0:T(8,128)(2,1)S(1)} %bitcast.3), channel_id=1, source_target_pairs={{0,8},{1,9},{2,10},{3,11},{4,12},{5,13},{6,14},{7,15},{8,0},{9,1},... | collective-permute-start | bytes 98312 | tf_op jit(solution)/shard_map/ppermute | solution.py:142
  21.6 2.2 %shard_map.69.refs_3_.refs_1_ = bf16[8,512,2,256]{3,2,1,0:T(2,128)(2,1)S(1)} custom-call(bf16[512,2,4096]{2,1,0:T(2,128)(2,1)S(1)} %copy-done), custom_call_target="tpu_custom_call" | custom-call | bytes 4194304 | tf_op jit(solution)/shard_map/pallas_call | solution.py:106
  23.8 0.5 %collective-permute-done.8 = bf16[1,128,128]{2,1,0:T(8,128)(2,1)S(1)} collective-permute-done((bf16[1,128,128]{2,1,0:T(8,128)(2,1)S(1)}, bf16[1,128,128]{2,1,0:T(8,128)(2,1)S(1)}, u32[]{:S(2)}, u32[]{:S(2)}) %collective-permute-start.8) | collective-permute-done | bytes 32800 | tf_op jit(solution)/shard_map/ppermute | solution.py:142
  24.4 1.2 %collective-permute-start.11 = (bf16[2,128,128]{2,1,0:T(8,128)(2,1)S(1)}, bf16[2,128,128]{2,1,0:T(8,128)(2,1)S(1)}, u32[]{:S(2)}, u32[]{:S(2)}) collective-permute-start(bf16[2,128,128]{2,1,0:T(8,128)(2,1)S(1)} %pad_maximum_fusion.2), channel_id=1, source_target_pairs={{0,4},{1,5},{2,6},{3,7},{4,0},{5,1},{6,2},{7,3},{8,12},{9,13},{10,... | collective-permute-start | bytes 196616 | tf_op jit(solution)/shard_map/ppermute | solution.py:142
  25.6 1.6 %collective-permute-start.10 = (bf16[4,128,128]{2,1,0:T(8,128)(2,1)S(1)}, bf16[4,128,128]{2,1,0:T(8,128)(2,1)S(1)}, u32[]{:S(2)}, u32[]{:S(2)}) collective-permute-start(bf16[4,128,128]{2,1,0:T(8,128)(2,1)S(1)} %pad_maximum_fusion.refs_0_), channel_id=1, source_target_pairs={{0,6},{1,3},{2,4},{3,1},{4,2},{5,7},{6,0},{7,5},{8,14},{9,11},{10,... | collective-permute-start | bytes 393224 | tf_op jit(solution)/shard_map/ppermute | solution.py:142
  27.3 0.8 %shard_map.70.refs_2_ = f32[1024,128]{1,0:T(8,128)S(1)} custom-call(bf16[4,128,128]{2,1,0:T(8,128)(2,1)S(1)} %pad_maximum_fusion.refs_0_, bf16[4,512,2,256]{3,2,1,0:T(2,128)(2,1)S(1)} %shard_map.66.refs_1_), custom_call_target="tpu_custom_call" | custom-call | tf_op jit(solution)/shard_map/pallas_call | solution.py:300
  28.1 0.8 %collective-permute-done.11.refs_0_ = bf16[2,128,128]{2,1,0:T(8,128)(2,1)S(1)} collective-permute-done((bf16[2,128,128]{2,1,0:T(8,128)(2,1)S(1)}, bf16[2,128,128]{2,1,0:T(8,128)(2,1)S(1)}, u32[]{:S(2)}, u32[]{:S(2)}) %collective-permute-start.11) | collective-permute-done | bytes 65568 | tf_op jit(solution)/shard_map/ppermute | solution.py:142
  28.9 0.5 %shard_map.71.refs_4_ = f32[1024,128]{1,0:T(8,128)S(1)} custom-call(bf16[2,128,128]{2,1,0:T(8,128)(2,1)S(1)} %collective-permute-done.11.refs_0_, bf16[4,512,2,256]{3,2,1,0:T(2,128)(2,1)S(1)} %shard_map.67.refs_1_.refs_2_, f32[1024,128]{1,0:T(8,128)S(1)} %shard_map.70.refs_2_), custom_call_target="tpu_custom_call" | custom-call | tf_op jit(solution)/shard_map/pallas_call | solution.py:300
  29.4 0.7 %collective-permute-done.12.refs_0_ = bf16[2,128,128]{2,1,0:T(8,128)(2,1)S(1)} collective-permute-done((bf16[2,128,128]{2,1,0:T(8,128)(2,1)S(1)}, bf16[2,128,128]{2,1,0:T(8,128)(2,1)S(1)}, u32[]{:S(2)}, u32[]{:S(2)}) %collective-permute-start.12) | collective-permute-done | bytes 65568 | tf_op jit(solution)/shard_map/ppermute | solution.py:142
  30.1 1.4 %collective-permute-done.10.refs_1_ = bf16[4,128,128]{2,1,0:T(8,128)(2,1)S(1)} collective-permute-done((bf16[4,128,128]{2,1,0:T(8,128)(2,1)S(1)}, bf16[4,128,128]{2,1,0:T(8,128)(2,1)S(1)}, u32[]{:S(2)}, u32[]{:S(2)}) %collective-permute-start.10) | collective-permute-done | bytes 131104 | tf_op jit(solution)/shard_map/ppermute | solution.py:142
  31.6 0.1 select_reduce_fusion
  31.7 1.1 %shard_map.72.refs_2_ = f32[1024,128]{1,0:T(8,128)S(1)} custom-call(bf16[2,128,128]{2,1,0:T(8,128)(2,1)S(1)} %collective-permute-done.12.refs_0_, bf16[4,128,128]{2,1,0:T(8,128)(2,1)S(1)} %collective-permute-done.10.refs_1_, bf16[4,512,2,256]{3,2,1,0:T(2,128)(2,1)S(1)} %shard_map.67.refs_1_.refs_2_, bf16[8,512,2,256]{3,2,1,0:T(2,128)(2,1)S(1)} %shard_map.69.refs_3_.refs_1_, ...), custom_call_target="tpu_custom_call" | custom-call | tf_op jit(solution)/shard_map/pallas_call | solution.py:300
  32.8 0.1 collective-permute-done.13.refs_0_
  32.9 1.6 %shard_map.73 = f32[32,512]{1,0:T(8,128)} custom-call(bf16[4,128,128]{2,1,0:T(8,128)(2,1)S(1)} %collective-permute-done.13.refs_0_, bf16[8,512,2,256]{3,2,1,0:T(2,128)(2,1)S(1)} %shard_map.69.refs_3_.refs_1_, f32[1024,128]{1,0:T(8,128)S(1)} %shard_map.72.refs_2_, f32[1,512]{1,0:T(1,128)S(1)} %bitcast.8), custom_call_target="tpu_custom_call" | custom-call | tf_op jit(solution)/shard_map/pallas_call | solution.py:329
  (21 shorter events, 0.4 us)
Async XLA Ops:
  0.7 0.8 %copy-start.2 = (bf16[2,2,64,128]{3,2,1,0:T(8,128)(2,1)S(1)}, bf16[2,2,64,128]{3,2,1,0:T(8,128)(2,1)}, u32[]{:S(2)}) copy-start(bf16[2,2,64,128]{3,2,1,0:T(8,128)(2,1)} %factors_ref.1) | copy-start | bytes 196612
  1.9 10.3 %copy-start = (bf16[512,2,4096]{2,1,0:T(2,128)(2,1)S(1)}, bf16[512,2,4096]{2,1,0:T(2,128)(2,1)}, u32[]{:S(2)}) copy-start(bf16[512,2,4096]{2,1,0:T(2,128)(2,1)} %source_ref.3) | copy-start | bytes 25165828
  1.9 6.6 %collective-permute-start = (bf16[1,64,2,128]{3,2,1,0:T(2,128)(2,1)S(1)}, bf16[1,64,2,128]{3,2,1,0:T(2,128)(2,1)S(1)}, u32[]{:S(2)}, u32[]{:S(2)}) collective-permute-start(bf16[1,64,2,128]{3,2,1,0:T(2,128)(2,1)S(1)} %bitcast.6), channel_id=1, source_target_pairs={{0,8},{1,9},{2,10},{3,11},{4,12},{5,13},{6,14},{7,15},{8,0},{9,1},... | collective-permute-start | bytes 98312 | tf_op jit(solution)/shard_map/ppermute | solution.py:142
  6.0 2.2 %copy-start.1 = (bf16[2,256,4096]{2,1,0:T(8,128)(2,1)S(1)}, bf16[2,256,4096]{2,1,0:T(8,128)(2,1)}, u32[]{:S(2)}) copy-start(bf16[2,256,4096]{2,1,0:T(8,128)(2,1)} %source_ref) | copy-start | bytes 12582916
  8.6 3.6 %collective-permute-start.2 = (bf16[2,64,2,128]{3,2,1,0:T(2,128)(2,1)S(1)}, bf16[2,64,2,128]{3,2,1,0:T(2,128)(2,1)S(1)}, u32[]{:S(2)}, u32[]{:S(2)}) collective-permute-start(bf16[2,64,2,128]{3,2,1,0:T(2,128)(2,1)S(1)} %pad_maximum_fusion.1.refs_0_), channel_id=1, source_target_pairs={{0,1},{1,0},{2,3},{3,2},{4,5},{5,4},{6,7},{7,6},{8,9},{9,8},{10,11... | collective-permute-start | bytes 196616 | tf_op jit(solution)/shard_map/ppermute | solution.py:142
  8.7 4.7 %collective-permute-start.1 = (bf16[2,64,2,128]{3,2,1,0:T(2,128)(2,1)S(1)}, bf16[2,64,2,128]{3,2,1,0:T(2,128)(2,1)S(1)}, u32[]{:S(2)}, u32[]{:S(2)}) collective-permute-start(bf16[2,64,2,128]{3,2,1,0:T(2,128)(2,1)S(1)} %pad_maximum_fusion.1.refs_0_), channel_id=1, source_target_pairs={{0,4},{1,7},{2,6},{3,5},{4,0},{5,3},{6,2},{7,1},{8,12},{9,15},{10,... | collective-permute-start | bytes 196616 | tf_op jit(solution)/shard_map/ppermute | solution.py:142
  10.3 5.5 %collective-permute-start.3 = (bf16[2,64,2,128]{3,2,1,0:T(2,128)(2,1)S(1)}, bf16[2,64,2,128]{3,2,1,0:T(2,128)(2,1)S(1)}, u32[]{:S(2)}, u32[]{:S(2)}) collective-permute-start(bf16[2,64,2,128]{3,2,1,0:T(2,128)(2,1)S(1)} %pad_maximum_fusion.1.refs_0_), channel_id=1, source_target_pairs={{0,6},{1,3},{2,4},{3,1},{4,2},{5,7},{6,0},{7,5},{8,14},{9,11},{10,... | collective-permute-start | bytes 196616 | tf_op jit(solution)/shard_map/ppermute | solution.py:142
  11.7 4.5 %collective-permute-start.4 = (bf16[2,64,2,128]{3,2,1,0:T(2,128)(2,1)S(1)}, bf16[2,64,2,128]{3,2,1,0:T(2,128)(2,1)S(1)}, u32[]{:S(2)}, u32[]{:S(2)}) collective-permute-start(bf16[2,64,2,128]{3,2,1,0:T(2,128)(2,1)S(1)} %pad_maximum_fusion.1.refs_0_), channel_id=1, source_target_pairs={{0,2},{1,5},{2,0},{3,7},{4,6},{5,1},{6,4},{7,3},{8,10},{9,13},{10,... | collective-permute-start | bytes 196616 | tf_op jit(solution)/shard_map/ppermute | solution.py:142
  13.4 2.9 %collective-permute-start.5 = (bf16[2,64,2,128]{3,2,1,0:T(2,128)(2,1)S(1)}, bf16[2,64,2,128]{3,2,1,0:T(2,128)(2,1)S(1)}, u32[]{:S(2)}, u32[]{:S(2)}) collective-permute-start(bf16[2,64,2,128]{3,2,1,0:T(2,128)(2,1)S(1)} %collective-permute-done.1.refs_2_), channel_id=1, source_target_pairs={{0,1},{1,0},{2,3},{3,2},{4,5},{5,4},{6,7},{7,6},{8,9},{9,8},{10,11... | collective-permute-start | bytes 196616 | tf_op jit(solution)/shard_map/ppermute | solution.py:142
  16.3 1.3 %collective-permute-start.6 = (bf16[2,64,2,128]{3,2,1,0:T(2,128)(2,1)S(1)}, bf16[2,64,2,128]{3,2,1,0:T(2,128)(2,1)S(1)}, u32[]{:S(2)}, u32[]{:S(2)}) collective-permute-start(bf16[2,64,2,128]{3,2,1,0:T(2,128)(2,1)S(1)} %collective-permute-done.3.refs_3_), channel_id=1, source_target_pairs={{0,1},{1,0},{2,3},{3,2},{4,5},{5,4},{6,7},{7,6},{8,9},{9,8},{10,11... | collective-permute-start | bytes 196616 | tf_op jit(solution)/shard_map/ppermute | solution.py:142
  16.3 1.4 %collective-permute-start.7 = (bf16[2,64,2,128]{3,2,1,0:T(2,128)(2,1)S(1)}, bf16[2,64,2,128]{3,2,1,0:T(2,128)(2,1)S(1)}, u32[]{:S(2)}, u32[]{:S(2)}) collective-permute-start(bf16[2,64,2,128]{3,2,1,0:T(2,128)(2,1)S(1)} %collective-permute-done.4.refs_4_), channel_id=1, source_target_pairs={{0,1},{1,0},{2,3},{3,2},{4,5},{5,4},{6,7},{7,6},{8,9},{9,8},{10,11... | collective-permute-start | bytes 196616 | tf_op jit(solution)/shard_map/ppermute | solution.py:142
  19.0 5.2 %collective-permute-start.8 = (bf16[1,128,128]{2,1,0:T(8,128)(2,1)S(1)}, bf16[1,128,128]{2,1,0:T(8,128)(2,1)S(1)}, u32[]{:S(2)}, u32[]{:S(2)}) collective-permute-start(bf16[1,128,128]{2,1,0:T(8,128)(2,1)S(1)} %bitcast.3), channel_id=1, source_target_pairs={{0,8},{1,9},{2,10},{3,11},{4,12},{5,13},{6,14},{7,15},{8,0},{9,1},... | collective-permute-start | bytes 98312 | tf_op jit(solution)/shard_map/ppermute | solution.py:142
  23.8 7.8 %copy-start.3 = (s32[512]{0:T(512)S(1)}, s32[512]{0:T(512)}, u32[]{:S(2)}) copy-start(s32[512]{0:T(512)} %param.10) | copy-start | bytes 6148
  23.8 7.8 %copy-start.4 = (f32[16]{0:T(128)S(1)}, f32[16]{0:T(128)}, u32[]{:S(2)}) copy-start(f32[16]{0:T(128)} %param.11) | copy-start | bytes 196
  24.3 1.3 %collective-permute-start.9 = (bf16[2,128,128]{2,1,0:T(8,128)(2,1)S(1)}, bf16[2,128,128]{2,1,0:T(8,128)(2,1)S(1)}, u32[]{:S(2)}, u32[]{:S(2)}) collective-permute-start(bf16[2,128,128]{2,1,0:T(8,128)(2,1)S(1)} %pad_maximum_fusion.2), channel_id=1, source_target_pairs={{0,1},{1,0},{2,3},{3,2},{4,5},{5,4},{6,7},{7,6},{8,9},{9,8},{10,11... | collective-permute-start | bytes 196616 | tf_op jit(solution)/shard_map/ppermute | solution.py:142
  24.4 4.5 %collective-permute-start.11 = (bf16[2,128,128]{2,1,0:T(8,128)(2,1)S(1)}, bf16[2,128,128]{2,1,0:T(8,128)(2,1)S(1)}, u32[]{:S(2)}, u32[]{:S(2)}) collective-permute-start(bf16[2,128,128]{2,1,0:T(8,128)(2,1)S(1)} %pad_maximum_fusion.2), channel_id=1, source_target_pairs={{0,4},{1,5},{2,6},{3,7},{4,0},{5,1},{6,2},{7,3},{8,12},{9,13},{10,... | collective-permute-start | bytes 196616 | tf_op jit(solution)/shard_map/ppermute | solution.py:142
  25.6 5.9 %collective-permute-start.10 = (bf16[4,128,128]{2,1,0:T(8,128)(2,1)S(1)}, bf16[4,128,128]{2,1,0:T(8,128)(2,1)S(1)}, u32[]{:S(2)}, u32[]{:S(2)}) collective-permute-start(bf16[4,128,128]{2,1,0:T(8,128)(2,1)S(1)} %pad_maximum_fusion.refs_0_), channel_id=1, source_target_pairs={{0,6},{1,3},{2,4},{3,1},{4,2},{5,7},{6,0},{7,5},{8,14},{9,11},{10,... | collective-permute-start | bytes 393224 | tf_op jit(solution)/shard_map/ppermute | solution.py:142
  28.9 1.3 %collective-permute-start.12 = (bf16[2,128,128]{2,1,0:T(8,128)(2,1)S(1)}, bf16[2,128,128]{2,1,0:T(8,128)(2,1)S(1)}, u32[]{:S(2)}, u32[]{:S(2)}) collective-permute-start(bf16[2,128,128]{2,1,0:T(8,128)(2,1)S(1)} %collective-permute-done.11.refs_0_), channel_id=1, source_target_pairs={{0,1},{1,0},{2,3},{3,2},{4,5},{5,4},{6,7},{7,6},{8,9},{9,8},{10,11... | collective-permute-start | bytes 196616 | tf_op jit(solution)/shard_map/ppermute | solution.py:142
  31.6 1.3 %collective-permute-start.13 = (bf16[4,128,128]{2,1,0:T(8,128)(2,1)S(1)}, bf16[4,128,128]{2,1,0:T(8,128)(2,1)S(1)}, u32[]{:S(2)}, u32[]{:S(2)}) collective-permute-start(bf16[4,128,128]{2,1,0:T(8,128)(2,1)S(1)} %collective-permute-done.10.refs_1_), channel_id=1, source_target_pairs={{0,1},{1,0},{2,3},{3,2},{4,5},{5,4},{6,7},{7,6},{8,9},{9,8},{10,11... | collective-permute-start | bytes 393224 | tf_op jit(solution)/shard_map/ppermute | solution.py:142

commit v5 on v4

--- a/solution.py
+++ b/solution.py
@@ -58,7 +58,7 @@
     for layer in range(layers):
         for query in range(queries):
             block = factors_ref[query, layer].astype(jnp.float32)
-            left = block[:, :rank].T * mask_ref[query : query + 1]
+            left = block[:, :rank].T * mask_ref[query : query + 1].astype(jnp.float32)
             outer_ref[...] = jnp.dot(
                 left.astype(jnp.bfloat16),
                 block[:, rank:].astype(jnp.bfloat16),
@@ -79,14 +79,18 @@
     return pl.pallas_call(
         grads_kernel,
         out_shape=jax.ShapeDtypeStruct((layers * tiles, queries, LANES), jnp.bfloat16),
-        in_specs=[IN_VMEM] * 2,
-        out_specs=IN_VMEM,
+        grid=(1,),
+        in_specs=[
+            pl.BlockSpec(factors.shape, lambda i: (0, 0, 0, 0)),
+            pl.BlockSpec(token_mask.shape, lambda i: (0, 0)),
+        ],
+        out_specs=pl.BlockSpec((layers * tiles, queries, LANES), lambda i: (0, 0, 0)),
         scratch_shapes=[
             pltpu.VMEM((rank, rank), jnp.float32),
             pltpu.VMEM((layers, tiles * queries, LANES), jnp.float32),
         ],
         compiler_params=PARAMS,
-    )(factors, token_mask.astype(jnp.float32))
+    )(factors, token_mask)
 
 
 def load_kernel(size, names, source_ref, out_ref, sem):
@@ -101,7 +105,7 @@
 def load_store(store, size, names, after):
     store, _ = lax.optimization_barrier((store, after))
     rows, layers, feats = store.shape
-    entries = sum(entry_count(name, size) for name in names)
+    entries = len(names) * entry_count(size)
     shape = (entries, rows, layers, feats // size)
     return pl.pallas_call(
         functools.partial(load_kernel, size, names),
@@ -146,10 +150,10 @@
     return [size >> k for k in range(1, size.bit_length()) if size >> k > 4]
 
 
-def gather_direct(chunk, size, early, middle, late):
+def gather(chunk, size, early, middle, late):
     share = chunk[None]
     for step in far_steps(size):
-        other = send(share, step, step, size)
+        other = send(share, step ^ 1, step ^ 1, size)
         if step == size // 2:
             other, *_ = lax.optimization_barrier((other, *early(share)))
         share = jnp.concatenate([share, other], axis=0)
@@ -163,59 +167,27 @@
     return got
 
 
-def gather_square(chunk, size, early, middle, late):
-    got = {}
-    share = chunk[None]
-    for step in far_steps(size):
-        other = send(share, step, step, size)
-        if step == size // 2:
-            other, *_ = lax.optimization_barrier((other, *early(share)))
-        share = jnp.concatenate([share, other], axis=0)
-    core = send(share, 1, 1, size)
-    near = send(share, 4, 4, size)
-    got["both"] = jnp.concatenate([share, core], axis=0)
-    corner = send(got["both"], 6, 2, size)
-    near, *_ = lax.optimization_barrier((near, *middle(got)))
-    got["near"] = near
-    got["core_near"] = send(near, 1, 1, size)
-    corner, *_ = lax.optimization_barrier((corner, got["core_near"], *late(got)))
-    got["corner"] = corner
-    got["core_corner"] = send(corner, 1, 1, size)
-    return got
-
-
 def owners(size):
     me = lax.axis_index("blk")
     core = me ^ 1
     is_odd = lax.rem(me, 2) == 1
     share = [0]
     for step in far_steps(size):
-        share = share + [step ^ entry for entry in share]
-    both = share + [1 ^ entry for entry in share]
-    places = {
-        "own": [me ^ entry for entry in share],
-        "core": [core ^ entry for entry in share],
-        "both": [me ^ entry for entry in both],
-        "near": [me ^ 4 ^ entry for entry in share],
-        "core_near": [core ^ 4 ^ entry for entry in share],
-    }
-    mine, theirs = jnp.where(is_odd, 2, 6), jnp.where(is_odd, 6, 2)
-    places["corner"] = [me ^ mine ^ entry for entry in both]
-    places["core_corner"] = [core ^ theirs ^ entry for entry in both]
+        share = share + [step ^ 1 ^ entry for entry in share]
+    places = {"own": [me ^ entry for entry in share], "core": [core ^ entry for entry in share]}
     for name, (even, odd) in zip(("one", "two", "three"), SQUARE):
-        mine, theirs = jnp.where(is_odd, odd, even), jnp.where(is_odd, even, odd)
+        mine, theirs = jnp.where(is_odd, even, odd), jnp.where(is_odd, odd, even)
         places[name] = [me ^ mine ^ entry for entry in share]
         places["core_" + name] = [core ^ theirs ^ entry for entry in share]
     return places
 
 
-def entry_count(name, size):
-    return (2 if name in TWICE else 1) << len(far_steps(size))
-
-
-SQUARE = ((4, 6), (6, 2), (2, 4))
-DIRECT = ("own", "core", "one", "two", "three", "core_one", "core_two", "core_three")
-TWICE = ("both", "corner", "core_corner")
+def entry_count(size):
+    return 1 << len(far_steps(size))
+
+
+SQUARE = ((7, 7), (5, 5), (3, 3))
+NAMES = ("own", "core", "one", "two", "three", "core_one", "core_two", "core_three")
 
 
 def fisher_kernel(size, *refs):
@@ -224,7 +196,7 @@
     tiles = feats // LANES
     queries = whole_ref.shape[2]
     places_of = owners(size)
-    for ref, name in zip(part_refs, DIRECT):
+    for ref, name in zip(part_refs, NAMES):
         for entry, place in enumerate(places_of[name]):
             whole_ref[place] = ref[entry]
     parts = []
@@ -255,11 +227,11 @@
     return pl.pallas_call(
         functools.partial(fisher_kernel, size),
         out_shape=jax.ShapeDtypeStruct((LANES, LANES), jnp.bfloat16),
-        in_specs=[IN_VMEM] * (len(DIRECT) + 1),
+        in_specs=[IN_VMEM] * (len(NAMES) + 1),
         out_specs=IN_VMEM,
         scratch_shapes=[pltpu.VMEM((size,) + chunk_shape, jnp.bfloat16)],
         compiler_params=PARAMS,
-    )(*[got[name] for name in DIRECT], inv_fisher)
+    )(*[got[name] for name in NAMES], inv_fisher)
 
 
 def products(chunk_refs, store_ref, start, total):
@@ -369,16 +341,15 @@
         def load(name, parts, after):
             return keep(name, load_store(store, size, parts, after))
 
-        homes = (("both",), ("near", "core_near"), ("corner", "core_corner"))
+        homes = (("own", "core"), ("one", "core_one"), ("two", "three", "core_two", "core_three"))
 
         def home_of(name):
             return next(k for k, home in enumerate(homes) if name in home)
 
         def start_of(name):
-            home = homes[home_of(name)]
-            return sum(entry_count(other, size) for other in home[: home.index(name)])
-
-        got = gather_direct(
+            return homes[home_of(name)].index(name) * entry_count(size)
+
+        got = gather(
             grads,
             size,
             lambda share: [keep("fisher", load_whole(inv_fisher, share))],
@@ -396,16 +367,16 @@
             )
             return keep("total", total)
 
-        got = gather_square(
+        got = gather(
             hidden,
             size,
             lambda share: [load(2, homes[2], share)],
-            lambda got: [add(got, "both")],
-            lambda got: [add(got, "near")],
-        )
-        add(got, "core_near", "corner")
+            lambda got: [add(got, "own", "core")],
+            lambda got: [add(got, "one")],
+        )
+        add(got, "core_one", "two", "three")
         return score_call(
-            [got["core_corner"]], ready[2], start_of("core_corner"),
+            [got["core_two"], got["core_three"]], ready[2], start_of("core_two"),
             ready["total"], scaling, factors.shape[0] * size,
         )
 

time: 34.7 us -> 33.8 us (0.974)
  waiting for transfers between devices: 6.28 us -> 4.75 us
  starting transfers between devices: 13.7 us -> 14.4 us
  other arithmetic: 0.88 us -> 0.19 us
  local copies, waits for them, and re-layouts: 3.05 us -> 3.72 us
    ppermute x14 -> x16, waiting for transfers between devices: 6.28 us -> 4.75 us  [send(): return lax.ppermute(value, 'blk', pairs)]
    ppermute x14 -> x16, starting transfers between devices: 13.7 us -> 14.4 us  [send(): return lax.ppermute(value, 'blk', pairs)]
    convert_element_type x1 -> x0, other arithmetic: 0.68 us -> none  [grads_call(): token_mask.astype(jnp.float32)]
    unnamed x10 -> x12, local copies, waits for them, and re-layouts: 3.05 us -> 3.72 us
  transfers between devices with their start and end apart: 14 -> 16, of which waited for: 10 -> 8; matrix products, arithmetic and copies ran while one was open for 0% -> 0% of each run, Pallas kernels for 21% -> 21%
where the time goes in v5:
time: 33.8 us; the launch traced here: 33.6 us
  starting transfers between devices  14.4 us (43%)
  Pallas kernels  10.4 us (31%)
  waiting for transfers between devices  4.75 us (14%)
  local copies, waits for them, and re-layouts  3.72 us (11%)
    ppermute x16, starting transfers between devices, send(): return lax.ppermute(value, 'blk', pairs)  14.4 us
    ppermute x16, waiting for transfers between devices, send(): return lax.ppermute(value, 'blk', pairs)  4.75 us
    pallas_call x3, Pallas kernels, load_store(): pl.pallas_call(functools.partial(load_kernel, size, names), out_shape=jax...  4.39 us
    unnamed x12, local copies, waits for them, and re-layouts  3.72 us
    pallas_call x3, Pallas kernels, partial_call(): pl.pallas_call(functools.partial(partial_kernel, tuple(starts)), out_shap...  2.42 us
    pallas_call x1, Pallas kernels, score_call(): pl.pallas_call(functools.partial(score_kernel, queries, start), out_shape...  1.6 us
    pallas_call x1, Pallas kernels, fisher_call(): pl.pallas_call(functools.partial(fisher_kernel, size), out_shape=jax.Shap...  1.35 us
  transfers between devices with their start and end apart: 16, of which 8 were waited for; matrix products, arithmetic and copies ran while one was open for 0% of the time, Pallas kernels for 21%

profile of v5, /device:TPU:0, one launch (start us, length us, event | category | flops | bytes accessed | tf_op | source)
XLA Modules:
  0.0 33.6 jit_solution(18102002060525548405)
XLA Ops:
  0.0 0.8 %copy-done.2 = bf16[2,2,64,128]{3,2,1,0:T(8,128)(2,1)S(1)} copy-done((bf16[2,2,64,128]{3,2,1,0:T(8,128)(2,1)S(1)}, bf16[2,2,64,128]{3,2,1,0:T(8,128)(2,1)}, u32[]{:S(2)}) %copy-start.2) | copy-done | bytes 65560
  0.8 0.7 %copy-done.3 = s32[2,64]{1,0:T(2,128)S(1)} copy-done((s32[2,64]{1,0:T(2,128)S(1)}, s32[2,64]{1,0:T(2,128)}, u32[]{:S(2)}) %copy-start.3) | copy-done | bytes 536
  1.5 0.3 %shard_map.64 = bf16[64,2,128]{2,1,0:T(2,128)(2,1)S(1)} custom-call(bf16[2,2,64,128]{3,2,1,0:T(8,128)(2,1)S(1)} %copy-done.2, s32[2,64]{1,0:T(2,128)S(1)} %copy-done.3), custom_call_target="tpu_custom_call" | custom-call | tf_op jit(solution)/shard_map/pallas_call | solution.py:79
  1.9 3.5 %collective-permute-start = (bf16[1,64,2,128]{3,2,1,0:T(2,128)(2,1)S(1)}, bf16[1,64,2,128]{3,2,1,0:T(2,128)(2,1)S(1)}, u32[]{:S(2)}, u32[]{:S(2)}) collective-permute-start(bf16[1,64,2,128]{3,2,1,0:T(2,128)(2,1)S(1)} %bitcast.5), channel_id=1, source_target_pairs={{0,9},{1,8},{2,11},{3,10},{4,13},{5,12},{6,15},{7,14},{8,1},{9,0},... | collective-permute-start | bytes 98312 | tf_op jit(solution)/shard_map/ppermute | solution.py:146
  5.4 2.2 %copy-done.1 = bf16[2,256,4096]{2,1,0:T(8,128)(2,1)S(1)} copy-done((bf16[2,256,4096]{2,1,0:T(8,128)(2,1)S(1)}, bf16[2,256,4096]{2,1,0:T(8,128)(2,1)}, u32[]{:S(2)}) %copy-start.1) | copy-done | bytes 4194328
  7.6 0.3 shard_map.65.refs_8_
  8.0 0.7 %collective-permute-start.2 = (bf16[2,64,2,128]{3,2,1,0:T(2,128)(2,1)S(1)}, bf16[2,64,2,128]{3,2,1,0:T(2,128)(2,1)S(1)}, u32[]{:S(2)}, u32[]{:S(2)}) collective-permute-start(bf16[2,64,2,128]{3,2,1,0:T(2,128)(2,1)S(1)} %pad_maximum_fusion.refs_0_), channel_id=1, source_target_pairs={{0,1},{1,0},{2,3},{3,2},{4,5},{5,4},{6,7},{7,6},{8,9},{9,8},{10,11... | collective-permute-start | bytes 196616 | tf_op jit(solution)/shard_map/ppermute | solution.py:146
  8.8 2.3 %collective-permute-start.1 = (bf16[2,64,2,128]{3,2,1,0:T(2,128)(2,1)S(1)}, bf16[2,64,2,128]{3,2,1,0:T(2,128)(2,1)S(1)}, u32[]{:S(2)}, u32[]{:S(2)}) collective-permute-start(bf16[2,64,2,128]{3,2,1,0:T(2,128)(2,1)S(1)} %pad_maximum_fusion.refs_0_), channel_id=1, source_target_pairs={{0,7},{1,6},{2,5},{3,4},{4,3},{5,2},{6,1},{7,0},{8,15},{9,14},{10,... | collective-permute-start | bytes 196616 | tf_op jit(solution)/shard_map/ppermute | solution.py:146
  11.0 0.4 %collective-permute-start.3 = (bf16[2,64,2,128]{3,2,1,0:T(2,128)(2,1)S(1)}, bf16[2,64,2,128]{3,2,1,0:T(2,128)(2,1)S(1)}, u32[]{:S(2)}, u32[]{:S(2)}) collective-permute-start(bf16[2,64,2,128]{3,2,1,0:T(2,128)(2,1)S(1)} %pad_maximum_fusion.refs_0_), channel_id=1, source_target_pairs={{0,5},{1,4},{2,7},{3,6},{4,1},{5,0},{6,3},{7,2},{8,13},{9,12},{10,... | collective-permute-start | bytes 196616 | tf_op jit(solution)/shard_map/ppermute | solution.py:146
  11.5 0.2 collective-permute-start.4
  11.7 1.1 %shard_map.66.refs_2_.refs_3_ = bf16[4,512,2,256]{3,2,1,0:T(2,128)(2,1)S(1)} custom-call(bf16[512,2,4096]{2,1,0:T(2,128)(2,1)S(1)} %copy-done), custom_call_target="tpu_custom_call" | custom-call | bytes 2097152 | tf_op jit(solution)/shard_map/pallas_call | solution.py:110
  12.8 1.0 %collective-permute-done.1.refs_2_ = bf16[2,64,2,128]{3,2,1,0:T(2,128)(2,1)S(1)} collective-permute-done((bf16[2,64,2,128]{3,2,1,0:T(2,128)(2,1)S(1)}, bf16[2,64,2,128]{3,2,1,0:T(2,128)(2,1)S(1)}, u32[]{:S(2)}, u32[]{:S(2)}) %collective-permute-start.1) | collective-permute-done | bytes 65568 | tf_op jit(solution)/shard_map/ppermute | solution.py:146
  13.9 1.1 %shard_map.67.refs_1_.refs_3_ = bf16[4,512,2,256]{3,2,1,0:T(2,128)(2,1)S(1)} custom-call(bf16[512,2,4096]{2,1,0:T(2,128)(2,1)S(1)} %copy-done), custom_call_target="tpu_custom_call" | custom-call | bytes 2097152 | tf_op jit(solution)/shard_map/pallas_call | solution.py:110
  15.1 0.4 %collective-permute-done.4.refs_4_ = bf16[2,64,2,128]{3,2,1,0:T(2,128)(2,1)S(1)} collective-permute-done((bf16[2,64,2,128]{3,2,1,0:T(2,128)(2,1)S(1)}, bf16[2,64,2,128]{3,2,1,0:T(2,128)(2,1)S(1)}, u32[]{:S(2)}, u32[]{:S(2)}) %collective-permute-start.4) | collective-permute-done | bytes 65568 | tf_op jit(solution)/shard_map/ppermute | solution.py:146
  15.7 0.4 %collective-permute-start.7 = (bf16[2,64,2,128]{3,2,1,0:T(2,128)(2,1)S(1)}, bf16[2,64,2,128]{3,2,1,0:T(2,128)(2,1)S(1)}, u32[]{:S(2)}, u32[]{:S(2)}) collective-permute-start(bf16[2,64,2,128]{3,2,1,0:T(2,128)(2,1)S(1)} %collective-permute-done.4.refs_4_), channel_id=1, source_target_pairs={{0,1},{1,0},{2,3},{3,2},{4,5},{5,4},{6,7},{7,6},{8,9},{9,8},{10,11... | collective-permute-start | bytes 196616 | tf_op jit(solution)/shard_map/ppermute | solution.py:146
  16.0 0.7 %collective-permute-done.6.refs_6_ = bf16[2,64,2,128]{3,2,1,0:T(2,128)(2,1)S(1)} collective-permute-done((bf16[2,64,2,128]{3,2,1,0:T(2,128)(2,1)S(1)}, bf16[2,64,2,128]{3,2,1,0:T(2,128)(2,1)S(1)}, u32[]{:S(2)}, u32[]{:S(2)}) %collective-permute-start.6) | collective-permute-done | bytes 65568 | tf_op jit(solution)/shard_map/ppermute | solution.py:146
  16.9 1.4 %shard_map.68 = bf16[128,128]{1,0:T(8,128)(2,1)S(1)} custom-call(bf16[2,64,2,128]{3,2,1,0:T(2,128)(2,1)S(1)} %pad_maximum_fusion.refs_0_, bf16[2,64,2,128]{3,2,1,0:T(2,128)(2,1)S(1)} %collective-permute-done.2.refs_1_, bf16[2,64,2,128]{3,2,1,0:T(2,128)(2,1)S(1)} %collective-permute-done.1.refs_2_, ...), custom_call_target="tpu_custom_call" | custom-call | tf_op jit(solution)/shard_map/pallas_call | solution.py:227
  18.3 2.6 %collective-permute-start.8 = (bf16[1,128,128]{2,1,0:T(8,128)(2,1)S(1)}, bf16[1,128,128]{2,1,0:T(8,128)(2,1)S(1)}, u32[]{:S(2)}, u32[]{:S(2)}) collective-permute-start(bf16[1,128,128]{2,1,0:T(8,128)(2,1)S(1)} %bitcast.3), channel_id=1, source_target_pairs={{0,9},{1,8},{2,11},{3,10},{4,13},{5,12},{6,15},{7,14},{8,1},{9,0},... | collective-permute-start | bytes 98312 | tf_op jit(solution)/shard_map/ppermute | solution.py:146
  20.9 2.2 %shard_map.69.refs_4_.refs_5_.refs_2_ = bf16[8,512,2,256]{3,2,1,0:T(2,128)(2,1)S(1)} custom-call(bf16[512,2,4096]{2,1,0:T(2,128)(2,1)S(1)} %copy-done), custom_call_target="tpu_custom_call" | custom-call | bytes 4194304 | tf_op jit(solution)/shard_map/pallas_call | solution.py:110
  23.2 0.2 collective-permute-start.12
  23.4 2.6 %collective-permute-start.11 = (bf16[2,128,128]{2,1,0:T(8,128)(2,1)S(1)}, bf16[2,128,128]{2,1,0:T(8,128)(2,1)S(1)}, u32[]{:S(2)}, u32[]{:S(2)}) collective-permute-start(bf16[2,128,128]{2,1,0:T(8,128)(2,1)S(1)} %pad_maximum_fusion.1.refs_0_), channel_id=1, source_target_pairs={{0,7},{1,6},{2,5},{3,4},{4,3},{5,2},{6,1},{7,0},{8,15},{9,14},{10,... | collective-permute-start | bytes 196616 | tf_op jit(solution)/shard_map/ppermute | solution.py:146
  26.0 0.3 collective-permute-start.10
  26.3 0.2 collective-permute-start.9
  26.6 0.8 %shard_map.70.refs_2_ = f32[1024,128]{1,0:T(8,128)S(1)} custom-call(bf16[2,128,128]{2,1,0:T(8,128)(2,1)S(1)} %pad_maximum_fusion.1.refs_0_, bf16[2,128,128]{2,1,0:T(8,128)(2,1)S(1)} %collective-permute-done.12.refs_1_, bf16[4,512,2,256]{3,2,1,0:T(2,128)(2,1)S(1)} %shard_map.66.refs_2_.refs_3_, bf16[4,512,2,256]{3,2,1,0:T(2,128)(2,1)S(1)} %shard_map.66.refs_2_.refs_3_), custom_call_target="tpu_custom_call" | custom-call | tf_op jit(solution)/shard_map/pallas_call | solution.py:272
  27.4 1.1 %collective-permute-done.11.refs_0_ = bf16[2,128,128]{2,1,0:T(8,128)(2,1)S(1)} collective-permute-done((bf16[2,128,128]{2,1,0:T(8,128)(2,1)S(1)}, bf16[2,128,128]{2,1,0:T(8,128)(2,1)S(1)}, u32[]{:S(2)}, u32[]{:S(2)}) %collective-permute-start.11) | collective-permute-done | bytes 65568 | tf_op jit(solution)/shard_map/ppermute | solution.py:146
  28.5 0.5 %shard_map.71.refs_6_ = f32[1024,128]{1,0:T(8,128)S(1)} custom-call(bf16[2,128,128]{2,1,0:T(8,128)(2,1)S(1)} %collective-permute-done.11.refs_0_, bf16[4,512,2,256]{3,2,1,0:T(2,128)(2,1)S(1)} %shard_map.67.refs_1_.refs_3_, f32[1024,128]{1,0:T(8,128)S(1)} %shard_map.70.refs_2_), custom_call_target="tpu_custom_call" | custom-call | tf_op jit(solution)/shard_map/pallas_call | solution.py:272
  29.0 1.1 %collective-permute-done.10.refs_2_ = bf16[2,128,128]{2,1,0:T(8,128)(2,1)S(1)} collective-permute-done((bf16[2,128,128]{2,1,0:T(8,128)(2,1)S(1)}, bf16[2,128,128]{2,1,0:T(8,128)(2,1)S(1)}, u32[]{:S(2)}, u32[]{:S(2)}) %collective-permute-start.10) | collective-permute-done | bytes 65568 | tf_op jit(solution)/shard_map/ppermute | solution.py:146
  30.1 0.2 collective-permute-done.9.refs_1_
  30.3 0.3 collective-permute-start.14
  30.6 0.2 collective-permute-start.15
  30.9 1.1 %shard_map.72.refs_3_ = f32[1024,128]{1,0:T(8,128)S(1)} custom-call(bf16[2,128,128]{2,1,0:T(8,128)(2,1)S(1)} %collective-permute-done.13.refs_0_, bf16[2,128,128]{2,1,0:T(8,128)(2,1)S(1)} %collective-permute-done.9.refs_1_, bf16[2,128,128]{2,1,0:T(8,128)(2,1)S(1)} %collective-permute-done.10.refs_2_, bf16[4,512,2,256]{3,2,1,0:T(2,128)(2,1)S(1)} %shard_map.67.refs_1_.refs_3_, ...), custom_call_target="tpu_custom_call" | custom-call | tf_op jit(solution)/shard_map/pallas_call | solution.py:272
  32.0 1.6 %shard_map.73 = f32[32,512]{1,0:T(8,128)} custom-call(bf16[2,128,128]{2,1,0:T(8,128)(2,1)S(1)} %collective-permute-done.14.refs_0_, bf16[2,128,128]{2,1,0:T(8,128)(2,1)S(1)} %collective-permute-done.15.refs_1_, bf16[8,512,2,256]{3,2,1,0:T(2,128)(2,1)S(1)} %shard_map.69.refs_4_.refs_5_.refs_2_, f32[1024,128]{1,0:T(8,128)S(1)} %shard_map.72.refs_3_, ...), custom_call_target="tpu_custom_call" | custom-call | tf_op jit(solution)/shard_map/pallas_call | solution.py:301
  (25 shorter events, 0.8 us)
Async XLA Ops:
  0.0 0.8 %copy-start.2 = (bf16[2,2,64,128]{3,2,1,0:T(8,128)(2,1)S(1)}, bf16[2,2,64,128]{3,2,1,0:T(8,128)(2,1)}, u32[]{:S(2)}) copy-start(bf16[2,2,64,128]{3,2,1,0:T(8,128)(2,1)} %factors_ref.1) | copy-start | bytes 196612
  0.8 0.7 %copy-start.3 = (s32[2,64]{1,0:T(2,128)S(1)}, s32[2,64]{1,0:T(2,128)}, u32[]{:S(2)}) copy-start(s32[2,64]{1,0:T(2,128)} %mask_ref.1) | copy-start | bytes 1540
  1.9 9.8 %copy-start = (bf16[512,2,4096]{2,1,0:T(2,128)(2,1)S(1)}, bf16[512,2,4096]{2,1,0:T(2,128)(2,1)}, u32[]{:S(2)}) copy-start(bf16[512,2,4096]{2,1,0:T(2,128)(2,1)} %source_ref.3) | copy-start | bytes 25165828
  1.9 6.0 %collective-permute-start = (bf16[1,64,2,128]{3,2,1,0:T(2,128)(2,1)S(1)}, bf16[1,64,2,128]{3,2,1,0:T(2,128)(2,1)S(1)}, u32[]{:S(2)}, u32[]{:S(2)}) collective-permute-start(bf16[1,64,2,128]{3,2,1,0:T(2,128)(2,1)S(1)} %bitcast.5), channel_id=1, source_target_pairs={{0,9},{1,8},{2,11},{3,10},{4,13},{5,12},{6,15},{7,14},{8,1},{9,0},... | collective-permute-start | bytes 98312 | tf_op jit(solution)/shard_map/ppermute | solution.py:146
  5.4 2.2 %copy-start.1 = (bf16[2,256,4096]{2,1,0:T(8,128)(2,1)S(1)}, bf16[2,256,4096]{2,1,0:T(8,128)(2,1)}, u32[]{:S(2)}) copy-start(bf16[2,256,4096]{2,1,0:T(8,128)(2,1)} %source_ref) | copy-start | bytes 12582916
  8.0 3.6 %collective-permute-start.2 = (bf16[2,64,2,128]{3,2,1,0:T(2,128)(2,1)S(1)}, bf16[2,64,2,128]{3,2,1,0:T(2,128)(2,1)S(1)}, u32[]{:S(2)}, u32[]{:S(2)}) collective-permute-start(bf16[2,64,2,128]{3,2,1,0:T(2,128)(2,1)S(1)} %pad_maximum_fusion.refs_0_), channel_id=1, source_target_pairs={{0,1},{1,0},{2,3},{3,2},{4,5},{5,4},{6,7},{7,6},{8,9},{9,8},{10,11... | collective-permute-start | bytes 196616 | tf_op jit(solution)/shard_map/ppermute | solution.py:146
  8.8 5.0 %collective-permute-start.1 = (bf16[2,64,2,128]{3,2,1,0:T(2,128)(2,1)S(1)}, bf16[2,64,2,128]{3,2,1,0:T(2,128)(2,1)S(1)}, u32[]{:S(2)}, u32[]{:S(2)}) collective-permute-start(bf16[2,64,2,128]{3,2,1,0:T(2,128)(2,1)S(1)} %pad_maximum_fusion.refs_0_), channel_id=1, source_target_pairs={{0,7},{1,6},{2,5},{3,4},{4,3},{5,2},{6,1},{7,0},{8,15},{9,14},{10,... | collective-permute-start | bytes 196616 | tf_op jit(solution)/shard_map/ppermute | solution.py:146
  11.0 4.1 %collective-permute-start.3 = (bf16[2,64,2,128]{3,2,1,0:T(2,128)(2,1)S(1)}, bf16[2,64,2,128]{3,2,1,0:T(2,128)(2,1)S(1)}, u32[]{:S(2)}, u32[]{:S(2)}) collective-permute-start(bf16[2,64,2,128]{3,2,1,0:T(2,128)(2,1)S(1)} %pad_maximum_fusion.refs_0_), channel_id=1, source_target_pairs={{0,5},{1,4},{2,7},{3,6},{4,1},{5,0},{6,3},{7,2},{8,13},{9,12},{10,... | collective-permute-start | bytes 196616 | tf_op jit(solution)/shard_map/ppermute | solution.py:146
  11.5 4.1 %collective-permute-start.4 = (bf16[2,64,2,128]{3,2,1,0:T(2,128)(2,1)S(1)}, bf16[2,64,2,128]{3,2,1,0:T(2,128)(2,1)S(1)}, u32[]{:S(2)}, u32[]{:S(2)}) collective-permute-start(bf16[2,64,2,128]{3,2,1,0:T(2,128)(2,1)S(1)} %pad_maximum_fusion.refs_0_), channel_id=1, source_target_pairs={{0,3},{1,2},{2,1},{3,0},{4,7},{5,6},{6,5},{7,4},{8,11},{9,10},{10,... | collective-permute-start | bytes 196616 | tf_op jit(solution)/shard_map/ppermute | solution.py:146
  13.8 1.7 %collective-permute-start.5 = (bf16[2,64,2,128]{3,2,1,0:T(2,128)(2,1)S(1)}, bf16[2,64,2,128]{3,2,1,0:T(2,128)(2,1)S(1)}, u32[]{:S(2)}, u32[]{:S(2)}) collective-permute-start(bf16[2,64,2,128]{3,2,1,0:T(2,128)(2,1)S(1)} %collective-permute-done.1.refs_2_), channel_id=1, source_target_pairs={{0,1},{1,0},{2,3},{3,2},{4,5},{5,4},{6,7},{7,6},{8,9},{9,8},{10,11... | collective-permute-start | bytes 196616 | tf_op jit(solution)/shard_map/ppermute | solution.py:146
  15.5 1.3 %collective-permute-start.6 = (bf16[2,64,2,128]{3,2,1,0:T(2,128)(2,1)S(1)}, bf16[2,64,2,128]{3,2,1,0:T(2,128)(2,1)S(1)}, u32[]{:S(2)}, u32[]{:S(2)}) collective-permute-start(bf16[2,64,2,128]{3,2,1,0:T(2,128)(2,1)S(1)} %collective-permute-done.3.refs_3_), channel_id=1, source_target_pairs={{0,1},{1,0},{2,3},{3,2},{4,5},{5,4},{6,7},{7,6},{8,9},{9,8},{10,11... | collective-permute-start | bytes 196616 | tf_op jit(solution)/shard_map/ppermute | solution.py:146
  15.7 1.3 %collective-permute-start.7 = (bf16[2,64,2,128]{3,2,1,0:T(2,128)(2,1)S(1)}, bf16[2,64,2,128]{3,2,1,0:T(2,128)(2,1)S(1)}, u32[]{:S(2)}, u32[]{:S(2)}) collective-permute-start(bf16[2,64,2,128]{3,2,1,0:T(2,128)(2,1)S(1)} %collective-permute-done.4.refs_4_), channel_id=1, source_target_pairs={{0,1},{1,0},{2,3},{3,2},{4,5},{5,4},{6,7},{7,6},{8,9},{9,8},{10,11... | collective-permute-start | bytes 196616 | tf_op jit(solution)/shard_map/ppermute | solution.py:146
  18.3 4.9 %collective-permute-start.8 = (bf16[1,128,128]{2,1,0:T(8,128)(2,1)S(1)}, bf16[1,128,128]{2,1,0:T(8,128)(2,1)S(1)}, u32[]{:S(2)}, u32[]{:S(2)}) collective-permute-start(bf16[1,128,128]{2,1,0:T(8,128)(2,1)S(1)} %bitcast.3), channel_id=1, source_target_pairs={{0,9},{1,8},{2,11},{3,10},{4,13},{5,12},{6,15},{7,14},{8,1},{9,0},... | collective-permute-start | bytes 98312 | tf_op jit(solution)/shard_map/ppermute | solution.py:146
  23.1 7.7 %copy-start.4 = (s32[512]{0:T(512)S(1)}, s32[512]{0:T(512)}, u32[]{:S(2)}) copy-start(s32[512]{0:T(512)} %param.10) | copy-start | bytes 6148
  23.1 7.6 %copy-start.5 = (f32[16]{0:T(128)S(1)}, f32[16]{0:T(128)}, u32[]{:S(2)}) copy-start(f32[16]{0:T(128)} %param.11) | copy-start | bytes 196
  23.2 3.4 %collective-permute-start.12 = (bf16[2,128,128]{2,1,0:T(8,128)(2,1)S(1)}, bf16[2,128,128]{2,1,0:T(8,128)(2,1)S(1)}, u32[]{:S(2)}, u32[]{:S(2)}) collective-permute-start(bf16[2,128,128]{2,1,0:T(8,128)(2,1)S(1)} %pad_maximum_fusion.1.refs_0_), channel_id=1, source_target_pairs={{0,1},{1,0},{2,3},{3,2},{4,5},{5,4},{6,7},{7,6},{8,9},{9,8},{10,11... | collective-permute-start | bytes 196616 | tf_op jit(solution)/shard_map/ppermute | solution.py:146
  23.4 5.1 %collective-permute-start.11 = (bf16[2,128,128]{2,1,0:T(8,128)(2,1)S(1)}, bf16[2,128,128]{2,1,0:T(8,128)(2,1)S(1)}, u32[]{:S(2)}, u32[]{:S(2)}) collective-permute-start(bf16[2,128,128]{2,1,0:T(8,128)(2,1)S(1)} %pad_maximum_fusion.1.refs_0_), channel_id=1, source_target_pairs={{0,7},{1,6},{2,5},{3,4},{4,3},{5,2},{6,1},{7,0},{8,15},{9,14},{10,... | collective-permute-start | bytes 196616 | tf_op jit(solution)/shard_map/ppermute | solution.py:146
  26.0 4.1 %collective-permute-start.10 = (bf16[2,128,128]{2,1,0:T(8,128)(2,1)S(1)}, bf16[2,128,128]{2,1,0:T(8,128)(2,1)S(1)}, u32[]{:S(2)}, u32[]{:S(2)}) collective-permute-start(bf16[2,128,128]{2,1,0:T(8,128)(2,1)S(1)} %pad_maximum_fusion.1.refs_0_), channel_id=1, source_target_pairs={{0,3},{1,2},{2,1},{3,0},{4,7},{5,6},{6,5},{7,4},{8,11},{9,10},{10,... | collective-permute-start | bytes 196616 | tf_op jit(solution)/shard_map/ppermute | solution.py:146
  26.3 3.9 %collective-permute-start.9 = (bf16[2,128,128]{2,1,0:T(8,128)(2,1)S(1)}, bf16[2,128,128]{2,1,0:T(8,128)(2,1)S(1)}, u32[]{:S(2)}, u32[]{:S(2)}) collective-permute-start(bf16[2,128,128]{2,1,0:T(8,128)(2,1)S(1)} %pad_maximum_fusion.1.refs_0_), channel_id=1, source_target_pairs={{0,5},{1,4},{2,7},{3,6},{4,1},{5,0},{6,3},{7,2},{8,13},{9,12},{10,... | collective-permute-start | bytes 196616 | tf_op jit(solution)/shard_map/ppermute | solution.py:146
  28.5 1.8 %collective-permute-start.13 = (bf16[2,128,128]{2,1,0:T(8,128)(2,1)S(1)}, bf16[2,128,128]{2,1,0:T(8,128)(2,1)S(1)}, u32[]{:S(2)}, u32[]{:S(2)}) collective-permute-start(bf16[2,128,128]{2,1,0:T(8,128)(2,1)S(1)} %collective-permute-done.11.refs_0_), channel_id=1, source_target_pairs={{0,1},{1,0},{2,3},{3,2},{4,5},{5,4},{6,7},{7,6},{8,9},{9,8},{10,11... | collective-permute-start | bytes 196616 | tf_op jit(solution)/shard_map/ppermute | solution.py:146
  30.3 1.7 %collective-permute-start.14 = (bf16[2,128,128]{2,1,0:T(8,128)(2,1)S(1)}, bf16[2,128,128]{2,1,0:T(8,128)(2,1)S(1)}, u32[]{:S(2)}, u32[]{:S(2)}) collective-permute-start(bf16[2,128,128]{2,1,0:T(8,128)(2,1)S(1)} %collective-permute-done.9.refs_1_), channel_id=1, source_target_pairs={{0,1},{1,0},{2,3},{3,2},{4,5},{5,4},{6,7},{7,6},{8,9},{9,8},{10,11... | collective-permute-start | bytes 196616 | tf_op jit(solution)/shard_map/ppermute | solution.py:146
  30.6 1.5 %collective-permute-start.15 = (bf16[2,128,128]{2,1,0:T(8,128)(2,1)S(1)}, bf16[2,128,128]{2,1,0:T(8,128)(2,1)S(1)}, u32[]{:S(2)}, u32[]{:S(2)}) collective-permute-start(bf16[2,128,128]{2,1,0:T(8,128)(2,1)S(1)} %collective-permute-done.10.refs_2_), channel_id=1, source_target_pairs={{0,1},{1,0},{2,3},{3,2},{4,5},{5,4},{6,7},{7,6},{8,9},{9,8},{10,11... | collective-permute-start | bytes 196616 | tf_op jit(solution)/shard_map/ppermute | solution.py:146

commit v6 on v5

--- a/solution.py
+++ b/solution.py
@@ -89,13 +89,14 @@
             pltpu.VMEM((rank, rank), jnp.float32),
             pltpu.VMEM((layers, tiles * queries, LANES), jnp.float32),
         ],
+        cost_estimate=pl.CostEstimate(flops=10**10, bytes_accessed=0, transcendentals=0),
         compiler_params=PARAMS,
     )(factors, token_mask)
 
 
 def load_kernel(size, names, source_ref, out_ref, sem):
     width = out_ref.shape[-1]
-    places = owners(size)
+    places = owners(size, SECOND)
     for entry, owner in enumerate(sum([places[name] for name in names], [])):
         columns = pl.ds(pl.multiple_of(owner * width, width), width)
         pltpu.make_async_copy(source_ref.at[:, :, columns], out_ref.at[entry], sem).start()
@@ -150,15 +151,15 @@
     return [size >> k for k in range(1, size.bit_length()) if size >> k > 4]
 
 
-def gather(chunk, size, early, middle, late):
+def gather(chunk, size, plan, early, middle, late):
     share = chunk[None]
     for step in far_steps(size):
-        other = send(share, step ^ 1, step ^ 1, size)
+        other = send(share, step ^ plan[0], step ^ plan[0], size)
         if step == size // 2:
             other, *_ = lax.optimization_barrier((other, *early(share)))
         share = jnp.concatenate([share, other], axis=0)
     got = {"own": share, "core": send(share, 1, 1, size)}
-    one, two, three = (send(share, even, odd, size) for even, odd in SQUARE)
+    one, two, three = (send(share, even, odd, size) for even, odd in plan[1])
     one, got["core"], *_ = lax.optimization_barrier((one, got["core"], *middle(got)))
     got.update(one=one, core_one=send(one, 1, 1, size))
     two, three, *_ = lax.optimization_barrier((two, three, got["core_one"], *late(got)))
@@ -167,16 +168,18 @@
     return got
 
 
-def owners(size):
+def owners(size, plan):
     me = lax.axis_index("blk")
     core = me ^ 1
     is_odd = lax.rem(me, 2) == 1
     share = [0]
     for step in far_steps(size):
-        share = share + [step ^ 1 ^ entry for entry in share]
+        share = share + [step ^ plan[0] ^ entry for entry in share]
     places = {"own": [me ^ entry for entry in share], "core": [core ^ entry for entry in share]}
-    for name, (even, odd) in zip(("one", "two", "three"), SQUARE):
-        mine, theirs = jnp.where(is_odd, even, odd), jnp.where(is_odd, odd, even)
+    for name, (even, odd) in zip(("one", "two", "three"), plan[1]):
+        if even % 2:
+            even, odd = odd, even
+        mine, theirs = jnp.where(is_odd, odd, even), jnp.where(is_odd, even, odd)
         places[name] = [me ^ mine ^ entry for entry in share]
         places["core_" + name] = [core ^ theirs ^ entry for entry in share]
     return places
@@ -186,7 +189,8 @@
     return 1 << len(far_steps(size))
 
 
-SQUARE = ((7, 7), (5, 5), (3, 3))
+FIRST = (1, ((7, 7), (5, 5), (3, 3)))
+SECOND = (1, ((7, 7), (5, 5), (3, 3)))
 NAMES = ("own", "core", "one", "two", "three", "core_one", "core_two", "core_three")
 
 
@@ -195,7 +199,7 @@
     layers, rows, feats = fisher_ref.shape
     tiles = feats // LANES
     queries = whole_ref.shape[2]
-    places_of = owners(size)
+    places_of = owners(size, FIRST)
     for ref, name in zip(part_refs, NAMES):
         for entry, place in enumerate(places_of[name]):
             whole_ref[place] = ref[entry]
@@ -341,7 +345,12 @@
         def load(name, parts, after):
             return keep(name, load_store(store, size, parts, after))
 
-        homes = (("own", "core"), ("one", "core_one"), ("two", "three", "core_two", "core_three"))
+        homes = (
+            ("own", "core"),
+            ("one", "core_one"),
+            ("two", "three"),
+            ("core_two", "core_three"),
+        )
 
         def home_of(name):
             return next(k for k, home in enumerate(homes) if name in home)
@@ -352,6 +361,7 @@
         got = gather(
             grads,
             size,
+            FIRST,
             lambda share: [keep("fisher", load_whole(inv_fisher, share))],
             lambda got: [load(0, homes[0], got["core"])],
             lambda got: [load(1, homes[1], got["one"])],
@@ -370,13 +380,14 @@
         got = gather(
             hidden,
             size,
+            SECOND,
             lambda share: [load(2, homes[2], share)],
-            lambda got: [add(got, "own", "core")],
+            lambda got: [add(got, "own", "core"), load(3, homes[3], got["core"])],
             lambda got: [add(got, "one")],
         )
         add(got, "core_one", "two", "three")
         return score_call(
-            [got["core_two"], got["core_three"]], ready[2], start_of("core_two"),
+            [got["core_two"], got["core_three"]], ready[3], start_of("core_two"),
             ready["total"], scaling, factors.shape[0] * size,
         )
 

time: 33.8 us -> 33.1 us (0.979)
  local copies, waits for them, and re-layouts: 3.72 us -> 1.54 us
  starting transfers between devices: 14.4 us -> 15.2 us
  waiting for transfers between devices: 4.75 us -> 5.43 us
    unnamed x12, local copies, waits for them, and re-layouts: 3.72 us -> 1.54 us
    ppermute x16, starting transfers between devices: 14.4 us -> 15.2 us  [send(): return lax.ppermute(value, 'blk', pairs)]
    ppermute x16, waiting for transfers between devices: 4.75 us -> 5.43 us  [send(): return lax.ppermute(value, 'blk', pairs)]
    pallas_call x3 -> x4, Pallas kernels: 4.39 us -> 4.42 us  [load_store(): pl.pallas_call(functools.partial(load_kernel, size, names), out_shape=jax...]
  transfers between devices with their start and end apart: 16 -> 16, of which waited for: 8 -> 8; matrix products, arithmetic and copies ran while one was open for 0% -> 0% of each run, Pallas kernels for 21% -> 22%
where the time goes in v6:
time: 33.1 us; the launch traced here: 32.9 us
  starting transfers between devices  15.2 us (46%)
  Pallas kernels  10.4 us (31%)
  waiting for transfers between devices  5.43 us (16%)
  local copies, waits for them, and re-layouts  1.54 us (5%)
    ppermute x16, starting transfers between devices, send(): return lax.ppermute(value, 'blk', pairs)  15.2 us
    ppermute x16, waiting for transfers between devices, send(): return lax.ppermute(value, 'blk', pairs)  5.43 us
    pallas_call x4, Pallas kernels, load_store(): pl.pallas_call(functools.partial(load_kernel, size, names), out_shape=jax...  4.42 us
    pallas_call x3, Pallas kernels, partial_call(): pl.pallas_call(functools.partial(partial_kernel, tuple(starts)), out_shap...  2.42 us
    pallas_call x1, Pallas kernels, score_call(): pl.pallas_call(functools.partial(score_kernel, queries, start), out_shape...  1.6 us
    unnamed x12, local copies, waits for them, and re-layouts  1.54 us
    pallas_call x1, Pallas kernels, fisher_call(): pl.pallas_call(functools.partial(fisher_kernel, size), out_shape=jax.Shap...  1.35 us
  transfers between devices with their start and end apart: 16, of which 8 were waited for; matrix products, arithmetic and copies ran while one was open for 0% of the time, Pallas kernels for 22%

profile of v6, /device:TPU:0, one launch (start us, length us, event | category | flops | bytes accessed | tf_op | source)
XLA Modules:
  0.0 32.9 jit_solution(4884273730901581316)
XLA Ops:
  0.0 0.8 %copy-done.2 = bf16[2,2,64,128]{3,2,1,0:T(8,128)(2,1)S(1)} copy-done((bf16[2,2,64,128]{3,2,1,0:T(8,128)(2,1)S(1)}, bf16[2,2,64,128]{3,2,1,0:T(8,128)(2,1)}, u32[]{:S(2)}) %copy-start.2) | copy-done | bytes 65560
  0.8 0.7 %copy-done.3 = s32[2,64]{1,0:T(2,128)S(1)} copy-done((s32[2,64]{1,0:T(2,128)S(1)}, s32[2,64]{1,0:T(2,128)}, u32[]{:S(2)}) %copy-start.3) | copy-done | bytes 536
  1.5 0.3 %shard_map.64 = bf16[64,2,128]{2,1,0:T(2,128)(2,1)S(1)} custom-call(bf16[2,2,64,128]{3,2,1,0:T(8,128)(2,1)S(1)} %copy-done.2, s32[2,64]{1,0:T(2,128)S(1)} %copy-done.3), custom_call_target="tpu_custom_call" | custom-call | flops 10000000000 | tf_op jit(solution)/shard_map/pallas_call | solution.py:79
  1.9 3.5 %collective-permute-start = (bf16[1,64,2,128]{3,2,1,0:T(2,128)(2,1)S(1)}, bf16[1,64,2,128]{3,2,1,0:T(2,128)(2,1)S(1)}, u32[]{:S(2)}, u32[]{:S(2)}) collective-permute-start(bf16[1,64,2,128]{3,2,1,0:T(2,128)(2,1)S(1)} %bitcast.5), channel_id=1, source_target_pairs={{0,9},{1,8},{2,11},{3,10},{4,13},{5,12},{6,15},{7,14},{8,1},{9,0},... | collective-permute-start | bytes 98312 | tf_op jit(solution)/shard_map/ppermute | solution.py:147
  5.4 0.3 shard_map.65.refs_8_
  5.7 1.5 %collective-permute-done = bf16[1,64,2,128]{3,2,1,0:T(2,128)(2,1)S(1)} collective-permute-done((bf16[1,64,2,128]{3,2,1,0:T(2,128)(2,1)S(1)}, bf16[1,64,2,128]{3,2,1,0:T(2,128)(2,1)S(1)}, u32[]{:S(2)}, u32[]{:S(2)}) %collective-permute-start) | collective-permute-done | bytes 32800 | tf_op jit(solution)/shard_map/ppermute | solution.py:147
  7.3 0.6 %collective-permute-start.2 = (bf16[2,64,2,128]{3,2,1,0:T(2,128)(2,1)S(1)}, bf16[2,64,2,128]{3,2,1,0:T(2,128)(2,1)S(1)}, u32[]{:S(2)}, u32[]{:S(2)}) collective-permute-start(bf16[2,64,2,128]{3,2,1,0:T(2,128)(2,1)S(1)} %pad_maximum_fusion.refs_0_), channel_id=1, source_target_pairs={{0,1},{1,0},{2,3},{3,2},{4,5},{5,4},{6,7},{7,6},{8,9},{9,8},{10,11... | collective-permute-start | bytes 196616 | tf_op jit(solution)/shard_map/ppermute | solution.py:147
  7.9 2.7 %collective-permute-start.1 = (bf16[2,64,2,128]{3,2,1,0:T(2,128)(2,1)S(1)}, bf16[2,64,2,128]{3,2,1,0:T(2,128)(2,1)S(1)}, u32[]{:S(2)}, u32[]{:S(2)}) collective-permute-start(bf16[2,64,2,128]{3,2,1,0:T(2,128)(2,1)S(1)} %pad_maximum_fusion.refs_0_), channel_id=1, source_target_pairs={{0,7},{1,6},{2,5},{3,4},{4,3},{5,2},{6,1},{7,0},{8,15},{9,14},{10,... | collective-permute-start | bytes 196616 | tf_op jit(solution)/shard_map/ppermute | solution.py:147
  10.5 0.2 collective-permute-start.3
  10.9 1.1 %shard_map.66.refs_2_.refs_3_ = bf16[4,512,2,256]{3,2,1,0:T(2,128)(2,1)S(1)} custom-call(bf16[512,2,4096]{2,1,0:T(2,128)(2,1)S(1)} %copy-done), custom_call_target="tpu_custom_call" | custom-call | bytes 2097152 | tf_op jit(solution)/shard_map/pallas_call | solution.py:111
  12.0 1.0 %collective-permute-done.1.refs_2_ = bf16[2,64,2,128]{3,2,1,0:T(2,128)(2,1)S(1)} collective-permute-done((bf16[2,64,2,128]{3,2,1,0:T(2,128)(2,1)S(1)}, bf16[2,64,2,128]{3,2,1,0:T(2,128)(2,1)S(1)}, u32[]{:S(2)}, u32[]{:S(2)}) %collective-permute-start.1) | collective-permute-done | bytes 65568 | tf_op jit(solution)/shard_map/ppermute | solution.py:147
  13.0 1.1 %shard_map.67.refs_1_.refs_3_ = bf16[4,512,2,256]{3,2,1,0:T(2,128)(2,1)S(1)} custom-call(bf16[512,2,4096]{2,1,0:T(2,128)(2,1)S(1)} %copy-done), custom_call_target="tpu_custom_call" | custom-call | bytes 2097152 | tf_op jit(solution)/shard_map/pallas_call | solution.py:111
  14.1 0.5 %collective-permute-done.3.refs_3_ = bf16[2,64,2,128]{3,2,1,0:T(2,128)(2,1)S(1)} collective-permute-done((bf16[2,64,2,128]{3,2,1,0:T(2,128)(2,1)S(1)}, bf16[2,64,2,128]{3,2,1,0:T(2,128)(2,1)S(1)}, u32[]{:S(2)}, u32[]{:S(2)}) %collective-permute-start.3) | collective-permute-done | bytes 65568 | tf_op jit(solution)/shard_map/ppermute | solution.py:147
  14.7 0.3 collective-permute-start.6
  15.0 0.2 collective-permute-start.7
  15.2 0.7 %collective-permute-done.6.refs_6_ = bf16[2,64,2,128]{3,2,1,0:T(2,128)(2,1)S(1)} collective-permute-done((bf16[2,64,2,128]{3,2,1,0:T(2,128)(2,1)S(1)}, bf16[2,64,2,128]{3,2,1,0:T(2,128)(2,1)S(1)}, u32[]{:S(2)}, u32[]{:S(2)}) %collective-permute-start.6) | collective-permute-done | bytes 65568 | tf_op jit(solution)/shard_map/ppermute | solution.py:147
  15.9 0.3 collective-permute-done.7.refs_7_
  16.2 1.4 %shard_map.68 = bf16[128,128]{1,0:T(8,128)(2,1)S(1)} custom-call(bf16[2,64,2,128]{3,2,1,0:T(2,128)(2,1)S(1)} %pad_maximum_fusion.refs_0_, bf16[2,64,2,128]{3,2,1,0:T(2,128)(2,1)S(1)} %collective-permute-done.2.refs_1_, bf16[2,64,2,128]{3,2,1,0:T(2,128)(2,1)S(1)} %collective-permute-done.1.refs_2_, ...), custom_call_target="tpu_custom_call" | custom-call | tf_op jit(solution)/shard_map/pallas_call | solution.py:231
  17.6 3.3 %collective-permute-start.8 = (bf16[1,128,128]{2,1,0:T(8,128)(2,1)S(1)}, bf16[1,128,128]{2,1,0:T(8,128)(2,1)S(1)}, u32[]{:S(2)}, u32[]{:S(2)}) collective-permute-start(bf16[1,128,128]{2,1,0:T(8,128)(2,1)S(1)} %bitcast.3), channel_id=1, source_target_pairs={{0,9},{1,8},{2,11},{3,10},{4,13},{5,12},{6,15},{7,14},{8,1},{9,0},... | collective-permute-start | bytes 98312 | tf_op jit(solution)/shard_map/ppermute | solution.py:147
  20.9 1.1 %shard_map.69.refs_4_.refs_5_ = bf16[4,512,2,256]{3,2,1,0:T(2,128)(2,1)S(1)} custom-call(bf16[512,2,4096]{2,1,0:T(2,128)(2,1)S(1)} %copy-done), custom_call_target="tpu_custom_call" | custom-call | bytes 2097152 | tf_op jit(solution)/shard_map/pallas_call | solution.py:111
  22.0 0.5 %collective-permute-done.8 = bf16[1,128,128]{2,1,0:T(8,128)(2,1)S(1)} collective-permute-done((bf16[1,128,128]{2,1,0:T(8,128)(2,1)S(1)}, bf16[1,128,128]{2,1,0:T(8,128)(2,1)S(1)}, u32[]{:S(2)}, u32[]{:S(2)}) %collective-permute-start.8) | collective-permute-done | bytes 32800 | tf_op jit(solution)/shard_map/ppermute | solution.py:147
  22.6 0.2 collective-permute-start.12
  22.8 2.6 %collective-permute-start.11 = (bf16[2,128,128]{2,1,0:T(8,128)(2,1)S(1)}, bf16[2,128,128]{2,1,0:T(8,128)(2,1)S(1)}, u32[]{:S(2)}, u32[]{:S(2)}) collective-permute-start(bf16[2,128,128]{2,1,0:T(8,128)(2,1)S(1)} %pad_maximum_fusion.1.refs_0_), channel_id=1, source_target_pairs={{0,7},{1,6},{2,5},{3,4},{4,3},{5,2},{6,1},{7,0},{8,15},{9,14},{10,... | collective-permute-start | bytes 196616 | tf_op jit(solution)/shard_map/ppermute | solution.py:147
  25.4 0.5 %collective-permute-start.10 = (bf16[2,128,128]{2,1,0:T(8,128)(2,1)S(1)}, bf16[2,128,128]{2,1,0:T(8,128)(2,1)S(1)}, u32[]{:S(2)}, u32[]{:S(2)}) collective-permute-start(bf16[2,128,128]{2,1,0:T(8,128)(2,1)S(1)} %pad_maximum_fusion.1.refs_0_), channel_id=1, source_target_pairs={{0,3},{1,2},{2,1},{3,0},{4,7},{5,6},{6,5},{7,4},{8,11},{9,10},{10,... | collective-permute-start | bytes 196616 | tf_op jit(solution)/shard_map/ppermute | solution.py:147
  26.0 1.1 %shard_map.71.refs_2_ = bf16[4,512,2,256]{3,2,1,0:T(2,128)(2,1)S(1)} custom-call(bf16[512,2,4096]{2,1,0:T(2,128)(2,1)S(1)} %copy-done), custom_call_target="tpu_custom_call" | custom-call | bytes 2097152 | tf_op jit(solution)/shard_map/pallas_call | solution.py:111
  27.1 0.8 %shard_map.70.refs_2_ = f32[1024,128]{1,0:T(8,128)S(1)} custom-call(bf16[2,128,128]{2,1,0:T(8,128)(2,1)S(1)} %pad_maximum_fusion.1.refs_0_, bf16[2,128,128]{2,1,0:T(8,128)(2,1)S(1)} %collective-permute-done.12.refs_1_, bf16[4,512,2,256]{3,2,1,0:T(2,128)(2,1)S(1)} %shard_map.66.refs_2_.refs_3_, bf16[4,512,2,256]{3,2,1,0:T(2,128)(2,1)S(1)} %shard_map.66.refs_2_.refs_3_), custom_call_target="tpu_custom_call" | custom-call | tf_op jit(solution)/shard_map/pallas_call | solution.py:276
  27.9 0.3 collective-permute-start.13
  28.2 0.5 %shard_map.72.refs_6_ = f32[1024,128]{1,0:T(8,128)S(1)} custom-call(bf16[2,128,128]{2,1,0:T(8,128)(2,1)S(1)} %collective-permute-done.11.refs_0_, bf16[4,512,2,256]{3,2,1,0:T(2,128)(2,1)S(1)} %shard_map.67.refs_1_.refs_3_, f32[1024,128]{1,0:T(8,128)S(1)} %shard_map.70.refs_2_), custom_call_target="tpu_custom_call" | custom-call | tf_op jit(solution)/shard_map/pallas_call | solution.py:276
  28.7 0.9 %collective-permute-done.9.refs_1_ = bf16[2,128,128]{2,1,0:T(8,128)(2,1)S(1)} collective-permute-done((bf16[2,128,128]{2,1,0:T(8,128)(2,1)S(1)}, bf16[2,128,128]{2,1,0:T(8,128)(2,1)S(1)}, u32[]{:S(2)}, u32[]{:S(2)}) %collective-permute-start.9) | collective-permute-done | bytes 65568 | tf_op jit(solution)/shard_map/ppermute | solution.py:147
  29.7 0.4 %collective-permute-start.15 = (bf16[2,128,128]{2,1,0:T(8,128)(2,1)S(1)}, bf16[2,128,128]{2,1,0:T(8,128)(2,1)S(1)}, u32[]{:S(2)}, u32[]{:S(2)}) collective-permute-start(bf16[2,128,128]{2,1,0:T(8,128)(2,1)S(1)} %collective-permute-done.10.refs_2_), channel_id=1, source_target_pairs={{0,1},{1,0},{2,3},{3,2},{4,5},{5,4},{6,7},{7,6},{8,9},{9,8},{10,11... | collective-permute-start | bytes 196616 | tf_op jit(solution)/shard_map/ppermute | solution.py:147
  30.2 1.1 %shard_map.73.refs_3_ = f32[1024,128]{1,0:T(8,128)S(1)} custom-call(bf16[2,128,128]{2,1,0:T(8,128)(2,1)S(1)} %collective-permute-done.13.refs_0_, bf16[2,128,128]{2,1,0:T(8,128)(2,1)S(1)} %collective-permute-done.9.refs_1_, bf16[2,128,128]{2,1,0:T(8,128)(2,1)S(1)} %collective-permute-done.10.refs_2_, bf16[4,512,2,256]{3,2,1,0:T(2,128)(2,1)S(1)} %shard_map.67.refs_1_.refs_3_, ...), custom_call_target="tpu_custom_call" | custom-call | tf_op jit(solution)/shard_map/pallas_call | solution.py:276
  31.3 1.6 %shard_map.74 = f32[32,512]{1,0:T(8,128)} custom-call(bf16[2,128,128]{2,1,0:T(8,128)(2,1)S(1)} %collective-permute-done.14.refs_0_, bf16[2,128,128]{2,1,0:T(8,128)(2,1)S(1)} %collective-permute-done.15.refs_1_, bf16[4,512,2,256]{3,2,1,0:T(2,128)(2,1)S(1)} %shard_map.71.refs_2_, f32[1024,128]{1,0:T(8,128)S(1)} %shard_map.73.refs_3_, f32[1,512]{1,0:T(1,128)S(1)} %bitcast.7), custom_call_target="tpu_custom_call" | custom-call | tf_op jit(solution)/shard_map/pallas_call | solution.py:305
  (26 shorter events, 0.6 us)
Async XLA Ops:
  0.0 0.8 %copy-start.2 = (bf16[2,2,64,128]{3,2,1,0:T(8,128)(2,1)S(1)}, bf16[2,2,64,128]{3,2,1,0:T(8,128)(2,1)}, u32[]{:S(2)}) copy-start(bf16[2,2,64,128]{3,2,1,0:T(8,128)(2,1)} %factors_ref.1) | copy-start | bytes 196612
  0.8 0.7 %copy-start.3 = (s32[2,64]{1,0:T(2,128)S(1)}, s32[2,64]{1,0:T(2,128)}, u32[]{:S(2)}) copy-start(s32[2,64]{1,0:T(2,128)} %mask_ref.1) | copy-start | bytes 1540
  1.5 3.9 %copy-start.1 = (bf16[2,256,4096]{2,1,0:T(8,128)(2,1)S(1)}, bf16[2,256,4096]{2,1,0:T(8,128)(2,1)}, u32[]{:S(2)}) copy-start(bf16[2,256,4096]{2,1,0:T(8,128)(2,1)} %source_ref) | copy-start | bytes 12582916
  1.9 5.3 %collective-permute-start = (bf16[1,64,2,128]{3,2,1,0:T(2,128)(2,1)S(1)}, bf16[1,64,2,128]{3,2,1,0:T(2,128)(2,1)S(1)}, u32[]{:S(2)}, u32[]{:S(2)}) collective-permute-start(bf16[1,64,2,128]{3,2,1,0:T(2,128)(2,1)S(1)} %bitcast.5), channel_id=1, source_target_pairs={{0,9},{1,8},{2,11},{3,10},{4,13},{5,12},{6,15},{7,14},{8,1},{9,0},... | collective-permute-start | bytes 98312 | tf_op jit(solution)/shard_map/ppermute | solution.py:147
  5.4 5.5 %copy-start = (bf16[512,2,4096]{2,1,0:T(2,128)(2,1)S(1)}, bf16[512,2,4096]{2,1,0:T(2,128)(2,1)}, u32[]{:S(2)}) copy-start(bf16[512,2,4096]{2,1,0:T(2,128)(2,1)} %source_ref.4) | copy-start | bytes 25165828
  7.3 3.6 %collective-permute-start.2 = (bf16[2,64,2,128]{3,2,1,0:T(2,128)(2,1)S(1)}, bf16[2,64,2,128]{3,2,1,0:T(2,128)(2,1)S(1)}, u32[]{:S(2)}, u32[]{:S(2)}) collective-permute-start(bf16[2,64,2,128]{3,2,1,0:T(2,128)(2,1)S(1)} %pad_maximum_fusion.refs_0_), channel_id=1, source_target_pairs={{0,1},{1,0},{2,3},{3,2},{4,5},{5,4},{6,7},{7,6},{8,9},{9,8},{10,11... | collective-permute-start | bytes 196616 | tf_op jit(solution)/shard_map/ppermute | solution.py:147
  7.9 5.1 %collective-permute-start.1 = (bf16[2,64,2,128]{3,2,1,0:T(2,128)(2,1)S(1)}, bf16[2,64,2,128]{3,2,1,0:T(2,128)(2,1)S(1)}, u32[]{:S(2)}, u32[]{:S(2)}) collective-permute-start(bf16[2,64,2,128]{3,2,1,0:T(2,128)(2,1)S(1)} %pad_maximum_fusion.refs_0_), channel_id=1, source_target_pairs={{0,7},{1,6},{2,5},{3,4},{4,3},{5,2},{6,1},{7,0},{8,15},{9,14},{10,... | collective-permute-start | bytes 196616 | tf_op jit(solution)/shard_map/ppermute | solution.py:147
  10.5 4.1 %collective-permute-start.3 = (bf16[2,64,2,128]{3,2,1,0:T(2,128)(2,1)S(1)}, bf16[2,64,2,128]{3,2,1,0:T(2,128)(2,1)S(1)}, u32[]{:S(2)}, u32[]{:S(2)}) collective-permute-start(bf16[2,64,2,128]{3,2,1,0:T(2,128)(2,1)S(1)} %pad_maximum_fusion.refs_0_), channel_id=1, source_target_pairs={{0,5},{1,4},{2,7},{3,6},{4,1},{5,0},{6,3},{7,2},{8,13},{9,12},{10,... | collective-permute-start | bytes 196616 | tf_op jit(solution)/shard_map/ppermute | solution.py:147
  10.7 3.9 %collective-permute-start.4 = (bf16[2,64,2,128]{3,2,1,0:T(2,128)(2,1)S(1)}, bf16[2,64,2,128]{3,2,1,0:T(2,128)(2,1)S(1)}, u32[]{:S(2)}, u32[]{:S(2)}) collective-permute-start(bf16[2,64,2,128]{3,2,1,0:T(2,128)(2,1)S(1)} %pad_maximum_fusion.refs_0_), channel_id=1, source_target_pairs={{0,3},{1,2},{2,1},{3,0},{4,7},{5,6},{6,5},{7,4},{8,11},{9,10},{10,... | collective-permute-start | bytes 196616 | tf_op jit(solution)/shard_map/ppermute | solution.py:147
  13.0 1.7 %collective-permute-start.5 = (bf16[2,64,2,128]{3,2,1,0:T(2,128)(2,1)S(1)}, bf16[2,64,2,128]{3,2,1,0:T(2,128)(2,1)S(1)}, u32[]{:S(2)}, u32[]{:S(2)}) collective-permute-start(bf16[2,64,2,128]{3,2,1,0:T(2,128)(2,1)S(1)} %collective-permute-done.1.refs_2_), channel_id=1, source_target_pairs={{0,1},{1,0},{2,3},{3,2},{4,5},{5,4},{6,7},{7,6},{8,9},{9,8},{10,11... | collective-permute-start | bytes 196616 | tf_op jit(solution)/shard_map/ppermute | solution.py:147
  14.7 1.3 %collective-permute-start.6 = (bf16[2,64,2,128]{3,2,1,0:T(2,128)(2,1)S(1)}, bf16[2,64,2,128]{3,2,1,0:T(2,128)(2,1)S(1)}, u32[]{:S(2)}, u32[]{:S(2)}) collective-permute-start(bf16[2,64,2,128]{3,2,1,0:T(2,128)(2,1)S(1)} %collective-permute-done.3.refs_3_), channel_id=1, source_target_pairs={{0,1},{1,0},{2,3},{3,2},{4,5},{5,4},{6,7},{7,6},{8,9},{9,8},{10,11... | collective-permute-start | bytes 196616 | tf_op jit(solution)/shard_map/ppermute | solution.py:147
  15.0 1.3 %collective-permute-start.7 = (bf16[2,64,2,128]{3,2,1,0:T(2,128)(2,1)S(1)}, bf16[2,64,2,128]{3,2,1,0:T(2,128)(2,1)S(1)}, u32[]{:S(2)}, u32[]{:S(2)}) collective-permute-start(bf16[2,64,2,128]{3,2,1,0:T(2,128)(2,1)S(1)} %collective-permute-done.4.refs_4_), channel_id=1, source_target_pairs={{0,1},{1,0},{2,3},{3,2},{4,5},{5,4},{6,7},{7,6},{8,9},{9,8},{10,11... | collective-permute-start | bytes 196616 | tf_op jit(solution)/shard_map/ppermute | solution.py:147
  17.6 5.0 %collective-permute-start.8 = (bf16[1,128,128]{2,1,0:T(8,128)(2,1)S(1)}, bf16[1,128,128]{2,1,0:T(8,128)(2,1)S(1)}, u32[]{:S(2)}, u32[]{:S(2)}) collective-permute-start(bf16[1,128,128]{2,1,0:T(8,128)(2,1)S(1)} %bitcast.3), channel_id=1, source_target_pairs={{0,9},{1,8},{2,11},{3,10},{4,13},{5,12},{6,15},{7,14},{8,1},{9,0},... | collective-permute-start | bytes 98312 | tf_op jit(solution)/shard_map/ppermute | solution.py:147
  22.6 3.4 %collective-permute-start.12 = (bf16[2,128,128]{2,1,0:T(8,128)(2,1)S(1)}, bf16[2,128,128]{2,1,0:T(8,128)(2,1)S(1)}, u32[]{:S(2)}, u32[]{:S(2)}) collective-permute-start(bf16[2,128,128]{2,1,0:T(8,128)(2,1)S(1)} %pad_maximum_fusion.1.refs_0_), channel_id=1, source_target_pairs={{0,1},{1,0},{2,3},{3,2},{4,5},{5,4},{6,7},{7,6},{8,9},{9,8},{10,11... | collective-permute-start | bytes 196616 | tf_op jit(solution)/shard_map/ppermute | solution.py:147
  22.8 5.1 %collective-permute-start.11 = (bf16[2,128,128]{2,1,0:T(8,128)(2,1)S(1)}, bf16[2,128,128]{2,1,0:T(8,128)(2,1)S(1)}, u32[]{:S(2)}, u32[]{:S(2)}) collective-permute-start(bf16[2,128,128]{2,1,0:T(8,128)(2,1)S(1)} %pad_maximum_fusion.1.refs_0_), channel_id=1, source_target_pairs={{0,7},{1,6},{2,5},{3,4},{4,3},{5,2},{6,1},{7,0},{8,15},{9,14},{10,... | collective-permute-start | bytes 196616 | tf_op jit(solution)/shard_map/ppermute | solution.py:147
  25.4 4.1 %collective-permute-start.9 = (bf16[2,128,128]{2,1,0:T(8,128)(2,1)S(1)}, bf16[2,128,128]{2,1,0:T(8,128)(2,1)S(1)}, u32[]{:S(2)}, u32[]{:S(2)}) collective-permute-start(bf16[2,128,128]{2,1,0:T(8,128)(2,1)S(1)} %pad_maximum_fusion.1.refs_0_), channel_id=1, source_target_pairs={{0,5},{1,4},{2,7},{3,6},{4,1},{5,0},{6,3},{7,2},{8,13},{9,12},{10,... | collective-permute-start | bytes 196616 | tf_op jit(solution)/shard_map/ppermute | solution.py:147
  25.4 4.1 %collective-permute-start.10 = (bf16[2,128,128]{2,1,0:T(8,128)(2,1)S(1)}, bf16[2,128,128]{2,1,0:T(8,128)(2,1)S(1)}, u32[]{:S(2)}, u32[]{:S(2)}) collective-permute-start(bf16[2,128,128]{2,1,0:T(8,128)(2,1)S(1)} %pad_maximum_fusion.1.refs_0_), channel_id=1, source_target_pairs={{0,3},{1,2},{2,1},{3,0},{4,7},{5,6},{6,5},{7,4},{8,11},{9,10},{10,... | collective-permute-start | bytes 196616 | tf_op jit(solution)/shard_map/ppermute | solution.py:147
  27.9 2.2 %copy-start.4 = (s32[512]{0:T(512)S(1)}, s32[512]{0:T(512)}, u32[]{:S(2)}) copy-start(s32[512]{0:T(512)} %param.10) | copy-start | bytes 6148
  27.9 2.2 %copy-start.5 = (f32[16]{0:T(128)S(1)}, f32[16]{0:T(128)}, u32[]{:S(2)}) copy-start(f32[16]{0:T(128)} %param.11) | copy-start | bytes 196
  27.9 1.6 %collective-permute-start.13 = (bf16[2,128,128]{2,1,0:T(8,128)(2,1)S(1)}, bf16[2,128,128]{2,1,0:T(8,128)(2,1)S(1)}, u32[]{:S(2)}, u32[]{:S(2)}) collective-permute-start(bf16[2,128,128]{2,1,0:T(8,128)(2,1)S(1)} %collective-permute-done.11.refs_0_), channel_id=1, source_target_pairs={{0,1},{1,0},{2,3},{3,2},{4,5},{5,4},{6,7},{7,6},{8,9},{9,8},{10,11... | collective-permute-start | bytes 196616 | tf_op jit(solution)/shard_map/ppermute | solution.py:147
  29.6 1.7 %collective-permute-start.14 = (bf16[2,128,128]{2,1,0:T(8,128)(2,1)S(1)}, bf16[2,128,128]{2,1,0:T(8,128)(2,1)S(1)}, u32[]{:S(2)}, u32[]{:S(2)}) collective-permute-start(bf16[2,128,128]{2,1,0:T(8,128)(2,1)S(1)} %collective-permute-done.9.refs_1_), channel_id=1, source_target_pairs={{0,1},{1,0},{2,3},{3,2},{4,5},{5,4},{6,7},{7,6},{8,9},{9,8},{10,11... | collective-permute-start | bytes 196616 | tf_op jit(solution)/shard_map/ppermute | solution.py:147
  29.7 1.6 %collective-permute-start.15 = (bf16[2,128,128]{2,1,0:T(8,128)(2,1)S(1)}, bf16[2,128,128]{2,1,0:T(8,128)(2,1)S(1)}, u32[]{:S(2)}, u32[]{:S(2)}) collective-permute-start(bf16[2,128,128]{2,1,0:T(8,128)(2,1)S(1)} %collective-permute-done.10.refs_2_), channel_id=1, source_target_pairs={{0,1},{1,0},{2,3},{3,2},{4,5},{5,4},{6,7},{7,6},{8,9},{9,8},{10,11... | collective-permute-start | bytes 196616 | tf_op jit(solution)/shard_map/ppermute | solution.py:147

commit v7 on v6

--- a/solution.py
+++ b/solution.py
@@ -152,17 +152,26 @@
 
 
 def gather(chunk, size, plan, early, middle, late):
+    flip, square, late_core = plan
     share = chunk[None]
     for step in far_steps(size):
-        other = send(share, step ^ plan[0], step ^ plan[0], size)
+        other = send(share, step ^ flip, step ^ flip, size)
         if step == size // 2:
             other, *_ = lax.optimization_barrier((other, *early(share)))
         share = jnp.concatenate([share, other], axis=0)
-    got = {"own": share, "core": send(share, 1, 1, size)}
-    one, two, three = (send(share, even, odd, size) for even, odd in plan[1])
-    one, got["core"], *_ = lax.optimization_barrier((one, got["core"], *middle(got)))
+    one, two, three = (send(share, even, odd, size) for even, odd in square)
+    got = {"own": share}
+    if late_core:
+        one, *_ = lax.optimization_barrier((one, *middle(got)))
+        held, _ = lax.optimization_barrier((share, one))
+        got["core"] = send(held, 1, 1, size)
+    else:
+        got["core"] = send(share, 1, 1, size)
+        one, got["core"], *_ = lax.optimization_barrier((one, got["core"], *middle(got)))
     got.update(one=one, core_one=send(one, 1, 1, size))
-    two, three, *_ = lax.optimization_barrier((two, three, got["core_one"], *late(got)))
+    two, three, *_ = lax.optimization_barrier(
+        (two, three, got["core"], got["core_one"], *late(got))
+    )
     got.update(two=two, core_two=send(two, 1, 1, size))
     got.update(three=three, core_three=send(three, 1, 1, size))
     return got
@@ -189,8 +198,8 @@
     return 1 << len(far_steps(size))
 
 
-FIRST = (1, ((7, 7), (5, 5), (3, 3)))
-SECOND = (1, ((7, 7), (5, 5), (3, 3)))
+FIRST = (1, ((7, 7), (5, 5), (3, 3)), True)
+SECOND = (1, ((7, 7), (5, 5), (3, 3)), False)
 NAMES = ("own", "core", "one", "two", "three", "core_one", "core_two", "core_three")
 
 
@@ -363,7 +372,7 @@
             size,
             FIRST,
             lambda share: [keep("fisher", load_whole(inv_fisher, share))],
-            lambda got: [load(0, homes[0], got["core"])],
+            lambda got: [load(0, homes[0], got["own"])],
             lambda got: [load(1, homes[1], got["one"])],
         )
         hidden = fisher_call(got, ready["fisher"], size)

time: 33.1 us -> 32.7 us (0.988)
  waiting for transfers between devices: 5.43 us -> 4.75 us
    ppermute x16, waiting for transfers between devices: 5.43 us -> 4.75 us  [send(): return lax.ppermute(value, 'blk', pairs)]
  transfers between devices with their start and end apart: 16 -> 16, of which waited for: 8 -> 7; matrix products, arithmetic and copies ran while one was open for 0% -> 0% of each run, Pallas kernels for 22% -> 22%
where the time goes in v7:
time: 32.7 us; the launch traced here: 32.5 us
  starting transfers between devices  15.4 us (47%)
  Pallas kernels  10.4 us (32%)
  waiting for transfers between devices  4.75 us (15%)
  local copies, waits for them, and re-layouts  1.54 us (5%)
    ppermute x16, starting transfers between devices, send(): return lax.ppermute(value, 'blk', pairs)  15.4 us
    ppermute x16, waiting for transfers between devices, send(): return lax.ppermute(value, 'blk', pairs)  4.75 us
    pallas_call x4, Pallas kernels, load_store(): pl.pallas_call(functools.partial(load_kernel, size, names), out_shape=jax...  4.42 us
    pallas_call x3, Pallas kernels, partial_call(): pl.pallas_call(functools.partial(partial_kernel, tuple(starts)), out_shap...  2.42 us
    pallas_call x1, Pallas kernels, score_call(): pl.pallas_call(functools.partial(score_kernel, queries, start), out_shape...  1.6 us
    unnamed x12, local copies, waits for them, and re-layouts  1.54 us
    pallas_call x1, Pallas kernels, fisher_call(): pl.pallas_call(functools.partial(fisher_kernel, size), out_shape=jax.Shap...  1.35 us
  transfers between devices with their start and end apart: 16, of which 7 were waited for; matrix products, arithmetic and copies ran while one was open for 0% of the time, Pallas kernels for 22%

profile of v7, /device:TPU:0, one launch (start us, length us, event | category | flops | bytes accessed | tf_op | source)
XLA Modules:
  0.0 32.5 jit_solution(2816305349128763827)
XLA Ops:
  0.0 0.8 %copy-done.2 = bf16[2,2,64,128]{3,2,1,0:T(8,128)(2,1)S(1)} copy-done((bf16[2,2,64,128]{3,2,1,0:T(8,128)(2,1)S(1)}, bf16[2,2,64,128]{3,2,1,0:T(8,128)(2,1)}, u32[]{:S(2)}) %copy-start.2) | copy-done | bytes 65560
  0.8 0.7 %copy-done.3 = s32[2,64]{1,0:T(2,128)S(1)} copy-done((s32[2,64]{1,0:T(2,128)S(1)}, s32[2,64]{1,0:T(2,128)}, u32[]{:S(2)}) %copy-start.3) | copy-done | bytes 536
  1.5 0.3 %shard_map.64 = bf16[64,2,128]{2,1,0:T(2,128)(2,1)S(1)} custom-call(bf16[2,2,64,128]{3,2,1,0:T(8,128)(2,1)S(1)} %copy-done.2, s32[2,64]{1,0:T(2,128)S(1)} %copy-done.3), custom_call_target="tpu_custom_call" | custom-call | flops 10000000000 | tf_op jit(solution)/shard_map/pallas_call | solution.py:79
  1.9 3.5 %collective-permute-start = (bf16[1,64,2,128]{3,2,1,0:T(2,128)(2,1)S(1)}, bf16[1,64,2,128]{3,2,1,0:T(2,128)(2,1)S(1)}, u32[]{:S(2)}, u32[]{:S(2)}) collective-permute-start(bf16[1,64,2,128]{3,2,1,0:T(2,128)(2,1)S(1)} %bitcast.5), channel_id=1, source_target_pairs={{0,9},{1,8},{2,11},{3,10},{4,13},{5,12},{6,15},{7,14},{8,1},{9,0},... | collective-permute-start | bytes 98312 | tf_op jit(solution)/shard_map/ppermute | solution.py:147
  5.4 0.3 shard_map.65.refs_8_
  5.7 1.5 %collective-permute-done = bf16[1,64,2,128]{3,2,1,0:T(2,128)(2,1)S(1)} collective-permute-done((bf16[1,64,2,128]{3,2,1,0:T(2,128)(2,1)S(1)}, bf16[1,64,2,128]{3,2,1,0:T(2,128)(2,1)S(1)}, u32[]{:S(2)}, u32[]{:S(2)}) %collective-permute-start) | collective-permute-done | bytes 32800 | tf_op jit(solution)/shard_map/ppermute | solution.py:147
  7.3 2.9 %collective-permute-start.1 = (bf16[2,64,2,128]{3,2,1,0:T(2,128)(2,1)S(1)}, bf16[2,64,2,128]{3,2,1,0:T(2,128)(2,1)S(1)}, u32[]{:S(2)}, u32[]{:S(2)}) collective-permute-start(bf16[2,64,2,128]{3,2,1,0:T(2,128)(2,1)S(1)} %pad_maximum_fusion.refs_0_), channel_id=1, source_target_pairs={{0,7},{1,6},{2,5},{3,4},{4,3},{5,2},{6,1},{7,0},{8,15},{9,14},{10,... | collective-permute-start | bytes 196616 | tf_op jit(solution)/shard_map/ppermute | solution.py:147
  10.1 0.5 %collective-permute-start.3 = (bf16[2,64,2,128]{3,2,1,0:T(2,128)(2,1)S(1)}, bf16[2,64,2,128]{3,2,1,0:T(2,128)(2,1)S(1)}, u32[]{:S(2)}, u32[]{:S(2)}) collective-permute-start(bf16[2,64,2,128]{3,2,1,0:T(2,128)(2,1)S(1)} %pad_maximum_fusion.refs_0_), channel_id=1, source_target_pairs={{0,5},{1,4},{2,7},{3,6},{4,1},{5,0},{6,3},{7,2},{8,13},{9,12},{10,... | collective-permute-start | bytes 196616 | tf_op jit(solution)/shard_map/ppermute | solution.py:147
  10.6 0.2 collective-permute-start.4
  10.8 1.1 %shard_map.66.refs_2_.refs_3_ = bf16[4,512,2,256]{3,2,1,0:T(2,128)(2,1)S(1)} custom-call(bf16[512,2,4096]{2,1,0:T(2,128)(2,1)S(1)} %copy-done), custom_call_target="tpu_custom_call" | custom-call | bytes 2097152 | tf_op jit(solution)/shard_map/pallas_call | solution.py:111
  11.9 0.7 %collective-permute-done.1.refs_2_ = bf16[2,64,2,128]{3,2,1,0:T(2,128)(2,1)S(1)} collective-permute-done((bf16[2,64,2,128]{3,2,1,0:T(2,128)(2,1)S(1)}, bf16[2,64,2,128]{3,2,1,0:T(2,128)(2,1)S(1)}, u32[]{:S(2)}, u32[]{:S(2)}) %collective-permute-start.1) | collective-permute-done | bytes 65568 | tf_op jit(solution)/shard_map/ppermute | solution.py:147
  12.6 0.5 %collective-permute-start.5 = (bf16[2,64,2,128]{3,2,1,0:T(2,128)(2,1)S(1)}, bf16[2,64,2,128]{3,2,1,0:T(2,128)(2,1)S(1)}, u32[]{:S(2)}, u32[]{:S(2)}) collective-permute-start(bf16[2,64,2,128]{3,2,1,0:T(2,128)(2,1)S(1)} %collective-permute-done.1.refs_2_), channel_id=1, source_target_pairs={{0,1},{1,0},{2,3},{3,2},{4,5},{5,4},{6,7},{7,6},{8,9},{9,8},{10,11... | collective-permute-start | bytes 196616 | tf_op jit(solution)/shard_map/ppermute | solution.py:147
  13.1 1.1 %shard_map.67.refs_1_.refs_3_ = bf16[4,512,2,256]{3,2,1,0:T(2,128)(2,1)S(1)} custom-call(bf16[512,2,4096]{2,1,0:T(2,128)(2,1)S(1)} %copy-done), custom_call_target="tpu_custom_call" | custom-call | bytes 2097152 | tf_op jit(solution)/shard_map/pallas_call | solution.py:111
  14.3 0.5 %collective-permute-done.4.refs_4_ = bf16[2,64,2,128]{3,2,1,0:T(2,128)(2,1)S(1)} collective-permute-done((bf16[2,64,2,128]{3,2,1,0:T(2,128)(2,1)S(1)}, bf16[2,64,2,128]{3,2,1,0:T(2,128)(2,1)S(1)}, u32[]{:S(2)}, u32[]{:S(2)}) %collective-permute-start.4) | collective-permute-done | bytes 65568 | tf_op jit(solution)/shard_map/ppermute | solution.py:147
  14.9 0.4 %collective-permute-start.7 = (bf16[2,64,2,128]{3,2,1,0:T(2,128)(2,1)S(1)}, bf16[2,64,2,128]{3,2,1,0:T(2,128)(2,1)S(1)}, u32[]{:S(2)}, u32[]{:S(2)}) collective-permute-start(bf16[2,64,2,128]{3,2,1,0:T(2,128)(2,1)S(1)} %collective-permute-done.4.refs_4_), channel_id=1, source_target_pairs={{0,1},{1,0},{2,3},{3,2},{4,5},{5,4},{6,7},{7,6},{8,9},{9,8},{10,11... | collective-permute-start | bytes 196616 | tf_op jit(solution)/shard_map/ppermute | solution.py:147
  15.3 0.7 %collective-permute-done.6.refs_6_ = bf16[2,64,2,128]{3,2,1,0:T(2,128)(2,1)S(1)} collective-permute-done((bf16[2,64,2,128]{3,2,1,0:T(2,128)(2,1)S(1)}, bf16[2,64,2,128]{3,2,1,0:T(2,128)(2,1)S(1)}, u32[]{:S(2)}, u32[]{:S(2)}) %collective-permute-start.6) | collective-permute-done | bytes 65568 | tf_op jit(solution)/shard_map/ppermute | solution.py:147
  16.2 1.4 %shard_map.68 = bf16[128,128]{1,0:T(8,128)(2,1)S(1)} custom-call(bf16[2,64,2,128]{3,2,1,0:T(2,128)(2,1)S(1)} %pad_maximum_fusion.refs_0_, bf16[2,64,2,128]{3,2,1,0:T(2,128)(2,1)S(1)} %collective-permute-done.2.refs_1_, bf16[2,64,2,128]{3,2,1,0:T(2,128)(2,1)S(1)} %collective-permute-done.1.refs_2_, ...), custom_call_target="tpu_custom_call" | custom-call | tf_op jit(solution)/shard_map/pallas_call | solution.py:240
  17.5 3.0 %collective-permute-start.8 = (bf16[1,128,128]{2,1,0:T(8,128)(2,1)S(1)}, bf16[1,128,128]{2,1,0:T(8,128)(2,1)S(1)}, u32[]{:S(2)}, u32[]{:S(2)}) collective-permute-start(bf16[1,128,128]{2,1,0:T(8,128)(2,1)S(1)} %bitcast.3), channel_id=1, source_target_pairs={{0,9},{1,8},{2,11},{3,10},{4,13},{5,12},{6,15},{7,14},{8,1},{9,0},... | collective-permute-start | bytes 98312 | tf_op jit(solution)/shard_map/ppermute | solution.py:147
  20.6 1.1 %shard_map.69.refs_4_.refs_5_ = bf16[4,512,2,256]{3,2,1,0:T(2,128)(2,1)S(1)} custom-call(bf16[512,2,4096]{2,1,0:T(2,128)(2,1)S(1)} %copy-done), custom_call_target="tpu_custom_call" | custom-call | bytes 2097152 | tf_op jit(solution)/shard_map/pallas_call | solution.py:111
  21.7 0.5 %collective-permute-done.8 = bf16[1,128,128]{2,1,0:T(8,128)(2,1)S(1)} collective-permute-done((bf16[1,128,128]{2,1,0:T(8,128)(2,1)S(1)}, bf16[1,128,128]{2,1,0:T(8,128)(2,1)S(1)}, u32[]{:S(2)}, u32[]{:S(2)}) %collective-permute-start.8) | collective-permute-done | bytes 32800 | tf_op jit(solution)/shard_map/ppermute | solution.py:147
  22.2 0.2 collective-permute-start.12
  22.4 2.8 %collective-permute-start.11 = (bf16[2,128,128]{2,1,0:T(8,128)(2,1)S(1)}, bf16[2,128,128]{2,1,0:T(8,128)(2,1)S(1)}, u32[]{:S(2)}, u32[]{:S(2)}) collective-permute-start(bf16[2,128,128]{2,1,0:T(8,128)(2,1)S(1)} %pad_maximum_fusion.1.refs_0_), channel_id=1, source_target_pairs={{0,7},{1,6},{2,5},{3,4},{4,3},{5,2},{6,1},{7,0},{8,15},{9,14},{10,... | collective-permute-start | bytes 196616 | tf_op jit(solution)/shard_map/ppermute | solution.py:147
  25.2 0.5 %collective-permute-start.10 = (bf16[2,128,128]{2,1,0:T(8,128)(2,1)S(1)}, bf16[2,128,128]{2,1,0:T(8,128)(2,1)S(1)}, u32[]{:S(2)}, u32[]{:S(2)}) collective-permute-start(bf16[2,128,128]{2,1,0:T(8,128)(2,1)S(1)} %pad_maximum_fusion.1.refs_0_), channel_id=1, source_target_pairs={{0,3},{1,2},{2,1},{3,0},{4,7},{5,6},{6,5},{7,4},{8,11},{9,10},{10,... | collective-permute-start | bytes 196616 | tf_op jit(solution)/shard_map/ppermute | solution.py:147
  25.7 1.1 %shard_map.71.refs_2_ = bf16[4,512,2,256]{3,2,1,0:T(2,128)(2,1)S(1)} custom-call(bf16[512,2,4096]{2,1,0:T(2,128)(2,1)S(1)} %copy-done), custom_call_target="tpu_custom_call" | custom-call | bytes 2097152 | tf_op jit(solution)/shard_map/pallas_call | solution.py:111
  26.9 0.8 %shard_map.70.refs_2_ = f32[1024,128]{1,0:T(8,128)S(1)} custom-call(bf16[2,128,128]{2,1,0:T(8,128)(2,1)S(1)} %pad_maximum_fusion.1.refs_0_, bf16[2,128,128]{2,1,0:T(8,128)(2,1)S(1)} %collective-permute-done.12.refs_1_, bf16[4,512,2,256]{3,2,1,0:T(2,128)(2,1)S(1)} %shard_map.66.refs_2_.refs_3_, bf16[4,512,2,256]{3,2,1,0:T(2,128)(2,1)S(1)} %shard_map.66.refs_2_.refs_3_), custom_call_target="tpu_custom_call" | custom-call | tf_op jit(solution)/shard_map/pallas_call | solution.py:285
  27.7 0.3 collective-permute-start.13
  28.0 0.5 %shard_map.72.refs_6_ = f32[1024,128]{1,0:T(8,128)S(1)} custom-call(bf16[2,128,128]{2,1,0:T(8,128)(2,1)S(1)} %collective-permute-done.11.refs_0_, bf16[4,512,2,256]{3,2,1,0:T(2,128)(2,1)S(1)} %shard_map.67.refs_1_.refs_3_, f32[1024,128]{1,0:T(8,128)S(1)} %shard_map.70.refs_2_), custom_call_target="tpu_custom_call" | custom-call | tf_op jit(solution)/shard_map/pallas_call | solution.py:285
  28.5 0.7 %collective-permute-done.9.refs_1_ = bf16[2,128,128]{2,1,0:T(8,128)(2,1)S(1)} collective-permute-done((bf16[2,128,128]{2,1,0:T(8,128)(2,1)S(1)}, bf16[2,128,128]{2,1,0:T(8,128)(2,1)S(1)}, u32[]{:S(2)}, u32[]{:S(2)}) %collective-permute-start.9) | collective-permute-done | bytes 65568 | tf_op jit(solution)/shard_map/ppermute | solution.py:147
  29.1 0.3 collective-permute-start.14
  29.4 0.2 collective-permute-start.15
  29.7 1.1 %shard_map.73.refs_3_ = f32[1024,128]{1,0:T(8,128)S(1)} custom-call(bf16[2,128,128]{2,1,0:T(8,128)(2,1)S(1)} %collective-permute-done.13.refs_0_, bf16[2,128,128]{2,1,0:T(8,128)(2,1)S(1)} %collective-permute-done.9.refs_1_, bf16[2,128,128]{2,1,0:T(8,128)(2,1)S(1)} %collective-permute-done.10.refs_2_, bf16[4,512,2,256]{3,2,1,0:T(2,128)(2,1)S(1)} %shard_map.67.refs_1_.refs_3_, ...), custom_call_target="tpu_custom_call" | custom-call | tf_op jit(solution)/shard_map/pallas_call | solution.py:285
  30.9 1.6 %shard_map.74 = f32[32,512]{1,0:T(8,128)} custom-call(bf16[2,128,128]{2,1,0:T(8,128)(2,1)S(1)} %collective-permute-done.14.refs_0_, bf16[2,128,128]{2,1,0:T(8,128)(2,1)S(1)} %collective-permute-done.15.refs_1_, bf16[4,512,2,256]{3,2,1,0:T(2,128)(2,1)S(1)} %shard_map.71.refs_2_, f32[1024,128]{1,0:T(8,128)S(1)} %shard_map.73.refs_3_, f32[1,512]{1,0:T(1,128)S(1)} %bitcast.7), custom_call_target="tpu_custom_call" | custom-call | tf_op jit(solution)/shard_map/pallas_call | solution.py:314
  (26 shorter events, 0.5 us)
Async XLA Ops:
  0.0 0.8 %copy-start.2 = (bf16[2,2,64,128]{3,2,1,0:T(8,128)(2,1)S(1)}, bf16[2,2,64,128]{3,2,1,0:T(8,128)(2,1)}, u32[]{:S(2)}) copy-start(bf16[2,2,64,128]{3,2,1,0:T(8,128)(2,1)} %factors_ref.1) | copy-start | bytes 196612
  0.8 0.7 %copy-start.3 = (s32[2,64]{1,0:T(2,128)S(1)}, s32[2,64]{1,0:T(2,128)}, u32[]{:S(2)}) copy-start(s32[2,64]{1,0:T(2,128)} %mask_ref.1) | copy-start | bytes 1540
  1.5 3.9 %copy-start.1 = (bf16[2,256,4096]{2,1,0:T(8,128)(2,1)S(1)}, bf16[2,256,4096]{2,1,0:T(8,128)(2,1)}, u32[]{:S(2)}) copy-start(bf16[2,256,4096]{2,1,0:T(8,128)(2,1)} %source_ref) | copy-start | bytes 12582916
  1.9 5.3 %collective-permute-start = (bf16[1,64,2,128]{3,2,1,0:T(2,128)(2,1)S(1)}, bf16[1,64,2,128]{3,2,1,0:T(2,128)(2,1)S(1)}, u32[]{:S(2)}, u32[]{:S(2)}) collective-permute-start(bf16[1,64,2,128]{3,2,1,0:T(2,128)(2,1)S(1)} %bitcast.5), channel_id=1, source_target_pairs={{0,9},{1,8},{2,11},{3,10},{4,13},{5,12},{6,15},{7,14},{8,1},{9,0},... | collective-permute-start | bytes 98312 | tf_op jit(solution)/shard_map/ppermute | solution.py:147
  5.4 5.4 %copy-start = (bf16[512,2,4096]{2,1,0:T(2,128)(2,1)S(1)}, bf16[512,2,4096]{2,1,0:T(2,128)(2,1)}, u32[]{:S(2)}) copy-start(bf16[512,2,4096]{2,1,0:T(2,128)(2,1)} %source_ref.4) | copy-start | bytes 25165828
  7.3 5.3 %collective-permute-start.1 = (bf16[2,64,2,128]{3,2,1,0:T(2,128)(2,1)S(1)}, bf16[2,64,2,128]{3,2,1,0:T(2,128)(2,1)S(1)}, u32[]{:S(2)}, u32[]{:S(2)}) collective-permute-start(bf16[2,64,2,128]{3,2,1,0:T(2,128)(2,1)S(1)} %pad_maximum_fusion.refs_0_), channel_id=1, source_target_pairs={{0,7},{1,6},{2,5},{3,4},{4,3},{5,2},{6,1},{7,0},{8,15},{9,14},{10,... | collective-permute-start | bytes 196616 | tf_op jit(solution)/shard_map/ppermute | solution.py:147
  10.1 4.1 %collective-permute-start.3 = (bf16[2,64,2,128]{3,2,1,0:T(2,128)(2,1)S(1)}, bf16[2,64,2,128]{3,2,1,0:T(2,128)(2,1)S(1)}, u32[]{:S(2)}, u32[]{:S(2)}) collective-permute-start(bf16[2,64,2,128]{3,2,1,0:T(2,128)(2,1)S(1)} %pad_maximum_fusion.refs_0_), channel_id=1, source_target_pairs={{0,5},{1,4},{2,7},{3,6},{4,1},{5,0},{6,3},{7,2},{8,13},{9,12},{10,... | collective-permute-start | bytes 196616 | tf_op jit(solution)/shard_map/ppermute | solution.py:147
  10.6 4.1 %collective-permute-start.4 = (bf16[2,64,2,128]{3,2,1,0:T(2,128)(2,1)S(1)}, bf16[2,64,2,128]{3,2,1,0:T(2,128)(2,1)S(1)}, u32[]{:S(2)}, u32[]{:S(2)}) collective-permute-start(bf16[2,64,2,128]{3,2,1,0:T(2,128)(2,1)S(1)} %pad_maximum_fusion.refs_0_), channel_id=1, source_target_pairs={{0,3},{1,2},{2,1},{3,0},{4,7},{5,6},{6,5},{7,4},{8,11},{9,10},{10,... | collective-permute-start | bytes 196616 | tf_op jit(solution)/shard_map/ppermute | solution.py:147
  12.6 2.1 %collective-permute-start.2 = (bf16[2,64,2,128]{3,2,1,0:T(2,128)(2,1)S(1)}, bf16[2,64,2,128]{3,2,1,0:T(2,128)(2,1)S(1)}, u32[]{:S(2)}, u32[]{:S(2)}) collective-permute-start(bf16[2,64,2,128]{3,2,1,0:T(2,128)(2,1)S(1)} %pad_maximum_fusion.refs_0_), channel_id=1, source_target_pairs={{0,1},{1,0},{2,3},{3,2},{4,5},{5,4},{6,7},{7,6},{8,9},{9,8},{10,11... | collective-permute-start | bytes 196616 | tf_op jit(solution)/shard_map/ppermute | solution.py:147
  12.6 2.1 %collective-permute-start.5 = (bf16[2,64,2,128]{3,2,1,0:T(2,128)(2,1)S(1)}, bf16[2,64,2,128]{3,2,1,0:T(2,128)(2,1)S(1)}, u32[]{:S(2)}, u32[]{:S(2)}) collective-permute-start(bf16[2,64,2,128]{3,2,1,0:T(2,128)(2,1)S(1)} %collective-permute-done.1.refs_2_), channel_id=1, source_target_pairs={{0,1},{1,0},{2,3},{3,2},{4,5},{5,4},{6,7},{7,6},{8,9},{9,8},{10,11... | collective-permute-start | bytes 196616 | tf_op jit(solution)/shard_map/ppermute | solution.py:147
  14.8 1.3 %collective-permute-start.6 = (bf16[2,64,2,128]{3,2,1,0:T(2,128)(2,1)S(1)}, bf16[2,64,2,128]{3,2,1,0:T(2,128)(2,1)S(1)}, u32[]{:S(2)}, u32[]{:S(2)}) collective-permute-start(bf16[2,64,2,128]{3,2,1,0:T(2,128)(2,1)S(1)} %collective-permute-done.3.refs_3_), channel_id=1, source_target_pairs={{0,1},{1,0},{2,3},{3,2},{4,5},{5,4},{6,7},{7,6},{8,9},{9,8},{10,11... | collective-permute-start | bytes 196616 | tf_op jit(solution)/shard_map/ppermute | solution.py:147
  14.9 1.3 %collective-permute-start.7 = (bf16[2,64,2,128]{3,2,1,0:T(2,128)(2,1)S(1)}, bf16[2,64,2,128]{3,2,1,0:T(2,128)(2,1)S(1)}, u32[]{:S(2)}, u32[]{:S(2)}) collective-permute-start(bf16[2,64,2,128]{3,2,1,0:T(2,128)(2,1)S(1)} %collective-permute-done.4.refs_4_), channel_id=1, source_target_pairs={{0,1},{1,0},{2,3},{3,2},{4,5},{5,4},{6,7},{7,6},{8,9},{9,8},{10,11... | collective-permute-start | bytes 196616 | tf_op jit(solution)/shard_map/ppermute | solution.py:147
  17.5 4.6 %collective-permute-start.8 = (bf16[1,128,128]{2,1,0:T(8,128)(2,1)S(1)}, bf16[1,128,128]{2,1,0:T(8,128)(2,1)S(1)}, u32[]{:S(2)}, u32[]{:S(2)}) collective-permute-start(bf16[1,128,128]{2,1,0:T(8,128)(2,1)S(1)} %bitcast.3), channel_id=1, source_target_pairs={{0,9},{1,8},{2,11},{3,10},{4,13},{5,12},{6,15},{7,14},{8,1},{9,0},... | collective-permute-start | bytes 98312 | tf_op jit(solution)/shard_map/ppermute | solution.py:147
  22.2 3.6 %collective-permute-start.12 = (bf16[2,128,128]{2,1,0:T(8,128)(2,1)S(1)}, bf16[2,128,128]{2,1,0:T(8,128)(2,1)S(1)}, u32[]{:S(2)}, u32[]{:S(2)}) collective-permute-start(bf16[2,128,128]{2,1,0:T(8,128)(2,1)S(1)} %pad_maximum_fusion.1.refs_0_), channel_id=1, source_target_pairs={{0,1},{1,0},{2,3},{3,2},{4,5},{5,4},{6,7},{7,6},{8,9},{9,8},{10,11... | collective-permute-start | bytes 196616 | tf_op jit(solution)/shard_map/ppermute | solution.py:147
  22.4 5.3 %collective-permute-start.11 = (bf16[2,128,128]{2,1,0:T(8,128)(2,1)S(1)}, bf16[2,128,128]{2,1,0:T(8,128)(2,1)S(1)}, u32[]{:S(2)}, u32[]{:S(2)}) collective-permute-start(bf16[2,128,128]{2,1,0:T(8,128)(2,1)S(1)} %pad_maximum_fusion.1.refs_0_), channel_id=1, source_target_pairs={{0,7},{1,6},{2,5},{3,4},{4,3},{5,2},{6,1},{7,0},{8,15},{9,14},{10,... | collective-permute-start | bytes 196616 | tf_op jit(solution)/shard_map/ppermute | solution.py:147
  25.2 3.9 %collective-permute-start.9 = (bf16[2,128,128]{2,1,0:T(8,128)(2,1)S(1)}, bf16[2,128,128]{2,1,0:T(8,128)(2,1)S(1)}, u32[]{:S(2)}, u32[]{:S(2)}) collective-permute-start(bf16[2,128,128]{2,1,0:T(8,128)(2,1)S(1)} %pad_maximum_fusion.1.refs_0_), channel_id=1, source_target_pairs={{0,5},{1,4},{2,7},{3,6},{4,1},{5,0},{6,3},{7,2},{8,13},{9,12},{10,... | collective-permute-start | bytes 196616 | tf_op jit(solution)/shard_map/ppermute | solution.py:147
  25.2 3.9 %collective-permute-start.10 = (bf16[2,128,128]{2,1,0:T(8,128)(2,1)S(1)}, bf16[2,128,128]{2,1,0:T(8,128)(2,1)S(1)}, u32[]{:S(2)}, u32[]{:S(2)}) collective-permute-start(bf16[2,128,128]{2,1,0:T(8,128)(2,1)S(1)} %pad_maximum_fusion.1.refs_0_), channel_id=1, source_target_pairs={{0,3},{1,2},{2,1},{3,0},{4,7},{5,6},{6,5},{7,4},{8,11},{9,10},{10,... | collective-permute-start | bytes 196616 | tf_op jit(solution)/shard_map/ppermute | solution.py:147
  27.7 2.0 %copy-start.4 = (s32[512]{0:T(512)S(1)}, s32[512]{0:T(512)}, u32[]{:S(2)}) copy-start(s32[512]{0:T(512)} %param.10) | copy-start | bytes 6148
  27.7 2.0 %copy-start.5 = (f32[16]{0:T(128)S(1)}, f32[16]{0:T(128)}, u32[]{:S(2)}) copy-start(f32[16]{0:T(128)} %param.11) | copy-start | bytes 196
  27.7 1.4 %collective-permute-start.13 = (bf16[2,128,128]{2,1,0:T(8,128)(2,1)S(1)}, bf16[2,128,128]{2,1,0:T(8,128)(2,1)S(1)}, u32[]{:S(2)}, u32[]{:S(2)}) collective-permute-start(bf16[2,128,128]{2,1,0:T(8,128)(2,1)S(1)} %collective-permute-done.11.refs_0_), channel_id=1, source_target_pairs={{0,1},{1,0},{2,3},{3,2},{4,5},{5,4},{6,7},{7,6},{8,9},{9,8},{10,11... | collective-permute-start | bytes 196616 | tf_op jit(solution)/shard_map/ppermute | solution.py:147
  29.1 1.7 %collective-permute-start.14 = (bf16[2,128,128]{2,1,0:T(8,128)(2,1)S(1)}, bf16[2,128,128]{2,1,0:T(8,128)(2,1)S(1)}, u32[]{:S(2)}, u32[]{:S(2)}) collective-permute-start(bf16[2,128,128]{2,1,0:T(8,128)(2,1)S(1)} %collective-permute-done.9.refs_1_), channel_id=1, source_target_pairs={{0,1},{1,0},{2,3},{3,2},{4,5},{5,4},{6,7},{7,6},{8,9},{9,8},{10,11... | collective-permute-start | bytes 196616 | tf_op jit(solution)/shard_map/ppermute | solution.py:147
  29.4 1.4 %collective-permute-start.15 = (bf16[2,128,128]{2,1,0:T(8,128)(2,1)S(1)}, bf16[2,128,128]{2,1,0:T(8,128)(2,1)S(1)}, u32[]{:S(2)}, u32[]{:S(2)}) collective-permute-start(bf16[2,128,128]{2,1,0:T(8,128)(2,1)S(1)} %collective-permute-done.10.refs_2_), channel_id=1, source_target_pairs={{0,1},{1,0},{2,3},{3,2},{4,5},{5,4},{6,7},{7,6},{8,9},{9,8},{10,11... | collective-permute-start | bytes 196616 | tf_op jit(solution)/shard_map/ppermute | solution.py:147

commit v8 on v7

--- a/solution.py
+++ b/solution.py
@@ -51,7 +51,21 @@
     return raw_scores * make_scaling(source_ids, source_weight)[None, :]
 
 
-def grads_kernel(factors_ref, mask_ref, out_ref, outer_ref, flat_ref):
+def zeros_kernel(out_ref):
+    out_ref[...] = jnp.zeros_like(out_ref)
+
+
+def zeros_call(shape):
+    return pl.pallas_call(
+        zeros_kernel,
+        out_shape=jax.ShapeDtypeStruct(shape, jnp.float32),
+        out_specs=IN_VMEM,
+        cost_estimate=pl.CostEstimate(flops=10**10, bytes_accessed=0, transcendentals=0),
+        compiler_params=PARAMS,
+    )()
+
+
+def grads_kernel(factors_ref, mask_ref, zeros_ref, out_ref, outer_ref, flat_ref):
     queries, layers, _, width = factors_ref.shape
     rank = width // 2
     tiles = rank * rank // LANES
@@ -59,7 +73,7 @@
         for query in range(queries):
             block = factors_ref[query, layer].astype(jnp.float32)
             left = block[:, :rank].T * mask_ref[query : query + 1].astype(jnp.float32)
-            outer_ref[...] = jnp.dot(
+            outer_ref[...] = zeros_ref[...] + jnp.dot(
                 left.astype(jnp.bfloat16),
                 block[:, rank:].astype(jnp.bfloat16),
                 preferred_element_type=jnp.float32,
@@ -83,6 +97,7 @@
         in_specs=[
             pl.BlockSpec(factors.shape, lambda i: (0, 0, 0, 0)),
             pl.BlockSpec(token_mask.shape, lambda i: (0, 0)),
+            IN_VMEM,
         ],
         out_specs=pl.BlockSpec((layers * tiles, queries, LANES), lambda i: (0, 0, 0)),
         scratch_shapes=[
@@ -91,7 +106,7 @@
         ],
         cost_estimate=pl.CostEstimate(flops=10**10, bytes_accessed=0, transcendentals=0),
         compiler_params=PARAMS,
-    )(factors, token_mask)
+    )(factors, token_mask, zeros_call((rank, rank)))
 
 
 def load_kernel(size, names, source_ref, out_ref, sem):

time: 32.7 us -> 32 us (0.979)
  local copies, waits for them, and re-layouts: 1.54 us -> 0.86 us
    unnamed x12 -> x14, local copies, waits for them, and re-layouts: 1.54 us -> 0.86 us
where the time goes in v8:
time: 32 us; the launch traced here: 31.9 us
  starting transfers between devices  15.4 us (48%)
  Pallas kernels  10.5 us (33%)
  waiting for transfers between devices  4.78 us (15%)
  local copies, waits for them, and re-layouts  0.86 us (3%)
    ppermute x16, starting transfers between devices, send(): return lax.ppermute(value, 'blk', pairs)  15.4 us
    ppermute x16, waiting for transfers between devices, send(): return lax.ppermute(value, 'blk', pairs)  4.78 us
    pallas_call x4, Pallas kernels, load_store(): pl.pallas_call(functools.partial(load_kernel, size, names), out_shape=jax...  4.42 us
    pallas_call x3, Pallas kernels, partial_call(): pl.pallas_call(functools.partial(partial_kernel, tuple(starts)), out_shap...  2.43 us
    pallas_call x1, Pallas kernels, score_call(): pl.pallas_call(functools.partial(score_kernel, queries, start), out_shape...  1.61 us
    pallas_call x1, Pallas kernels, fisher_call(): pl.pallas_call(functools.partial(fisher_kernel, size), out_shape=jax.Shap...  1.35 us
    unnamed x14, local copies, waits for them, and re-layouts  0.86 us
  transfers between devices with their start and end apart: 16, of which 7 were waited for; matrix products, arithmetic and copies ran while one was open for 0% of the time, Pallas kernels for 22%

profile of v8, /device:TPU:0, one launch (start us, length us, event | category | flops | bytes accessed | tf_op | source)
XLA Modules:
  0.0 31.9 jit_solution(17871669550944635646)
XLA Ops:
  0.0 0.8 %copy-done.1 = bf16[2,2,64,128]{3,2,1,0:T(8,128)(2,1)S(1)} copy-done((bf16[2,2,64,128]{3,2,1,0:T(8,128)(2,1)S(1)}, bf16[2,2,64,128]{3,2,1,0:T(8,128)(2,1)}, u32[]{:S(2)}) %copy-start.1) | copy-done | bytes 65560
  0.8 0.3 %shard_map.65 = bf16[64,2,128]{2,1,0:T(2,128)(2,1)S(1)} custom-call(bf16[2,2,64,128]{3,2,1,0:T(8,128)(2,1)S(1)} %copy-done.1, s32[2,64]{1,0:T(2,128)S(1)} %copy-done.2, f32[64,64]{1,0:T(8,128)S(1)} %shard_map.64.zeros_ref), custom_call_target="tpu_custom_call" | custom-call | flops 10000000000 | tf_op jit(solution)/shard_map/pallas_call | solution.py:93
  1.2 3.5 %collective-permute-start = (bf16[1,64,2,128]{3,2,1,0:T(2,128)(2,1)S(1)}, bf16[1,64,2,128]{3,2,1,0:T(2,128)(2,1)S(1)}, u32[]{:S(2)}, u32[]{:S(2)}) collective-permute-start(bf16[1,64,2,128]{3,2,1,0:T(2,128)(2,1)S(1)} %bitcast.7), channel_id=1, source_target_pairs={{0,9},{1,8},{2,11},{3,10},{4,13},{5,12},{6,15},{7,14},{8,1},{9,0},... | collective-permute-start | bytes 98312 | tf_op jit(solution)/shard_map/ppermute | solution.py:162
  4.7 0.3 shard_map.66.refs_8_
  5.0 1.5 %collective-permute-done = bf16[1,64,2,128]{3,2,1,0:T(2,128)(2,1)S(1)} collective-permute-done((bf16[1,64,2,128]{3,2,1,0:T(2,128)(2,1)S(1)}, bf16[1,64,2,128]{3,2,1,0:T(2,128)(2,1)S(1)}, u32[]{:S(2)}, u32[]{:S(2)}) %collective-permute-start) | collective-permute-done | bytes 32800 | tf_op jit(solution)/shard_map/ppermute | solution.py:162
  6.6 2.9 %collective-permute-start.1 = (bf16[2,64,2,128]{3,2,1,0:T(2,128)(2,1)S(1)}, bf16[2,64,2,128]{3,2,1,0:T(2,128)(2,1)S(1)}, u32[]{:S(2)}, u32[]{:S(2)}) collective-permute-start(bf16[2,64,2,128]{3,2,1,0:T(2,128)(2,1)S(1)} %pad_maximum_fusion.refs_0_), channel_id=1, source_target_pairs={{0,7},{1,6},{2,5},{3,4},{4,3},{5,2},{6,1},{7,0},{8,15},{9,14},{10,... | collective-permute-start | bytes 196616 | tf_op jit(solution)/shard_map/ppermute | solution.py:162
  9.5 0.5 %collective-permute-start.3 = (bf16[2,64,2,128]{3,2,1,0:T(2,128)(2,1)S(1)}, bf16[2,64,2,128]{3,2,1,0:T(2,128)(2,1)S(1)}, u32[]{:S(2)}, u32[]{:S(2)}) collective-permute-start(bf16[2,64,2,128]{3,2,1,0:T(2,128)(2,1)S(1)} %pad_maximum_fusion.refs_0_), channel_id=1, source_target_pairs={{0,5},{1,4},{2,7},{3,6},{4,1},{5,0},{6,3},{7,2},{8,13},{9,12},{10,... | collective-permute-start | bytes 196616 | tf_op jit(solution)/shard_map/ppermute | solution.py:162
  10.0 0.2 collective-permute-start.4
  10.2 1.1 %shard_map.67.refs_2_.refs_3_ = bf16[4,512,2,256]{3,2,1,0:T(2,128)(2,1)S(1)} custom-call(bf16[512,2,4096]{2,1,0:T(2,128)(2,1)S(1)} %bitcast.4), custom_call_target="tpu_custom_call" | custom-call | bytes 2097152 | tf_op jit(solution)/shard_map/pallas_call | solution.py:126
  11.3 0.7 %collective-permute-done.1.refs_2_ = bf16[2,64,2,128]{3,2,1,0:T(2,128)(2,1)S(1)} collective-permute-done((bf16[2,64,2,128]{3,2,1,0:T(2,128)(2,1)S(1)}, bf16[2,64,2,128]{3,2,1,0:T(2,128)(2,1)S(1)}, u32[]{:S(2)}, u32[]{:S(2)}) %collective-permute-start.1) | collective-permute-done | bytes 65568 | tf_op jit(solution)/shard_map/ppermute | solution.py:162
  12.0 0.5 %collective-permute-start.5 = (bf16[2,64,2,128]{3,2,1,0:T(2,128)(2,1)S(1)}, bf16[2,64,2,128]{3,2,1,0:T(2,128)(2,1)S(1)}, u32[]{:S(2)}, u32[]{:S(2)}) collective-permute-start(bf16[2,64,2,128]{3,2,1,0:T(2,128)(2,1)S(1)} %collective-permute-done.1.refs_2_), channel_id=1, source_target_pairs={{0,1},{1,0},{2,3},{3,2},{4,5},{5,4},{6,7},{7,6},{8,9},{9,8},{10,11... | collective-permute-start | bytes 196616 | tf_op jit(solution)/shard_map/ppermute | solution.py:162
  12.5 1.1 %shard_map.68.refs_1_.refs_3_ = bf16[4,512,2,256]{3,2,1,0:T(2,128)(2,1)S(1)} custom-call(bf16[512,2,4096]{2,1,0:T(2,128)(2,1)S(1)} %bitcast.4), custom_call_target="tpu_custom_call" | custom-call | bytes 2097152 | tf_op jit(solution)/shard_map/pallas_call | solution.py:126
  13.6 0.5 %collective-permute-done.4.refs_4_ = bf16[2,64,2,128]{3,2,1,0:T(2,128)(2,1)S(1)} collective-permute-done((bf16[2,64,2,128]{3,2,1,0:T(2,128)(2,1)S(1)}, bf16[2,64,2,128]{3,2,1,0:T(2,128)(2,1)S(1)}, u32[]{:S(2)}, u32[]{:S(2)}) %collective-permute-start.4) | collective-permute-done | bytes 65568 | tf_op jit(solution)/shard_map/ppermute | solution.py:162
  14.2 0.4 %collective-permute-start.7 = (bf16[2,64,2,128]{3,2,1,0:T(2,128)(2,1)S(1)}, bf16[2,64,2,128]{3,2,1,0:T(2,128)(2,1)S(1)}, u32[]{:S(2)}, u32[]{:S(2)}) collective-permute-start(bf16[2,64,2,128]{3,2,1,0:T(2,128)(2,1)S(1)} %collective-permute-done.4.refs_4_), channel_id=1, source_target_pairs={{0,1},{1,0},{2,3},{3,2},{4,5},{5,4},{6,7},{7,6},{8,9},{9,8},{10,11... | collective-permute-start | bytes 196616 | tf_op jit(solution)/shard_map/ppermute | solution.py:162
  14.6 0.7 %collective-permute-done.6.refs_6_ = bf16[2,64,2,128]{3,2,1,0:T(2,128)(2,1)S(1)} collective-permute-done((bf16[2,64,2,128]{3,2,1,0:T(2,128)(2,1)S(1)}, bf16[2,64,2,128]{3,2,1,0:T(2,128)(2,1)S(1)}, u32[]{:S(2)}, u32[]{:S(2)}) %collective-permute-start.6) | collective-permute-done | bytes 65568 | tf_op jit(solution)/shard_map/ppermute | solution.py:162
  15.3 0.2 collective-permute-done.7.refs_7_
  15.5 1.4 %shard_map.69 = bf16[128,128]{1,0:T(8,128)(2,1)S(1)} custom-call(bf16[2,64,2,128]{3,2,1,0:T(2,128)(2,1)S(1)} %pad_maximum_fusion.refs_0_, bf16[2,64,2,128]{3,2,1,0:T(2,128)(2,1)S(1)} %collective-permute-done.2.refs_1_, bf16[2,64,2,128]{3,2,1,0:T(2,128)(2,1)S(1)} %collective-permute-done.1.refs_2_, ...), custom_call_target="tpu_custom_call" | custom-call | tf_op jit(solution)/shard_map/pallas_call | solution.py:255
  16.9 3.0 %collective-permute-start.8 = (bf16[1,128,128]{2,1,0:T(8,128)(2,1)S(1)}, bf16[1,128,128]{2,1,0:T(8,128)(2,1)S(1)}, u32[]{:S(2)}, u32[]{:S(2)}) collective-permute-start(bf16[1,128,128]{2,1,0:T(8,128)(2,1)S(1)} %bitcast.5), channel_id=1, source_target_pairs={{0,9},{1,8},{2,11},{3,10},{4,13},{5,12},{6,15},{7,14},{8,1},{9,0},... | collective-permute-start | bytes 98312 | tf_op jit(solution)/shard_map/ppermute | solution.py:162
  19.9 1.1 %shard_map.70.refs_4_.refs_5_ = bf16[4,512,2,256]{3,2,1,0:T(2,128)(2,1)S(1)} custom-call(bf16[512,2,4096]{2,1,0:T(2,128)(2,1)S(1)} %bitcast.4), custom_call_target="tpu_custom_call" | custom-call | bytes 2097152 | tf_op jit(solution)/shard_map/pallas_call | solution.py:126
  21.0 0.5 %collective-permute-done.8 = bf16[1,128,128]{2,1,0:T(8,128)(2,1)S(1)} collective-permute-done((bf16[1,128,128]{2,1,0:T(8,128)(2,1)S(1)}, bf16[1,128,128]{2,1,0:T(8,128)(2,1)S(1)}, u32[]{:S(2)}, u32[]{:S(2)}) %collective-permute-start.8) | collective-permute-done | bytes 32800 | tf_op jit(solution)/shard_map/ppermute | solution.py:162
  21.5 0.2 collective-permute-start.12
  21.7 2.8 %collective-permute-start.11 = (bf16[2,128,128]{2,1,0:T(8,128)(2,1)S(1)}, bf16[2,128,128]{2,1,0:T(8,128)(2,1)S(1)}, u32[]{:S(2)}, u32[]{:S(2)}) collective-permute-start(bf16[2,128,128]{2,1,0:T(8,128)(2,1)S(1)} %pad_maximum_fusion.1.refs_0_), channel_id=1, source_target_pairs={{0,7},{1,6},{2,5},{3,4},{4,3},{5,2},{6,1},{7,0},{8,15},{9,14},{10,... | collective-permute-start | bytes 196616 | tf_op jit(solution)/shard_map/ppermute | solution.py:162
  24.5 0.5 %collective-permute-start.10 = (bf16[2,128,128]{2,1,0:T(8,128)(2,1)S(1)}, bf16[2,128,128]{2,1,0:T(8,128)(2,1)S(1)}, u32[]{:S(2)}, u32[]{:S(2)}) collective-permute-start(bf16[2,128,128]{2,1,0:T(8,128)(2,1)S(1)} %pad_maximum_fusion.1.refs_0_), channel_id=1, source_target_pairs={{0,3},{1,2},{2,1},{3,0},{4,7},{5,6},{6,5},{7,4},{8,11},{9,10},{10,... | collective-permute-start | bytes 196616 | tf_op jit(solution)/shard_map/ppermute | solution.py:162
  25.1 1.1 %shard_map.72.refs_2_ = bf16[4,512,2,256]{3,2,1,0:T(2,128)(2,1)S(1)} custom-call(bf16[512,2,4096]{2,1,0:T(2,128)(2,1)S(1)} %bitcast.4), custom_call_target="tpu_custom_call" | custom-call | bytes 2097152 | tf_op jit(solution)/shard_map/pallas_call | solution.py:126
  26.2 0.8 %shard_map.71.refs_2_ = f32[1024,128]{1,0:T(8,128)S(1)} custom-call(bf16[2,128,128]{2,1,0:T(8,128)(2,1)S(1)} %pad_maximum_fusion.1.refs_0_, bf16[2,128,128]{2,1,0:T(8,128)(2,1)S(1)} %collective-permute-done.12.refs_1_, bf16[4,512,2,256]{3,2,1,0:T(2,128)(2,1)S(1)} %shard_map.67.refs_2_.refs_3_, bf16[4,512,2,256]{3,2,1,0:T(2,128)(2,1)S(1)} %shard_map.67.refs_2_.refs_3_), custom_call_target="tpu_custom_call" | custom-call | tf_op jit(solution)/shard_map/pallas_call | solution.py:300
  27.0 0.3 collective-permute-start.13
  27.3 0.5 %shard_map.73.refs_6_ = f32[1024,128]{1,0:T(8,128)S(1)} custom-call(bf16[2,128,128]{2,1,0:T(8,128)(2,1)S(1)} %collective-permute-done.11.refs_0_, bf16[4,512,2,256]{3,2,1,0:T(2,128)(2,1)S(1)} %shard_map.68.refs_1_.refs_3_, f32[1024,128]{1,0:T(8,128)S(1)} %shard_map.71.refs_2_), custom_call_target="tpu_custom_call" | custom-call | tf_op jit(solution)/shard_map/pallas_call | solution.py:300
  27.8 0.7 %collective-permute-done.9.refs_1_ = bf16[2,128,128]{2,1,0:T(8,128)(2,1)S(1)} collective-permute-done((bf16[2,128,128]{2,1,0:T(8,128)(2,1)S(1)}, bf16[2,128,128]{2,1,0:T(8,128)(2,1)S(1)}, u32[]{:S(2)}, u32[]{:S(2)}) %collective-permute-start.9) | collective-permute-done | bytes 65568 | tf_op jit(solution)/shard_map/ppermute | solution.py:162
  28.5 0.3 collective-permute-start.14
  28.8 0.2 collective-permute-start.15
  29.1 1.1 %shard_map.74.refs_3_ = f32[1024,128]{1,0:T(8,128)S(1)} custom-call(bf16[2,128,128]{2,1,0:T(8,128)(2,1)S(1)} %collective-permute-done.13.refs_0_, bf16[2,128,128]{2,1,0:T(8,128)(2,1)S(1)} %collective-permute-done.9.refs_1_, bf16[2,128,128]{2,1,0:T(8,128)(2,1)S(1)} %collective-permute-done.10.refs_2_, bf16[4,512,2,256]{3,2,1,0:T(2,128)(2,1)S(1)} %shard_map.68.refs_1_.refs_3_, ...), custom_call_target="tpu_custom_call" | custom-call | tf_op jit(solution)/shard_map/pallas_call | solution.py:300
  30.2 1.6 %shard_map.75 = f32[32,512]{1,0:T(8,128)} custom-call(bf16[2,128,128]{2,1,0:T(8,128)(2,1)S(1)} %collective-permute-done.14.refs_0_, bf16[2,128,128]{2,1,0:T(8,128)(2,1)S(1)} %collective-permute-done.15.refs_1_, bf16[4,512,2,256]{3,2,1,0:T(2,128)(2,1)S(1)} %shard_map.72.refs_2_, f32[1024,128]{1,0:T(8,128)S(1)} %shard_map.74.refs_3_, f32[1,512]{1,0:T(1,128)S(1)} %bitcast.9), custom_call_target="tpu_custom_call" | custom-call | tf_op jit(solution)/shard_map/pallas_call | solution.py:329
  (30 shorter events, 0.4 us)
Async XLA Ops:
  0.0 0.8 %copy-start.1 = (bf16[2,2,64,128]{3,2,1,0:T(8,128)(2,1)S(1)}, bf16[2,2,64,128]{3,2,1,0:T(8,128)(2,1)}, u32[]{:S(2)}) copy-start(bf16[2,2,64,128]{3,2,1,0:T(8,128)(2,1)} %factors_ref.1) | copy-start | bytes 196612
  0.0 0.8 %copy-start.2 = (s32[2,64]{1,0:T(2,128)S(1)}, s32[2,64]{1,0:T(2,128)}, u32[]{:S(2)}) copy-start(s32[2,64]{1,0:T(2,128)} %mask_ref.1) | copy-start | bytes 1540
  0.0 10.1 %slice-start = ((s8[8388608]{0:T(1024)(128)(4,1)}), s8[4194304]{0:T(1024)(128)(4,1)S(1)}, s32[]{:S(2)}) async-start(s8[8388608]{0:T(1024)(128)(4,1)} %bitcast.3), calls=%async_computation | async-start | bytes 8388608
  0.8 3.9 %copy-start = (bf16[2,256,4096]{2,1,0:T(8,128)(2,1)S(1)}, bf16[2,256,4096]{2,1,0:T(8,128)(2,1)}, u32[]{:S(2)}) copy-start(bf16[2,256,4096]{2,1,0:T(8,128)(2,1)} %source_ref) | copy-start | bytes 12582916
  0.8 9.3 %slice-start.1 = ((s8[8388608]{0:T(1024)(128)(4,1)}), s8[4194304]{0:T(1024)(128)(4,1)S(1)}, s32[]{:S(2)}) async-start(s8[8388608]{0:T(1024)(128)(4,1)} %bitcast.3), calls=%async_computation.1 | async-start | bytes 8388608
  1.2 5.3 %collective-permute-start = (bf16[1,64,2,128]{3,2,1,0:T(2,128)(2,1)S(1)}, bf16[1,64,2,128]{3,2,1,0:T(2,128)(2,1)S(1)}, u32[]{:S(2)}, u32[]{:S(2)}) collective-permute-start(bf16[1,64,2,128]{3,2,1,0:T(2,128)(2,1)S(1)} %bitcast.7), channel_id=1, source_target_pairs={{0,9},{1,8},{2,11},{3,10},{4,13},{5,12},{6,15},{7,14},{8,1},{9,0},... | collective-permute-start | bytes 98312 | tf_op jit(solution)/shard_map/ppermute | solution.py:162
  6.6 5.3 %collective-permute-start.1 = (bf16[2,64,2,128]{3,2,1,0:T(2,128)(2,1)S(1)}, bf16[2,64,2,128]{3,2,1,0:T(2,128)(2,1)S(1)}, u32[]{:S(2)}, u32[]{:S(2)}) collective-permute-start(bf16[2,64,2,128]{3,2,1,0:T(2,128)(2,1)S(1)} %pad_maximum_fusion.refs_0_), channel_id=1, source_target_pairs={{0,7},{1,6},{2,5},{3,4},{4,3},{5,2},{6,1},{7,0},{8,15},{9,14},{10,... | collective-permute-start | bytes 196616 | tf_op jit(solution)/shard_map/ppermute | solution.py:162
  9.5 4.1 %collective-permute-start.3 = (bf16[2,64,2,128]{3,2,1,0:T(2,128)(2,1)S(1)}, bf16[2,64,2,128]{3,2,1,0:T(2,128)(2,1)S(1)}, u32[]{:S(2)}, u32[]{:S(2)}) collective-permute-start(bf16[2,64,2,128]{3,2,1,0:T(2,128)(2,1)S(1)} %pad_maximum_fusion.refs_0_), channel_id=1, source_target_pairs={{0,5},{1,4},{2,7},{3,6},{4,1},{5,0},{6,3},{7,2},{8,13},{9,12},{10,... | collective-permute-start | bytes 196616 | tf_op jit(solution)/shard_map/ppermute | solution.py:162
  10.0 4.1 %collective-permute-start.4 = (bf16[2,64,2,128]{3,2,1,0:T(2,128)(2,1)S(1)}, bf16[2,64,2,128]{3,2,1,0:T(2,128)(2,1)S(1)}, u32[]{:S(2)}, u32[]{:S(2)}) collective-permute-start(bf16[2,64,2,128]{3,2,1,0:T(2,128)(2,1)S(1)} %pad_maximum_fusion.refs_0_), channel_id=1, source_target_pairs={{0,3},{1,2},{2,1},{3,0},{4,7},{5,6},{6,5},{7,4},{8,11},{9,10},{10,... | collective-permute-start | bytes 196616 | tf_op jit(solution)/shard_map/ppermute | solution.py:162
  12.0 2.1 %collective-permute-start.2 = (bf16[2,64,2,128]{3,2,1,0:T(2,128)(2,1)S(1)}, bf16[2,64,2,128]{3,2,1,0:T(2,128)(2,1)S(1)}, u32[]{:S(2)}, u32[]{:S(2)}) collective-permute-start(bf16[2,64,2,128]{3,2,1,0:T(2,128)(2,1)S(1)} %pad_maximum_fusion.refs_0_), channel_id=1, source_target_pairs={{0,1},{1,0},{2,3},{3,2},{4,5},{5,4},{6,7},{7,6},{8,9},{9,8},{10,11... | collective-permute-start | bytes 196616 | tf_op jit(solution)/shard_map/ppermute | solution.py:162
  12.0 2.1 %collective-permute-start.5 = (bf16[2,64,2,128]{3,2,1,0:T(2,128)(2,1)S(1)}, bf16[2,64,2,128]{3,2,1,0:T(2,128)(2,1)S(1)}, u32[]{:S(2)}, u32[]{:S(2)}) collective-permute-start(bf16[2,64,2,128]{3,2,1,0:T(2,128)(2,1)S(1)} %collective-permute-done.1.refs_2_), channel_id=1, source_target_pairs={{0,1},{1,0},{2,3},{3,2},{4,5},{5,4},{6,7},{7,6},{8,9},{9,8},{10,11... | collective-permute-start | bytes 196616 | tf_op jit(solution)/shard_map/ppermute | solution.py:162
  14.1 1.3 %collective-permute-start.6 = (bf16[2,64,2,128]{3,2,1,0:T(2,128)(2,1)S(1)}, bf16[2,64,2,128]{3,2,1,0:T(2,128)(2,1)S(1)}, u32[]{:S(2)}, u32[]{:S(2)}) collective-permute-start(bf16[2,64,2,128]{3,2,1,0:T(2,128)(2,1)S(1)} %collective-permute-done.3.refs_3_), channel_id=1, source_target_pairs={{0,1},{1,0},{2,3},{3,2},{4,5},{5,4},{6,7},{7,6},{8,9},{9,8},{10,11... | collective-permute-start | bytes 196616 | tf_op jit(solution)/shard_map/ppermute | solution.py:162
  14.2 1.3 %collective-permute-start.7 = (bf16[2,64,2,128]{3,2,1,0:T(2,128)(2,1)S(1)}, bf16[2,64,2,128]{3,2,1,0:T(2,128)(2,1)S(1)}, u32[]{:S(2)}, u32[]{:S(2)}) collective-permute-start(bf16[2,64,2,128]{3,2,1,0:T(2,128)(2,1)S(1)} %collective-permute-done.4.refs_4_), channel_id=1, source_target_pairs={{0,1},{1,0},{2,3},{3,2},{4,5},{5,4},{6,7},{7,6},{8,9},{9,8},{10,11... | collective-permute-start | bytes 196616 | tf_op jit(solution)/shard_map/ppermute | solution.py:162
  16.9 4.6 %collective-permute-start.8 = (bf16[1,128,128]{2,1,0:T(8,128)(2,1)S(1)}, bf16[1,128,128]{2,1,0:T(8,128)(2,1)S(1)}, u32[]{:S(2)}, u32[]{:S(2)}) collective-permute-start(bf16[1,128,128]{2,1,0:T(8,128)(2,1)S(1)} %bitcast.5), channel_id=1, source_target_pairs={{0,9},{1,8},{2,11},{3,10},{4,13},{5,12},{6,15},{7,14},{8,1},{9,0},... | collective-permute-start | bytes 98312 | tf_op jit(solution)/shard_map/ppermute | solution.py:162
  21.5 3.5 %collective-permute-start.12 = (bf16[2,128,128]{2,1,0:T(8,128)(2,1)S(1)}, bf16[2,128,128]{2,1,0:T(8,128)(2,1)S(1)}, u32[]{:S(2)}, u32[]{:S(2)}) collective-permute-start(bf16[2,128,128]{2,1,0:T(8,128)(2,1)S(1)} %pad_maximum_fusion.1.refs_0_), channel_id=1, source_target_pairs={{0,1},{1,0},{2,3},{3,2},{4,5},{5,4},{6,7},{7,6},{8,9},{9,8},{10,11... | collective-permute-start | bytes 196616 | tf_op jit(solution)/shard_map/ppermute | solution.py:162
  21.7 5.3 %collective-permute-start.11 = (bf16[2,128,128]{2,1,0:T(8,128)(2,1)S(1)}, bf16[2,128,128]{2,1,0:T(8,128)(2,1)S(1)}, u32[]{:S(2)}, u32[]{:S(2)}) collective-permute-start(bf16[2,128,128]{2,1,0:T(8,128)(2,1)S(1)} %pad_maximum_fusion.1.refs_0_), channel_id=1, source_target_pairs={{0,7},{1,6},{2,5},{3,4},{4,3},{5,2},{6,1},{7,0},{8,15},{9,14},{10,... | collective-permute-start | bytes 196616 | tf_op jit(solution)/shard_map/ppermute | solution.py:162
  24.5 4.0 %collective-permute-start.9 = (bf16[2,128,128]{2,1,0:T(8,128)(2,1)S(1)}, bf16[2,128,128]{2,1,0:T(8,128)(2,1)S(1)}, u32[]{:S(2)}, u32[]{:S(2)}) collective-permute-start(bf16[2,128,128]{2,1,0:T(8,128)(2,1)S(1)} %pad_maximum_fusion.1.refs_0_), channel_id=1, source_target_pairs={{0,5},{1,4},{2,7},{3,6},{4,1},{5,0},{6,3},{7,2},{8,13},{9,12},{10,... | collective-permute-start | bytes 196616 | tf_op jit(solution)/shard_map/ppermute | solution.py:162
  24.5 4.0 %collective-permute-start.10 = (bf16[2,128,128]{2,1,0:T(8,128)(2,1)S(1)}, bf16[2,128,128]{2,1,0:T(8,128)(2,1)S(1)}, u32[]{:S(2)}, u32[]{:S(2)}) collective-permute-start(bf16[2,128,128]{2,1,0:T(8,128)(2,1)S(1)} %pad_maximum_fusion.1.refs_0_), channel_id=1, source_target_pairs={{0,3},{1,2},{2,1},{3,0},{4,7},{5,6},{6,5},{7,4},{8,11},{9,10},{10,... | collective-permute-start | bytes 196616 | tf_op jit(solution)/shard_map/ppermute | solution.py:162
  27.0 2.0 %copy-start.3 = (s32[512]{0:T(512)S(1)}, s32[512]{0:T(512)}, u32[]{:S(2)}) copy-start(s32[512]{0:T(512)} %param.10) | copy-start | bytes 6148
  27.0 2.0 %copy-start.4 = (f32[16]{0:T(128)S(1)}, f32[16]{0:T(128)}, u32[]{:S(2)}) copy-start(f32[16]{0:T(128)} %param.11) | copy-start | bytes 196
  27.0 1.5 %collective-permute-start.13 = (bf16[2,128,128]{2,1,0:T(8,128)(2,1)S(1)}, bf16[2,128,128]{2,1,0:T(8,128)(2,1)S(1)}, u32[]{:S(2)}, u32[]{:S(2)}) collective-permute-start(bf16[2,128,128]{2,1,0:T(8,128)(2,1)S(1)} %collective-permute-done.11.refs_0_), channel_id=1, source_target_pairs={{0,1},{1,0},{2,3},{3,2},{4,5},{5,4},{6,7},{7,6},{8,9},{9,8},{10,11... | collective-permute-start | bytes 196616 | tf_op jit(solution)/shard_map/ppermute | solution.py:162
  28.5 1.7 %collective-permute-start.14 = (bf16[2,128,128]{2,1,0:T(8,128)(2,1)S(1)}, bf16[2,128,128]{2,1,0:T(8,128)(2,1)S(1)}, u32[]{:S(2)}, u32[]{:S(2)}) collective-permute-start(bf16[2,128,128]{2,1,0:T(8,128)(2,1)S(1)} %collective-permute-done.9.refs_1_), channel_id=1, source_target_pairs={{0,1},{1,0},{2,3},{3,2},{4,5},{5,4},{6,7},{7,6},{8,9},{9,8},{10,11... | collective-permute-start | bytes 196616 | tf_op jit(solution)/shard_map/ppermute | solution.py:162
  28.8 1.5 %collective-permute-start.15 = (bf16[2,128,128]{2,1,0:T(8,128)(2,1)S(1)}, bf16[2,128,128]{2,1,0:T(8,128)(2,1)S(1)}, u32[]{:S(2)}, u32[]{:S(2)}) collective-permute-start(bf16[2,128,128]{2,1,0:T(8,128)(2,1)S(1)} %collective-permute-done.10.refs_2_), channel_id=1, source_target_pairs={{0,1},{1,0},{2,3},{3,2},{4,5},{5,4},{6,7},{7,6},{8,9},{9,8},{10,11... | collective-permute-start | bytes 196616 | tf_op jit(solution)/shard_map/ppermute | solution.py:162

commit v9 on v8

--- a/solution.py
+++ b/solution.py
@@ -121,7 +121,7 @@
 def load_store(store, size, names, after):
     store, _ = lax.optimization_barrier((store, after))
     rows, layers, feats = store.shape
-    entries = len(names) * entry_count(size)
+    entries = sum(entry_count(name, size) for name in names)
     shape = (entries, rows, layers, feats // size)
     return pl.pallas_call(
         functools.partial(load_kernel, size, names),
@@ -187,8 +187,8 @@
     two, three, *_ = lax.optimization_barrier(
         (two, three, got["core"], got["core_one"], *late(got))
     )
-    got.update(two=two, core_two=send(two, 1, 1, size))
-    got.update(three=three, core_three=send(three, 1, 1, size))
+    last = jnp.concatenate([two, three], axis=0)
+    got.update(last=last, core_last=send(last, 1, 1, size))
     return got
 
 
@@ -206,16 +206,18 @@
         mine, theirs = jnp.where(is_odd, odd, even), jnp.where(is_odd, even, odd)
         places[name] = [me ^ mine ^ entry for entry in share]
         places["core_" + name] = [core ^ theirs ^ entry for entry in share]
+    for name in ("", "core_"):
+        places[name + "last"] = places.pop(name + "two") + places.pop(name + "three")
     return places
 
 
-def entry_count(size):
-    return 1 << len(far_steps(size))
+def entry_count(name, size):
+    return (2 if name.endswith("last") else 1) << len(far_steps(size))
 
 
 FIRST = (1, ((7, 7), (5, 5), (3, 3)), True)
 SECOND = (1, ((7, 7), (5, 5), (3, 3)), False)
-NAMES = ("own", "core", "one", "two", "three", "core_one", "core_two", "core_three")
+NAMES = ("own", "core", "one", "core_one", "last", "core_last")
 
 
 def fisher_kernel(size, *refs):
@@ -372,15 +374,16 @@
         homes = (
             ("own", "core"),
             ("one", "core_one"),
-            ("two", "three"),
-            ("core_two", "core_three"),
+            ("last",),
+            ("core_last",),
         )
 
         def home_of(name):
             return next(k for k, home in enumerate(homes) if name in home)
 
         def start_of(name):
-            return homes[home_of(name)].index(name) * entry_count(size)
+            home = homes[home_of(name)]
+            return sum(entry_count(other, size) for other in home[: home.index(name)])
 
         got = gather(
             grads,
@@ -409,9 +412,9 @@
             lambda got: [add(got, "own", "core"), load(3, homes[3], got["core"])],
             lambda got: [add(got, "one")],
         )
-        add(got, "core_one", "two", "three")
+        add(got, "core_one", "last")
         return score_call(
-            [got["core_two"], got["core_three"]], ready[3], start_of("core_two"),
+            [got["core_last"]], ready[3], start_of("core_last"),
             ready["total"], scaling, factors.shape[0] * size,
         )
 

time: 32 us -> 31.9 us (level)
  starting transfers between devices: 15.4 us -> 14.7 us
  waiting for transfers between devices: 4.78 us -> 5.27 us
    ppermute x16 -> x14, starting transfers between devices: 15.4 us -> 14.7 us  [send(): return lax.ppermute(value, 'blk', pairs)]
    ppermute x16 -> x14, waiting for transfers between devices: 4.78 us -> 5.27 us  [send(): return lax.ppermute(value, 'blk', pairs)]
    unnamed x14 -> x16, local copies, waits for them, and re-layouts: 0.86 us -> 0.91 us
  transfers between devices with their start and end apart: 16 -> 14, of which waited for: 7 -> 6; matrix products, arithmetic and copies ran while one was open for 0% -> 0% of each run, Pallas kernels for 22% -> 23%
where the time goes in v9:
time: 31.9 us; the launch traced here: 31.7 us
  starting transfers between devices  14.7 us (46%)
  Pallas kernels  10.4 us (33%)
  waiting for transfers between devices  5.27 us (17%)
  local copies, waits for them, and re-layouts  0.98 us (3%)
    ppermute x14, starting transfers between devices, send(): return lax.ppermute(value, 'blk', pairs)  14.7 us
    ppermute x14, waiting for transfers between devices, send(): return lax.ppermute(value, 'blk', pairs)  5.27 us
    pallas_call x4, Pallas kernels, load_store(): pl.pallas_call(functools.partial(load_kernel, size, names), out_shape=jax...  4.42 us
    pallas_call x3, Pallas kernels, partial_call(): pl.pallas_call(functools.partial(partial_kernel, tuple(starts)), out_shap...  2.42 us
    pallas_call x1, Pallas kernels, score_call(): pl.pallas_call(functools.partial(score_kernel, queries, start), out_shape...  1.61 us
    pallas_call x1, Pallas kernels, fisher_call(): pl.pallas_call(functools.partial(fisher_kernel, size), out_shape=jax.Shap...  1.36 us
    unnamed x16, local copies, waits for them, and re-layouts  0.91 us
  transfers between devices with their start and end apart: 14, of which 6 were waited for; matrix products, arithmetic and copies ran while one was open for 0% of the time, Pallas kernels for 23%

profile of v9, /device:TPU:0, one launch (start us, length us, event | category | flops | bytes accessed | tf_op | source)
XLA Modules:
  0.0 31.7 jit_solution(1133481857745029553)
XLA Ops:
  0.0 0.8 %copy-done.1 = bf16[2,2,64,128]{3,2,1,0:T(8,128)(2,1)S(1)} copy-done((bf16[2,2,64,128]{3,2,1,0:T(8,128)(2,1)S(1)}, bf16[2,2,64,128]{3,2,1,0:T(8,128)(2,1)}, u32[]{:S(2)}) %copy-start.1) | copy-done | bytes 65560
  0.8 0.3 %shard_map.65 = bf16[64,2,128]{2,1,0:T(2,128)(2,1)S(1)} custom-call(bf16[2,2,64,128]{3,2,1,0:T(8,128)(2,1)S(1)} %copy-done.1, s32[2,64]{1,0:T(2,128)S(1)} %copy-done.2, f32[64,64]{1,0:T(8,128)S(1)} %shard_map.64.zeros_ref), custom_call_target="tpu_custom_call" | custom-call | flops 10000000000 | tf_op jit(solution)/shard_map/pallas_call | solution.py:93
  1.2 3.5 %collective-permute-start = (bf16[1,64,2,128]{3,2,1,0:T(2,128)(2,1)S(1)}, bf16[1,64,2,128]{3,2,1,0:T(2,128)(2,1)S(1)}, u32[]{:S(2)}, u32[]{:S(2)}) collective-permute-start(bf16[1,64,2,128]{3,2,1,0:T(2,128)(2,1)S(1)} %bitcast.7), channel_id=1, source_target_pairs={{0,9},{1,8},{2,11},{3,10},{4,13},{5,12},{6,15},{7,14},{8,1},{9,0},... | collective-permute-start | bytes 98312 | tf_op jit(solution)/shard_map/ppermute | solution.py:162
  4.7 0.3 shard_map.66.refs_6_
  5.0 1.5 %collective-permute-done = bf16[1,64,2,128]{3,2,1,0:T(2,128)(2,1)S(1)} collective-permute-done((bf16[1,64,2,128]{3,2,1,0:T(2,128)(2,1)S(1)}, bf16[1,64,2,128]{3,2,1,0:T(2,128)(2,1)S(1)}, u32[]{:S(2)}, u32[]{:S(2)}) %collective-permute-start) | collective-permute-done | bytes 32800 | tf_op jit(solution)/shard_map/ppermute | solution.py:162
  6.5 0.1 pad_maximum_fusion.refs_0_
  6.6 2.9 %collective-permute-start.1 = (bf16[2,64,2,128]{3,2,1,0:T(2,128)(2,1)S(1)}, bf16[2,64,2,128]{3,2,1,0:T(2,128)(2,1)S(1)}, u32[]{:S(2)}, u32[]{:S(2)}) collective-permute-start(bf16[2,64,2,128]{3,2,1,0:T(2,128)(2,1)S(1)} %pad_maximum_fusion.refs_0_), channel_id=1, source_target_pairs={{0,7},{1,6},{2,5},{3,4},{4,3},{5,2},{6,1},{7,0},{8,15},{9,14},{10,... | collective-permute-start | bytes 196616 | tf_op jit(solution)/shard_map/ppermute | solution.py:162
  9.5 0.5 %collective-permute-start.4 = (bf16[2,64,2,128]{3,2,1,0:T(2,128)(2,1)S(1)}, bf16[2,64,2,128]{3,2,1,0:T(2,128)(2,1)S(1)}, u32[]{:S(2)}, u32[]{:S(2)}) collective-permute-start(bf16[2,64,2,128]{3,2,1,0:T(2,128)(2,1)S(1)} %pad_maximum_fusion.refs_0_), channel_id=1, source_target_pairs={{0,5},{1,4},{2,7},{3,6},{4,1},{5,0},{6,3},{7,2},{8,13},{9,12},{10,... | collective-permute-start | bytes 196616 | tf_op jit(solution)/shard_map/ppermute | solution.py:162
  10.0 0.2 collective-permute-start.5
  10.2 1.1 %shard_map.67.refs_2_.refs_3_ = bf16[4,512,2,256]{3,2,1,0:T(2,128)(2,1)S(1)} custom-call(bf16[512,2,4096]{2,1,0:T(2,128)(2,1)S(1)} %bitcast.4), custom_call_target="tpu_custom_call" | custom-call | bytes 2097152 | tf_op jit(solution)/shard_map/pallas_call | solution.py:126
  11.3 0.7 %collective-permute-done.1.refs_2_ = bf16[2,64,2,128]{3,2,1,0:T(2,128)(2,1)S(1)} collective-permute-done((bf16[2,64,2,128]{3,2,1,0:T(2,128)(2,1)S(1)}, bf16[2,64,2,128]{3,2,1,0:T(2,128)(2,1)S(1)}, u32[]{:S(2)}, u32[]{:S(2)}) %collective-permute-start.1) | collective-permute-done | bytes 65568 | tf_op jit(solution)/shard_map/ppermute | solution.py:162
  12.0 0.5 %collective-permute-start.3 = (bf16[2,64,2,128]{3,2,1,0:T(2,128)(2,1)S(1)}, bf16[2,64,2,128]{3,2,1,0:T(2,128)(2,1)S(1)}, u32[]{:S(2)}, u32[]{:S(2)}) collective-permute-start(bf16[2,64,2,128]{3,2,1,0:T(2,128)(2,1)S(1)} %collective-permute-done.1.refs_2_), channel_id=1, source_target_pairs={{0,1},{1,0},{2,3},{3,2},{4,5},{5,4},{6,7},{7,6},{8,9},{9,8},{10,11... | collective-permute-start | bytes 196616 | tf_op jit(solution)/shard_map/ppermute | solution.py:162
  12.5 1.1 %shard_map.68.refs_1_.refs_2_ = bf16[4,512,2,256]{3,2,1,0:T(2,128)(2,1)S(1)} custom-call(bf16[512,2,4096]{2,1,0:T(2,128)(2,1)S(1)} %bitcast.4), custom_call_target="tpu_custom_call" | custom-call | bytes 2097152 | tf_op jit(solution)/shard_map/pallas_call | solution.py:126
  13.6 0.5 %collective-permute-done.5 = bf16[2,64,2,128]{3,2,1,0:T(2,128)(2,1)S(1)} collective-permute-done((bf16[2,64,2,128]{3,2,1,0:T(2,128)(2,1)S(1)}, bf16[2,64,2,128]{3,2,1,0:T(2,128)(2,1)S(1)}, u32[]{:S(2)}, u32[]{:S(2)}) %collective-permute-start.5) | collective-permute-done | bytes 65568 | tf_op jit(solution)/shard_map/ppermute | solution.py:162
  14.2 0.2 collective-permute-start.6
  14.4 1.2 %collective-permute-done.6.refs_5_ = bf16[4,64,2,128]{3,2,1,0:T(2,128)(2,1)S(1)} collective-permute-done((bf16[4,64,2,128]{3,2,1,0:T(2,128)(2,1)S(1)}, bf16[4,64,2,128]{3,2,1,0:T(2,128)(2,1)S(1)}, u32[]{:S(2)}, u32[]{:S(2)}) %collective-permute-start.6) | collective-permute-done | bytes 131104 | tf_op jit(solution)/shard_map/ppermute | solution.py:162
  15.6 1.4 %shard_map.69 = bf16[128,128]{1,0:T(8,128)(2,1)S(1)} custom-call(bf16[2,64,2,128]{3,2,1,0:T(2,128)(2,1)S(1)} %pad_maximum_fusion.refs_0_, bf16[2,64,2,128]{3,2,1,0:T(2,128)(2,1)S(1)} %collective-permute-done.2.refs_1_, bf16[2,64,2,128]{3,2,1,0:T(2,128)(2,1)S(1)} %collective-permute-done.1.refs_2_, ...), custom_call_target="tpu_custom_call" | custom-call | tf_op jit(solution)/shard_map/pallas_call | solution.py:257
  17.0 2.8 %collective-permute-start.7 = (bf16[1,128,128]{2,1,0:T(8,128)(2,1)S(1)}, bf16[1,128,128]{2,1,0:T(8,128)(2,1)S(1)}, u32[]{:S(2)}, u32[]{:S(2)}) collective-permute-start(bf16[1,128,128]{2,1,0:T(8,128)(2,1)S(1)} %bitcast.5), channel_id=1, source_target_pairs={{0,9},{1,8},{2,11},{3,10},{4,13},{5,12},{6,15},{7,14},{8,1},{9,0},... | collective-permute-start | bytes 98312 | tf_op jit(solution)/shard_map/ppermute | solution.py:162
  19.7 1.1 %shard_map.70.refs_3_ = bf16[4,512,2,256]{3,2,1,0:T(2,128)(2,1)S(1)} custom-call(bf16[512,2,4096]{2,1,0:T(2,128)(2,1)S(1)} %bitcast.4), custom_call_target="tpu_custom_call" | custom-call | bytes 2097152 | tf_op jit(solution)/shard_map/pallas_call | solution.py:126
  20.8 0.5 %collective-permute-done.7 = bf16[1,128,128]{2,1,0:T(8,128)(2,1)S(1)} collective-permute-done((bf16[1,128,128]{2,1,0:T(8,128)(2,1)S(1)}, bf16[1,128,128]{2,1,0:T(8,128)(2,1)S(1)}, u32[]{:S(2)}, u32[]{:S(2)}) %collective-permute-start.7) | collective-permute-done | bytes 32800 | tf_op jit(solution)/shard_map/ppermute | solution.py:162
  21.4 0.4 %collective-permute-start.11 = (bf16[2,128,128]{2,1,0:T(8,128)(2,1)S(1)}, bf16[2,128,128]{2,1,0:T(8,128)(2,1)S(1)}, u32[]{:S(2)}, u32[]{:S(2)}) collective-permute-start(bf16[2,128,128]{2,1,0:T(8,128)(2,1)S(1)} %pad_maximum_fusion.1.refs_0_), channel_id=1, source_target_pairs={{0,1},{1,0},{2,3},{3,2},{4,5},{5,4},{6,7},{7,6},{8,9},{9,8},{10,11... | collective-permute-start | bytes 196616 | tf_op jit(solution)/shard_map/ppermute | solution.py:162
  21.8 2.8 %collective-permute-start.10 = (bf16[2,128,128]{2,1,0:T(8,128)(2,1)S(1)}, bf16[2,128,128]{2,1,0:T(8,128)(2,1)S(1)}, u32[]{:S(2)}, u32[]{:S(2)}) collective-permute-start(bf16[2,128,128]{2,1,0:T(8,128)(2,1)S(1)} %pad_maximum_fusion.1.refs_0_), channel_id=1, source_target_pairs={{0,7},{1,6},{2,5},{3,4},{4,3},{5,2},{6,1},{7,0},{8,15},{9,14},{10,... | collective-permute-start | bytes 196616 | tf_op jit(solution)/shard_map/ppermute | solution.py:162
  24.6 0.4 %collective-permute-start.9 = (bf16[2,128,128]{2,1,0:T(8,128)(2,1)S(1)}, bf16[2,128,128]{2,1,0:T(8,128)(2,1)S(1)}, u32[]{:S(2)}, u32[]{:S(2)}) collective-permute-start(bf16[2,128,128]{2,1,0:T(8,128)(2,1)S(1)} %pad_maximum_fusion.1.refs_0_), channel_id=1, source_target_pairs={{0,3},{1,2},{2,1},{3,0},{4,7},{5,6},{6,5},{7,4},{8,11},{9,10},{10,... | collective-permute-start | bytes 196616 | tf_op jit(solution)/shard_map/ppermute | solution.py:162
  25.0 1.1 %shard_map.72.refs_1_ = bf16[4,512,2,256]{3,2,1,0:T(2,128)(2,1)S(1)} custom-call(bf16[512,2,4096]{2,1,0:T(2,128)(2,1)S(1)} %bitcast.4), custom_call_target="tpu_custom_call" | custom-call | bytes 2097152 | tf_op jit(solution)/shard_map/pallas_call | solution.py:126
  26.1 0.8 %shard_map.71.refs_2_ = f32[1024,128]{1,0:T(8,128)S(1)} custom-call(bf16[2,128,128]{2,1,0:T(8,128)(2,1)S(1)} %pad_maximum_fusion.1.refs_0_, bf16[2,128,128]{2,1,0:T(8,128)(2,1)S(1)} %collective-permute-done.11.refs_1_, bf16[4,512,2,256]{3,2,1,0:T(2,128)(2,1)S(1)} %shard_map.67.refs_2_.refs_3_, bf16[4,512,2,256]{3,2,1,0:T(2,128)(2,1)S(1)} %shard_map.67.refs_2_.refs_3_), custom_call_target="tpu_custom_call" | custom-call | tf_op jit(solution)/shard_map/pallas_call | solution.py:302
  27.0 0.3 collective-permute-start.12
  27.3 0.5 %shard_map.73.refs_4_ = f32[1024,128]{1,0:T(8,128)S(1)} custom-call(bf16[2,128,128]{2,1,0:T(8,128)(2,1)S(1)} %collective-permute-done.10.refs_0_, bf16[4,512,2,256]{3,2,1,0:T(2,128)(2,1)S(1)} %shard_map.68.refs_1_.refs_2_, f32[1024,128]{1,0:T(8,128)S(1)} %shard_map.71.refs_2_), custom_call_target="tpu_custom_call" | custom-call | tf_op jit(solution)/shard_map/pallas_call | solution.py:302
  27.8 0.8 %collective-permute-done.8 = bf16[2,128,128]{2,1,0:T(8,128)(2,1)S(1)} collective-permute-done((bf16[2,128,128]{2,1,0:T(8,128)(2,1)S(1)}, bf16[2,128,128]{2,1,0:T(8,128)(2,1)S(1)}, u32[]{:S(2)}, u32[]{:S(2)}) %collective-permute-start.8) | collective-permute-done | bytes 65568 | tf_op jit(solution)/shard_map/ppermute | solution.py:162
  28.7 0.2 collective-permute-start.13
  28.9 0.1 select_reduce_fusion
  29.0 1.1 %shard_map.74.refs_2_ = f32[1024,128]{1,0:T(8,128)S(1)} custom-call(bf16[2,128,128]{2,1,0:T(8,128)(2,1)S(1)} %collective-permute-done.12.refs_0_, bf16[4,128,128]{2,1,0:T(8,128)(2,1)S(1)} %constant_dynamic-update-slice_fusion.2.refs_1_, bf16[4,512,2,256]{3,2,1,0:T(2,128)(2,1)S(1)} %shard_map.68.refs_1_.refs_2_, ...), custom_call_target="tpu_custom_call" | custom-call | tf_op jit(solution)/shard_map/pallas_call | solution.py:302
  30.1 1.6 %shard_map.75 = f32[32,512]{1,0:T(8,128)} custom-call(bf16[4,128,128]{2,1,0:T(8,128)(2,1)S(1)} %collective-permute-done.13.refs_0_, bf16[4,512,2,256]{3,2,1,0:T(2,128)(2,1)S(1)} %shard_map.72.refs_1_, f32[1024,128]{1,0:T(8,128)S(1)} %shard_map.74.refs_2_, f32[1,512]{1,0:T(1,128)S(1)} %bitcast.9), custom_call_target="tpu_custom_call" | custom-call | tf_op jit(solution)/shard_map/pallas_call | solution.py:331
  (30 shorter events, 0.2 us)
Async XLA Ops:
  0.0 0.8 %copy-start.1 = (bf16[2,2,64,128]{3,2,1,0:T(8,128)(2,1)S(1)}, bf16[2,2,64,128]{3,2,1,0:T(8,128)(2,1)}, u32[]{:S(2)}) copy-start(bf16[2,2,64,128]{3,2,1,0:T(8,128)(2,1)} %factors_ref.1) | copy-start | bytes 196612
  0.0 0.8 %copy-start.2 = (s32[2,64]{1,0:T(2,128)S(1)}, s32[2,64]{1,0:T(2,128)}, u32[]{:S(2)}) copy-start(s32[2,64]{1,0:T(2,128)} %mask_ref.1) | copy-start | bytes 1540
  0.0 10.1 %slice-start = ((s8[8388608]{0:T(1024)(128)(4,1)}), s8[4194304]{0:T(1024)(128)(4,1)S(1)}, s32[]{:S(2)}) async-start(s8[8388608]{0:T(1024)(128)(4,1)} %bitcast.3), calls=%async_computation | async-start | bytes 8388608
  0.8 3.9 %copy-start = (bf16[2,256,4096]{2,1,0:T(8,128)(2,1)S(1)}, bf16[2,256,4096]{2,1,0:T(8,128)(2,1)}, u32[]{:S(2)}) copy-start(bf16[2,256,4096]{2,1,0:T(8,128)(2,1)} %source_ref) | copy-start | bytes 12582916
  0.8 9.3 %slice-start.1 = ((s8[8388608]{0:T(1024)(128)(4,1)}), s8[4194304]{0:T(1024)(128)(4,1)S(1)}, s32[]{:S(2)}) async-start(s8[8388608]{0:T(1024)(128)(4,1)} %bitcast.3), calls=%async_computation.1 | async-start | bytes 8388608
  1.2 5.3 %collective-permute-start = (bf16[1,64,2,128]{3,2,1,0:T(2,128)(2,1)S(1)}, bf16[1,64,2,128]{3,2,1,0:T(2,128)(2,1)S(1)}, u32[]{:S(2)}, u32[]{:S(2)}) collective-permute-start(bf16[1,64,2,128]{3,2,1,0:T(2,128)(2,1)S(1)} %bitcast.7), channel_id=1, source_target_pairs={{0,9},{1,8},{2,11},{3,10},{4,13},{5,12},{6,15},{7,14},{8,1},{9,0},... | collective-permute-start | bytes 98312 | tf_op jit(solution)/shard_map/ppermute | solution.py:162
  6.6 5.3 %collective-permute-start.1 = (bf16[2,64,2,128]{3,2,1,0:T(2,128)(2,1)S(1)}, bf16[2,64,2,128]{3,2,1,0:T(2,128)(2,1)S(1)}, u32[]{:S(2)}, u32[]{:S(2)}) collective-permute-start(bf16[2,64,2,128]{3,2,1,0:T(2,128)(2,1)S(1)} %pad_maximum_fusion.refs_0_), channel_id=1, source_target_pairs={{0,7},{1,6},{2,5},{3,4},{4,3},{5,2},{6,1},{7,0},{8,15},{9,14},{10,... | collective-permute-start | bytes 196616 | tf_op jit(solution)/shard_map/ppermute | solution.py:162
  9.5 4.1 %collective-permute-start.4 = (bf16[2,64,2,128]{3,2,1,0:T(2,128)(2,1)S(1)}, bf16[2,64,2,128]{3,2,1,0:T(2,128)(2,1)S(1)}, u32[]{:S(2)}, u32[]{:S(2)}) collective-permute-start(bf16[2,64,2,128]{3,2,1,0:T(2,128)(2,1)S(1)} %pad_maximum_fusion.refs_0_), channel_id=1, source_target_pairs={{0,5},{1,4},{2,7},{3,6},{4,1},{5,0},{6,3},{7,2},{8,13},{9,12},{10,... | collective-permute-start | bytes 196616 | tf_op jit(solution)/shard_map/ppermute | solution.py:162
  10.0 4.1 %collective-permute-start.5 = (bf16[2,64,2,128]{3,2,1,0:T(2,128)(2,1)S(1)}, bf16[2,64,2,128]{3,2,1,0:T(2,128)(2,1)S(1)}, u32[]{:S(2)}, u32[]{:S(2)}) collective-permute-start(bf16[2,64,2,128]{3,2,1,0:T(2,128)(2,1)S(1)} %pad_maximum_fusion.refs_0_), channel_id=1, source_target_pairs={{0,3},{1,2},{2,1},{3,0},{4,7},{5,6},{6,5},{7,4},{8,11},{9,10},{10,... | collective-permute-start | bytes 196616 | tf_op jit(solution)/shard_map/ppermute | solution.py:162
  12.0 2.1 %collective-permute-start.2 = (bf16[2,64,2,128]{3,2,1,0:T(2,128)(2,1)S(1)}, bf16[2,64,2,128]{3,2,1,0:T(2,128)(2,1)S(1)}, u32[]{:S(2)}, u32[]{:S(2)}) collective-permute-start(bf16[2,64,2,128]{3,2,1,0:T(2,128)(2,1)S(1)} %pad_maximum_fusion.refs_0_), channel_id=1, source_target_pairs={{0,1},{1,0},{2,3},{3,2},{4,5},{5,4},{6,7},{7,6},{8,9},{9,8},{10,11... | collective-permute-start | bytes 196616 | tf_op jit(solution)/shard_map/ppermute | solution.py:162
  12.0 2.1 %collective-permute-start.3 = (bf16[2,64,2,128]{3,2,1,0:T(2,128)(2,1)S(1)}, bf16[2,64,2,128]{3,2,1,0:T(2,128)(2,1)S(1)}, u32[]{:S(2)}, u32[]{:S(2)}) collective-permute-start(bf16[2,64,2,128]{3,2,1,0:T(2,128)(2,1)S(1)} %collective-permute-done.1.refs_2_), channel_id=1, source_target_pairs={{0,1},{1,0},{2,3},{3,2},{4,5},{5,4},{6,7},{7,6},{8,9},{9,8},{10,11... | collective-permute-start | bytes 196616 | tf_op jit(solution)/shard_map/ppermute | solution.py:162
  14.2 1.4 %collective-permute-start.6 = (bf16[4,64,2,128]{3,2,1,0:T(2,128)(2,1)S(1)}, bf16[4,64,2,128]{3,2,1,0:T(2,128)(2,1)S(1)}, u32[]{:S(2)}, u32[]{:S(2)}) collective-permute-start(bf16[4,64,2,128]{3,2,1,0:T(2,128)(2,1)S(1)} %constant_dynamic-update-slice_fusion.refs_4_), channel_id=1, source_target_pairs={{0,1},{1,0},{2,3},{3,2},{4,5},{5,4},{6,7},{7,6},{8,9},{9,8},{10,11... | collective-permute-start | bytes 393224 | tf_op jit(solution)/shard_map/ppermute | solution.py:162
  17.0 4.4 %collective-permute-start.7 = (bf16[1,128,128]{2,1,0:T(8,128)(2,1)S(1)}, bf16[1,128,128]{2,1,0:T(8,128)(2,1)S(1)}, u32[]{:S(2)}, u32[]{:S(2)}) collective-permute-start(bf16[1,128,128]{2,1,0:T(8,128)(2,1)S(1)} %bitcast.5), channel_id=1, source_target_pairs={{0,9},{1,8},{2,11},{3,10},{4,13},{5,12},{6,15},{7,14},{8,1},{9,0},... | collective-permute-start | bytes 98312 | tf_op jit(solution)/shard_map/ppermute | solution.py:162
  21.4 3.7 %collective-permute-start.11 = (bf16[2,128,128]{2,1,0:T(8,128)(2,1)S(1)}, bf16[2,128,128]{2,1,0:T(8,128)(2,1)S(1)}, u32[]{:S(2)}, u32[]{:S(2)}) collective-permute-start(bf16[2,128,128]{2,1,0:T(8,128)(2,1)S(1)} %pad_maximum_fusion.1.refs_0_), channel_id=1, source_target_pairs={{0,1},{1,0},{2,3},{3,2},{4,5},{5,4},{6,7},{7,6},{8,9},{9,8},{10,11... | collective-permute-start | bytes 196616 | tf_op jit(solution)/shard_map/ppermute | solution.py:162
  21.8 5.2 %collective-permute-start.10 = (bf16[2,128,128]{2,1,0:T(8,128)(2,1)S(1)}, bf16[2,128,128]{2,1,0:T(8,128)(2,1)S(1)}, u32[]{:S(2)}, u32[]{:S(2)}) collective-permute-start(bf16[2,128,128]{2,1,0:T(8,128)(2,1)S(1)} %pad_maximum_fusion.1.refs_0_), channel_id=1, source_target_pairs={{0,7},{1,6},{2,5},{3,4},{4,3},{5,2},{6,1},{7,0},{8,15},{9,14},{10,... | collective-permute-start | bytes 196616 | tf_op jit(solution)/shard_map/ppermute | solution.py:162
  24.6 4.0 %collective-permute-start.8 = (bf16[2,128,128]{2,1,0:T(8,128)(2,1)S(1)}, bf16[2,128,128]{2,1,0:T(8,128)(2,1)S(1)}, u32[]{:S(2)}, u32[]{:S(2)}) collective-permute-start(bf16[2,128,128]{2,1,0:T(8,128)(2,1)S(1)} %pad_maximum_fusion.1.refs_0_), channel_id=1, source_target_pairs={{0,5},{1,4},{2,7},{3,6},{4,1},{5,0},{6,3},{7,2},{8,13},{9,12},{10,... | collective-permute-start | bytes 196616 | tf_op jit(solution)/shard_map/ppermute | solution.py:162
  24.6 4.0 %collective-permute-start.9 = (bf16[2,128,128]{2,1,0:T(8,128)(2,1)S(1)}, bf16[2,128,128]{2,1,0:T(8,128)(2,1)S(1)}, u32[]{:S(2)}, u32[]{:S(2)}) collective-permute-start(bf16[2,128,128]{2,1,0:T(8,128)(2,1)S(1)} %pad_maximum_fusion.1.refs_0_), channel_id=1, source_target_pairs={{0,3},{1,2},{2,1},{3,0},{4,7},{5,6},{6,5},{7,4},{8,11},{9,10},{10,... | collective-permute-start | bytes 196616 | tf_op jit(solution)/shard_map/ppermute | solution.py:162
  27.0 2.0 %copy-start.3 = (s32[512]{0:T(512)S(1)}, s32[512]{0:T(512)}, u32[]{:S(2)}) copy-start(s32[512]{0:T(512)} %param.10) | copy-start | bytes 6148
  27.0 1.9 %copy-start.4 = (f32[16]{0:T(128)S(1)}, f32[16]{0:T(128)}, u32[]{:S(2)}) copy-start(f32[16]{0:T(128)} %param.11) | copy-start | bytes 196
  27.0 1.6 %collective-permute-start.12 = (bf16[2,128,128]{2,1,0:T(8,128)(2,1)S(1)}, bf16[2,128,128]{2,1,0:T(8,128)(2,1)S(1)}, u32[]{:S(2)}, u32[]{:S(2)}) collective-permute-start(bf16[2,128,128]{2,1,0:T(8,128)(2,1)S(1)} %collective-permute-done.10.refs_0_), channel_id=1, source_target_pairs={{0,1},{1,0},{2,3},{3,2},{4,5},{5,4},{6,7},{7,6},{8,9},{9,8},{10,11... | collective-permute-start | bytes 196616 | tf_op jit(solution)/shard_map/ppermute | solution.py:162
  28.7 1.5 %collective-permute-start.13 = (bf16[4,128,128]{2,1,0:T(8,128)(2,1)S(1)}, bf16[4,128,128]{2,1,0:T(8,128)(2,1)S(1)}, u32[]{:S(2)}, u32[]{:S(2)}) collective-permute-start(bf16[4,128,128]{2,1,0:T(8,128)(2,1)S(1)} %constant_dynamic-update-slice_fusion.2.refs_1_), channel_id=1, source_target_pairs={{0,1},{1,0},{2,3},{3,2},{4,5},{5,4},{6,7},{7,6},{8,9},{9,8},{10,11... | collective-permute-start | bytes 393224 | tf_op jit(solution)/shard_map/ppermute | solution.py:162

commit v10 on v9

--- a/solution.py
+++ b/solution.py
@@ -393,6 +393,9 @@
             lambda got: [load(0, homes[0], got["own"])],
             lambda got: [load(1, homes[1], got["one"])],
         )
+        got["core_last"], ready[2] = lax.optimization_barrier(
+            (got["core_last"], load(2, homes[2], got["last"]))
+        )
         hidden = fisher_call(got, ready["fisher"], size)
 
         def add(got, *names):
@@ -408,9 +411,9 @@
             hidden,
             size,
             SECOND,
-            lambda share: [load(2, homes[2], share)],
-            lambda got: [add(got, "own", "core"), load(3, homes[3], got["core"])],
-            lambda got: [add(got, "one")],
+            lambda share: [load(3, homes[3], share)],
+            lambda got: [],
+            lambda got: [add(got, "own", "core", "one")],
         )
         add(got, "core_one", "last")
         return score_call(

time: 31.9 us -> 31.9 us (level)
    pallas_call x3 -> x2, Pallas kernels: 2.42 us -> 2.23 us  [partial_call(): pl.pallas_call(functools.partial(partial_kernel, tuple(starts)), out_shap...]
  transfers between devices with their start and end apart: 14 -> 14, of which waited for: 6 -> 7; matrix products, arithmetic and copies ran while one was open for 0% -> 0% of each run, Pallas kernels for 23% -> 22%
where the time goes in v10:
time: 31.9 us; the launch traced here: 31.8 us
  starting transfers between devices  14.6 us (46%)
  Pallas kernels  10.3 us (32%)
  waiting for transfers between devices  5.57 us (17%)
  local copies, waits for them, and re-layouts  0.98 us (3%)
    ppermute x14, starting transfers between devices, send(): return lax.ppermute(value, 'blk', pairs)  14.6 us
    ppermute x14, waiting for transfers between devices, send(): return lax.ppermute(value, 'blk', pairs)  5.57 us
    pallas_call x4, Pallas kernels, load_store(): pl.pallas_call(functools.partial(load_kernel, size, names), out_shape=jax...  4.41 us
    pallas_call x2, Pallas kernels, partial_call(): pl.pallas_call(functools.partial(partial_kernel, tuple(starts)), out_shap...  2.23 us
    pallas_call x1, Pallas kernels, score_call(): pl.pallas_call(functools.partial(score_kernel, queries, start), out_shape...  1.61 us
    pallas_call x1, Pallas kernels, fisher_call(): pl.pallas_call(functools.partial(fisher_kernel, size), out_shape=jax.Shap...  1.36 us
    unnamed x16, local copies, waits for them, and re-layouts  0.91 us
  transfers between devices with their start and end apart: 14, of which 7 were waited for; matrix products, arithmetic and copies ran while one was open for 0% of the time, Pallas kernels for 22%

profile of v10, /device:TPU:0, one launch (start us, length us, event | category | flops | bytes accessed | tf_op | source)
XLA Modules:
  0.0 31.8 jit_solution(5406741869905945269)
XLA Ops:
  0.0 0.8 %copy-done.1 = bf16[2,2,64,128]{3,2,1,0:T(8,128)(2,1)S(1)} copy-done((bf16[2,2,64,128]{3,2,1,0:T(8,128)(2,1)S(1)}, bf16[2,2,64,128]{3,2,1,0:T(8,128)(2,1)}, u32[]{:S(2)}) %copy-start.1) | copy-done | bytes 65560
  0.8 0.3 %shard_map.65 = bf16[64,2,128]{2,1,0:T(2,128)(2,1)S(1)} custom-call(bf16[2,2,64,128]{3,2,1,0:T(8,128)(2,1)S(1)} %copy-done.1, s32[2,64]{1,0:T(2,128)S(1)} %copy-done.2, f32[64,64]{1,0:T(8,128)S(1)} %shard_map.64.zeros_ref), custom_call_target="tpu_custom_call" | custom-call | flops 10000000000 | tf_op jit(solution)/shard_map/pallas_call | solution.py:93
  1.2 3.5 %collective-permute-start = (bf16[1,64,2,128]{3,2,1,0:T(2,128)(2,1)S(1)}, bf16[1,64,2,128]{3,2,1,0:T(2,128)(2,1)S(1)}, u32[]{:S(2)}, u32[]{:S(2)}) collective-permute-start(bf16[1,64,2,128]{3,2,1,0:T(2,128)(2,1)S(1)} %bitcast.7), channel_id=1, source_target_pairs={{0,9},{1,8},{2,11},{3,10},{4,13},{5,12},{6,15},{7,14},{8,1},{9,0},... | collective-permute-start | bytes 98312 | tf_op jit(solution)/shard_map/ppermute | solution.py:162
  4.7 0.3 shard_map.66.refs_6_
  5.0 1.5 %collective-permute-done = bf16[1,64,2,128]{3,2,1,0:T(2,128)(2,1)S(1)} collective-permute-done((bf16[1,64,2,128]{3,2,1,0:T(2,128)(2,1)S(1)}, bf16[1,64,2,128]{3,2,1,0:T(2,128)(2,1)S(1)}, u32[]{:S(2)}, u32[]{:S(2)}) %collective-permute-start) | collective-permute-done | bytes 32800 | tf_op jit(solution)/shard_map/ppermute | solution.py:162
  6.5 0.1 pad_maximum_fusion.refs_0_
  6.6 2.9 %collective-permute-start.1 = (bf16[2,64,2,128]{3,2,1,0:T(2,128)(2,1)S(1)}, bf16[2,64,2,128]{3,2,1,0:T(2,128)(2,1)S(1)}, u32[]{:S(2)}, u32[]{:S(2)}) collective-permute-start(bf16[2,64,2,128]{3,2,1,0:T(2,128)(2,1)S(1)} %pad_maximum_fusion.refs_0_), channel_id=1, source_target_pairs={{0,7},{1,6},{2,5},{3,4},{4,3},{5,2},{6,1},{7,0},{8,15},{9,14},{10,... | collective-permute-start | bytes 196616 | tf_op jit(solution)/shard_map/ppermute | solution.py:162
  9.5 0.5 %collective-permute-start.4 = (bf16[2,64,2,128]{3,2,1,0:T(2,128)(2,1)S(1)}, bf16[2,64,2,128]{3,2,1,0:T(2,128)(2,1)S(1)}, u32[]{:S(2)}, u32[]{:S(2)}) collective-permute-start(bf16[2,64,2,128]{3,2,1,0:T(2,128)(2,1)S(1)} %pad_maximum_fusion.refs_0_), channel_id=1, source_target_pairs={{0,5},{1,4},{2,7},{3,6},{4,1},{5,0},{6,3},{7,2},{8,13},{9,12},{10,... | collective-permute-start | bytes 196616 | tf_op jit(solution)/shard_map/ppermute | solution.py:162
  10.0 0.2 collective-permute-start.5
  10.2 1.1 %shard_map.67.refs_3_.refs_4_ = bf16[4,512,2,256]{3,2,1,0:T(2,128)(2,1)S(1)} custom-call(bf16[512,2,4096]{2,1,0:T(2,128)(2,1)S(1)} %bitcast.4), custom_call_target="tpu_custom_call" | custom-call | bytes 2097152 | tf_op jit(solution)/shard_map/pallas_call | solution.py:126
  11.3 0.7 %collective-permute-done.1.refs_2_ = bf16[2,64,2,128]{3,2,1,0:T(2,128)(2,1)S(1)} collective-permute-done((bf16[2,64,2,128]{3,2,1,0:T(2,128)(2,1)S(1)}, bf16[2,64,2,128]{3,2,1,0:T(2,128)(2,1)S(1)}, u32[]{:S(2)}, u32[]{:S(2)}) %collective-permute-start.1) | collective-permute-done | bytes 65568 | tf_op jit(solution)/shard_map/ppermute | solution.py:162
  12.0 0.5 %collective-permute-start.3 = (bf16[2,64,2,128]{3,2,1,0:T(2,128)(2,1)S(1)}, bf16[2,64,2,128]{3,2,1,0:T(2,128)(2,1)S(1)}, u32[]{:S(2)}, u32[]{:S(2)}) collective-permute-start(bf16[2,64,2,128]{3,2,1,0:T(2,128)(2,1)S(1)} %collective-permute-done.1.refs_2_), channel_id=1, source_target_pairs={{0,1},{1,0},{2,3},{3,2},{4,5},{5,4},{6,7},{7,6},{8,9},{9,8},{10,11... | collective-permute-start | bytes 196616 | tf_op jit(solution)/shard_map/ppermute | solution.py:162
  12.5 1.1 %shard_map.68.refs_5_.refs_2_ = bf16[4,512,2,256]{3,2,1,0:T(2,128)(2,1)S(1)} custom-call(bf16[512,2,4096]{2,1,0:T(2,128)(2,1)S(1)} %bitcast.4), custom_call_target="tpu_custom_call" | custom-call | bytes 2097152 | tf_op jit(solution)/shard_map/pallas_call | solution.py:126
  13.6 0.5 %collective-permute-done.5 = bf16[2,64,2,128]{3,2,1,0:T(2,128)(2,1)S(1)} collective-permute-done((bf16[2,64,2,128]{3,2,1,0:T(2,128)(2,1)S(1)}, bf16[2,64,2,128]{3,2,1,0:T(2,128)(2,1)S(1)}, u32[]{:S(2)}, u32[]{:S(2)}) %collective-permute-start.5) | collective-permute-done | bytes 65568 | tf_op jit(solution)/shard_map/ppermute | solution.py:162
  14.2 0.2 collective-permute-start.6
  14.4 1.1 %shard_map.69.refs_3_ = bf16[4,512,2,256]{3,2,1,0:T(2,128)(2,1)S(1)} custom-call(bf16[512,2,4096]{2,1,0:T(2,128)(2,1)S(1)} %bitcast.4), custom_call_target="tpu_custom_call" | custom-call | bytes 2097152 | tf_op jit(solution)/shard_map/pallas_call | solution.py:126
  15.5 0.1 collective-permute-done.6.refs_5_
  15.6 1.4 %shard_map.70 = bf16[128,128]{1,0:T(8,128)(2,1)S(1)} custom-call(bf16[2,64,2,128]{3,2,1,0:T(2,128)(2,1)S(1)} %pad_maximum_fusion.refs_0_, bf16[2,64,2,128]{3,2,1,0:T(2,128)(2,1)S(1)} %collective-permute-done.2.refs_1_, bf16[2,64,2,128]{3,2,1,0:T(2,128)(2,1)S(1)} %collective-permute-done.1.refs_2_, ...), custom_call_target="tpu_custom_call" | custom-call | tf_op jit(solution)/shard_map/pallas_call | solution.py:257
  17.0 2.9 %collective-permute-start.7 = (bf16[1,128,128]{2,1,0:T(8,128)(2,1)S(1)}, bf16[1,128,128]{2,1,0:T(8,128)(2,1)S(1)}, u32[]{:S(2)}, u32[]{:S(2)}) collective-permute-start(bf16[1,128,128]{2,1,0:T(8,128)(2,1)S(1)} %bitcast.5), channel_id=1, source_target_pairs={{0,9},{1,8},{2,11},{3,10},{4,13},{5,12},{6,15},{7,14},{8,1},{9,0},... | collective-permute-start | bytes 98312 | tf_op jit(solution)/shard_map/ppermute | solution.py:162
  19.9 1.1 %shard_map.71.refs_1_ = bf16[4,512,2,256]{3,2,1,0:T(2,128)(2,1)S(1)} custom-call(bf16[512,2,4096]{2,1,0:T(2,128)(2,1)S(1)} %bitcast.4), custom_call_target="tpu_custom_call" | custom-call | bytes 2097152 | tf_op jit(solution)/shard_map/pallas_call | solution.py:126
  21.0 0.5 %collective-permute-done.7 = bf16[1,128,128]{2,1,0:T(8,128)(2,1)S(1)} collective-permute-done((bf16[1,128,128]{2,1,0:T(8,128)(2,1)S(1)}, bf16[1,128,128]{2,1,0:T(8,128)(2,1)S(1)}, u32[]{:S(2)}, u32[]{:S(2)}) %collective-permute-start.7) | collective-permute-done | bytes 32800 | tf_op jit(solution)/shard_map/ppermute | solution.py:162
  21.5 2.9 %collective-permute-start.10 = (bf16[2,128,128]{2,1,0:T(8,128)(2,1)S(1)}, bf16[2,128,128]{2,1,0:T(8,128)(2,1)S(1)}, u32[]{:S(2)}, u32[]{:S(2)}) collective-permute-start(bf16[2,128,128]{2,1,0:T(8,128)(2,1)S(1)} %pad_maximum_fusion.1.refs_0_), channel_id=1, source_target_pairs={{0,7},{1,6},{2,5},{3,4},{4,3},{5,2},{6,1},{7,0},{8,15},{9,14},{10,... | collective-permute-start | bytes 196616 | tf_op jit(solution)/shard_map/ppermute | solution.py:162
  24.4 0.2 collective-permute-start.11
  24.6 0.5 %collective-permute-start.9 = (bf16[2,128,128]{2,1,0:T(8,128)(2,1)S(1)}, bf16[2,128,128]{2,1,0:T(8,128)(2,1)S(1)}, u32[]{:S(2)}, u32[]{:S(2)}) collective-permute-start(bf16[2,128,128]{2,1,0:T(8,128)(2,1)S(1)} %pad_maximum_fusion.1.refs_0_), channel_id=1, source_target_pairs={{0,3},{1,2},{2,1},{3,0},{4,7},{5,6},{6,5},{7,4},{8,11},{9,10},{10,... | collective-permute-start | bytes 196616 | tf_op jit(solution)/shard_map/ppermute | solution.py:162
  25.1 1.6 %collective-permute-done.10.refs_2_ = bf16[2,128,128]{2,1,0:T(8,128)(2,1)S(1)} collective-permute-done((bf16[2,128,128]{2,1,0:T(8,128)(2,1)S(1)}, bf16[2,128,128]{2,1,0:T(8,128)(2,1)S(1)}, u32[]{:S(2)}, u32[]{:S(2)}) %collective-permute-start.10) | collective-permute-done | bytes 65568 | tf_op jit(solution)/shard_map/ppermute | solution.py:162
  26.8 0.1 collective-permute-start.12
  26.9 1.1 %shard_map.72.refs_4_ = f32[1024,128]{1,0:T(8,128)S(1)} custom-call(bf16[2,128,128]{2,1,0:T(8,128)(2,1)S(1)} %pad_maximum_fusion.1.refs_0_, bf16[2,128,128]{2,1,0:T(8,128)(2,1)S(1)} %collective-permute-done.11.refs_1_, bf16[2,128,128]{2,1,0:T(8,128)(2,1)S(1)} %collective-permute-done.10.refs_2_, bf16[4,512,2,256]{3,2,1,0:T(2,128)(2,1)S(1)} %shard_map.67.refs_3_.refs_4_, ...), custom_call_target="tpu_custom_call" | custom-call | tf_op jit(solution)/shard_map/pallas_call | solution.py:302
  28.0 0.6 %collective-permute-done.8 = bf16[2,128,128]{2,1,0:T(8,128)(2,1)S(1)} collective-permute-done((bf16[2,128,128]{2,1,0:T(8,128)(2,1)S(1)}, bf16[2,128,128]{2,1,0:T(8,128)(2,1)S(1)}, u32[]{:S(2)}, u32[]{:S(2)}) %collective-permute-start.8) | collective-permute-done | bytes 65568 | tf_op jit(solution)/shard_map/ppermute | solution.py:162
  28.6 0.3 collective-permute-start.13
  28.9 0.1 select_reduce_fusion
  29.0 1.1 %shard_map.73.refs_2_ = f32[1024,128]{1,0:T(8,128)S(1)} custom-call(bf16[2,128,128]{2,1,0:T(8,128)(2,1)S(1)} %collective-permute-done.12.refs_0_, bf16[4,128,128]{2,1,0:T(8,128)(2,1)S(1)} %constant_dynamic-update-slice_fusion.2.refs_1_, bf16[4,512,2,256]{3,2,1,0:T(2,128)(2,1)S(1)} %shard_map.68.refs_5_.refs_2_, ...), custom_call_target="tpu_custom_call" | custom-call | tf_op jit(solution)/shard_map/pallas_call | solution.py:302
  30.1 1.6 %shard_map.74 = f32[32,512]{1,0:T(8,128)} custom-call(bf16[4,128,128]{2,1,0:T(8,128)(2,1)S(1)} %collective-permute-done.13.refs_0_, bf16[4,512,2,256]{3,2,1,0:T(2,128)(2,1)S(1)} %shard_map.71.refs_1_, f32[1024,128]{1,0:T(8,128)S(1)} %shard_map.73.refs_2_, f32[1,512]{1,0:T(1,128)S(1)} %bitcast.9), custom_call_target="tpu_custom_call" | custom-call | tf_op jit(solution)/shard_map/pallas_call | solution.py:331
  (29 shorter events, 0.2 us)
Async XLA Ops:
  0.0 0.8 %copy-start.1 = (bf16[2,2,64,128]{3,2,1,0:T(8,128)(2,1)S(1)}, bf16[2,2,64,128]{3,2,1,0:T(8,128)(2,1)}, u32[]{:S(2)}) copy-start(bf16[2,2,64,128]{3,2,1,0:T(8,128)(2,1)} %factors_ref.1) | copy-start | bytes 196612
  0.0 0.8 %copy-start.2 = (s32[2,64]{1,0:T(2,128)S(1)}, s32[2,64]{1,0:T(2,128)}, u32[]{:S(2)}) copy-start(s32[2,64]{1,0:T(2,128)} %mask_ref.1) | copy-start | bytes 1540
  0.0 10.1 %slice-start = ((s8[8388608]{0:T(1024)(128)(4,1)}), s8[4194304]{0:T(1024)(128)(4,1)S(1)}, s32[]{:S(2)}) async-start(s8[8388608]{0:T(1024)(128)(4,1)} %bitcast.3), calls=%async_computation | async-start | bytes 8388608
  0.8 3.9 %copy-start = (bf16[2,256,4096]{2,1,0:T(8,128)(2,1)S(1)}, bf16[2,256,4096]{2,1,0:T(8,128)(2,1)}, u32[]{:S(2)}) copy-start(bf16[2,256,4096]{2,1,0:T(8,128)(2,1)} %source_ref) | copy-start | bytes 12582916
  0.8 9.3 %slice-start.1 = ((s8[8388608]{0:T(1024)(128)(4,1)}), s8[4194304]{0:T(1024)(128)(4,1)S(1)}, s32[]{:S(2)}) async-start(s8[8388608]{0:T(1024)(128)(4,1)} %bitcast.3), calls=%async_computation.1 | async-start | bytes 8388608
  1.2 5.3 %collective-permute-start = (bf16[1,64,2,128]{3,2,1,0:T(2,128)(2,1)S(1)}, bf16[1,64,2,128]{3,2,1,0:T(2,128)(2,1)S(1)}, u32[]{:S(2)}, u32[]{:S(2)}) collective-permute-start(bf16[1,64,2,128]{3,2,1,0:T(2,128)(2,1)S(1)} %bitcast.7), channel_id=1, source_target_pairs={{0,9},{1,8},{2,11},{3,10},{4,13},{5,12},{6,15},{7,14},{8,1},{9,0},... | collective-permute-start | bytes 98312 | tf_op jit(solution)/shard_map/ppermute | solution.py:162
  6.6 5.3 %collective-permute-start.1 = (bf16[2,64,2,128]{3,2,1,0:T(2,128)(2,1)S(1)}, bf16[2,64,2,128]{3,2,1,0:T(2,128)(2,1)S(1)}, u32[]{:S(2)}, u32[]{:S(2)}) collective-permute-start(bf16[2,64,2,128]{3,2,1,0:T(2,128)(2,1)S(1)} %pad_maximum_fusion.refs_0_), channel_id=1, source_target_pairs={{0,7},{1,6},{2,5},{3,4},{4,3},{5,2},{6,1},{7,0},{8,15},{9,14},{10,... | collective-permute-start | bytes 196616 | tf_op jit(solution)/shard_map/ppermute | solution.py:162
  9.5 4.1 %collective-permute-start.4 = (bf16[2,64,2,128]{3,2,1,0:T(2,128)(2,1)S(1)}, bf16[2,64,2,128]{3,2,1,0:T(2,128)(2,1)S(1)}, u32[]{:S(2)}, u32[]{:S(2)}) collective-permute-start(bf16[2,64,2,128]{3,2,1,0:T(2,128)(2,1)S(1)} %pad_maximum_fusion.refs_0_), channel_id=1, source_target_pairs={{0,5},{1,4},{2,7},{3,6},{4,1},{5,0},{6,3},{7,2},{8,13},{9,12},{10,... | collective-permute-start | bytes 196616 | tf_op jit(solution)/shard_map/ppermute | solution.py:162
  10.0 4.1 %collective-permute-start.5 = (bf16[2,64,2,128]{3,2,1,0:T(2,128)(2,1)S(1)}, bf16[2,64,2,128]{3,2,1,0:T(2,128)(2,1)S(1)}, u32[]{:S(2)}, u32[]{:S(2)}) collective-permute-start(bf16[2,64,2,128]{3,2,1,0:T(2,128)(2,1)S(1)} %pad_maximum_fusion.refs_0_), channel_id=1, source_target_pairs={{0,3},{1,2},{2,1},{3,0},{4,7},{5,6},{6,5},{7,4},{8,11},{9,10},{10,... | collective-permute-start | bytes 196616 | tf_op jit(solution)/shard_map/ppermute | solution.py:162
  12.0 2.1 %collective-permute-start.2 = (bf16[2,64,2,128]{3,2,1,0:T(2,128)(2,1)S(1)}, bf16[2,64,2,128]{3,2,1,0:T(2,128)(2,1)S(1)}, u32[]{:S(2)}, u32[]{:S(2)}) collective-permute-start(bf16[2,64,2,128]{3,2,1,0:T(2,128)(2,1)S(1)} %pad_maximum_fusion.refs_0_), channel_id=1, source_target_pairs={{0,1},{1,0},{2,3},{3,2},{4,5},{5,4},{6,7},{7,6},{8,9},{9,8},{10,11... | collective-permute-start | bytes 196616 | tf_op jit(solution)/shard_map/ppermute | solution.py:162
  12.0 2.1 %collective-permute-start.3 = (bf16[2,64,2,128]{3,2,1,0:T(2,128)(2,1)S(1)}, bf16[2,64,2,128]{3,2,1,0:T(2,128)(2,1)S(1)}, u32[]{:S(2)}, u32[]{:S(2)}) collective-permute-start(bf16[2,64,2,128]{3,2,1,0:T(2,128)(2,1)S(1)} %collective-permute-done.1.refs_2_), channel_id=1, source_target_pairs={{0,1},{1,0},{2,3},{3,2},{4,5},{5,4},{6,7},{7,6},{8,9},{9,8},{10,11... | collective-permute-start | bytes 196616 | tf_op jit(solution)/shard_map/ppermute | solution.py:162
  14.2 1.4 %collective-permute-start.6 = (bf16[4,64,2,128]{3,2,1,0:T(2,128)(2,1)S(1)}, bf16[4,64,2,128]{3,2,1,0:T(2,128)(2,1)S(1)}, u32[]{:S(2)}, u32[]{:S(2)}) collective-permute-start(bf16[4,64,2,128]{3,2,1,0:T(2,128)(2,1)S(1)} %constant_dynamic-update-slice_fusion.refs_4_), channel_id=1, source_target_pairs={{0,1},{1,0},{2,3},{3,2},{4,5},{5,4},{6,7},{7,6},{8,9},{9,8},{10,11... | collective-permute-start | bytes 393224 | tf_op jit(solution)/shard_map/ppermute | solution.py:162
  17.0 4.5 %collective-permute-start.7 = (bf16[1,128,128]{2,1,0:T(8,128)(2,1)S(1)}, bf16[1,128,128]{2,1,0:T(8,128)(2,1)S(1)}, u32[]{:S(2)}, u32[]{:S(2)}) collective-permute-start(bf16[1,128,128]{2,1,0:T(8,128)(2,1)S(1)} %bitcast.5), channel_id=1, source_target_pairs={{0,9},{1,8},{2,11},{3,10},{4,13},{5,12},{6,15},{7,14},{8,1},{9,0},... | collective-permute-start | bytes 98312 | tf_op jit(solution)/shard_map/ppermute | solution.py:162
  21.5 7.4 %copy-start.3 = (s32[512]{0:T(512)S(1)}, s32[512]{0:T(512)}, u32[]{:S(2)}) copy-start(s32[512]{0:T(512)} %param.10) | copy-start | bytes 6148
  21.5 7.4 %copy-start.4 = (f32[16]{0:T(128)S(1)}, f32[16]{0:T(128)}, u32[]{:S(2)}) copy-start(f32[16]{0:T(128)} %param.11) | copy-start | bytes 196
  21.5 5.3 %collective-permute-start.10 = (bf16[2,128,128]{2,1,0:T(8,128)(2,1)S(1)}, bf16[2,128,128]{2,1,0:T(8,128)(2,1)S(1)}, u32[]{:S(2)}, u32[]{:S(2)}) collective-permute-start(bf16[2,128,128]{2,1,0:T(8,128)(2,1)S(1)} %pad_maximum_fusion.1.refs_0_), channel_id=1, source_target_pairs={{0,7},{1,6},{2,5},{3,4},{4,3},{5,2},{6,1},{7,0},{8,15},{9,14},{10,... | collective-permute-start | bytes 196616 | tf_op jit(solution)/shard_map/ppermute | solution.py:162
  24.4 2.4 %collective-permute-start.11 = (bf16[2,128,128]{2,1,0:T(8,128)(2,1)S(1)}, bf16[2,128,128]{2,1,0:T(8,128)(2,1)S(1)}, u32[]{:S(2)}, u32[]{:S(2)}) collective-permute-start(bf16[2,128,128]{2,1,0:T(8,128)(2,1)S(1)} %pad_maximum_fusion.1.refs_0_), channel_id=1, source_target_pairs={{0,1},{1,0},{2,3},{3,2},{4,5},{5,4},{6,7},{7,6},{8,9},{9,8},{10,11... | collective-permute-start | bytes 196616 | tf_op jit(solution)/shard_map/ppermute | solution.py:162
  24.6 4.0 %collective-permute-start.8 = (bf16[2,128,128]{2,1,0:T(8,128)(2,1)S(1)}, bf16[2,128,128]{2,1,0:T(8,128)(2,1)S(1)}, u32[]{:S(2)}, u32[]{:S(2)}) collective-permute-start(bf16[2,128,128]{2,1,0:T(8,128)(2,1)S(1)} %pad_maximum_fusion.1.refs_0_), channel_id=1, source_target_pairs={{0,5},{1,4},{2,7},{3,6},{4,1},{5,0},{6,3},{7,2},{8,13},{9,12},{10,... | collective-permute-start | bytes 196616 | tf_op jit(solution)/shard_map/ppermute | solution.py:162
  24.6 4.0 %collective-permute-start.9 = (bf16[2,128,128]{2,1,0:T(8,128)(2,1)S(1)}, bf16[2,128,128]{2,1,0:T(8,128)(2,1)S(1)}, u32[]{:S(2)}, u32[]{:S(2)}) collective-permute-start(bf16[2,128,128]{2,1,0:T(8,128)(2,1)S(1)} %pad_maximum_fusion.1.refs_0_), channel_id=1, source_target_pairs={{0,3},{1,2},{2,1},{3,0},{4,7},{5,6},{6,5},{7,4},{8,11},{9,10},{10,... | collective-permute-start | bytes 196616 | tf_op jit(solution)/shard_map/ppermute | solution.py:162
  26.8 1.8 %collective-permute-start.12 = (bf16[2,128,128]{2,1,0:T(8,128)(2,1)S(1)}, bf16[2,128,128]{2,1,0:T(8,128)(2,1)S(1)}, u32[]{:S(2)}, u32[]{:S(2)}) collective-permute-start(bf16[2,128,128]{2,1,0:T(8,128)(2,1)S(1)} %collective-permute-done.10.refs_2_), channel_id=1, source_target_pairs={{0,1},{1,0},{2,3},{3,2},{4,5},{5,4},{6,7},{7,6},{8,9},{9,8},{10,11... | collective-permute-start | bytes 196616 | tf_op jit(solution)/shard_map/ppermute | solution.py:162
  28.6 1.5 %collective-permute-start.13 = (bf16[4,128,128]{2,1,0:T(8,128)(2,1)S(1)}, bf16[4,128,128]{2,1,0:T(8,128)(2,1)S(1)}, u32[]{:S(2)}, u32[]{:S(2)}) collective-permute-start(bf16[4,128,128]{2,1,0:T(8,128)(2,1)S(1)} %constant_dynamic-update-slice_fusion.2.refs_1_), channel_id=1, source_target_pairs={{0,1},{1,0},{2,3},{3,2},{4,5},{5,4},{6,7},{7,6},{8,9},{9,8},{10,11... | collective-permute-start | bytes 393224 | tf_op jit(solution)/shard_map/ppermute | solution.py:162

commit v11 on v9

--- a/solution.py
+++ b/solution.py
@@ -391,7 +391,10 @@
             FIRST,
             lambda share: [keep("fisher", load_whole(inv_fisher, share))],
             lambda got: [load(0, homes[0], got["own"])],
-            lambda got: [load(1, homes[1], got["one"])],
+            lambda got: [],
+        )
+        got["core_last"], ready[1] = lax.optimization_barrier(
+            (got["core_last"], load(1, homes[1], got["last"]))
         )
         hidden = fisher_call(got, ready["fisher"], size)
 

time: 31.9 us -> 31.8 us (level)
  transfers between devices with their start and end apart: 14 -> 14, of which waited for: 6 -> 7; matrix products, arithmetic and copies ran while one was open for 0% -> 0% of each run, Pallas kernels for 23% -> 23%
where the time goes in v11:
time: 31.8 us; the launch traced here: 31.6 us
  starting transfers between devices  14.7 us (46%)
  Pallas kernels  10.5 us (33%)
  waiting for transfers between devices  5.13 us (16%)
  local copies, waits for them, and re-layouts  0.98 us (3%)
    ppermute x14, starting transfers between devices, send(): return lax.ppermute(value, 'blk', pairs)  14.7 us
    ppermute x14, waiting for transfers between devices, send(): return lax.ppermute(value, 'blk', pairs)  5.13 us
    pallas_call x4, Pallas kernels, load_store(): pl.pallas_call(functools.partial(load_kernel, size, names), out_shape=jax...  4.43 us
    pallas_call x3, Pallas kernels, partial_call(): pl.pallas_call(functools.partial(partial_kernel, tuple(starts)), out_shap...  2.42 us
    pallas_call x1, Pallas kernels, score_call(): pl.pallas_call(functools.partial(score_kernel, queries, start), out_shape...  1.61 us
    pallas_call x1, Pallas kernels, fisher_call(): pl.pallas_call(functools.partial(fisher_kernel, size), out_shape=jax.Shap...  1.36 us
    unnamed x16, local copies, waits for them, and re-layouts  0.91 us
  transfers between devices with their start and end apart: 14, of which 7 were waited for; matrix products, arithmetic and copies ran while one was open for 0% of the time, Pallas kernels for 23%

profile of v11, /device:TPU:0, one launch (start us, length us, event | category | flops | bytes accessed | tf_op | source)
XLA Modules:
  0.0 31.6 jit_solution(145860597622457903)
XLA Ops:
  0.0 0.8 %copy-done.1 = bf16[2,2,64,128]{3,2,1,0:T(8,128)(2,1)S(1)} copy-done((bf16[2,2,64,128]{3,2,1,0:T(8,128)(2,1)S(1)}, bf16[2,2,64,128]{3,2,1,0:T(8,128)(2,1)}, u32[]{:S(2)}) %copy-start.1) | copy-done | bytes 65560
  0.8 0.3 %shard_map.65 = bf16[64,2,128]{2,1,0:T(2,128)(2,1)S(1)} custom-call(bf16[2,2,64,128]{3,2,1,0:T(8,128)(2,1)S(1)} %copy-done.1, s32[2,64]{1,0:T(2,128)S(1)} %copy-done.2, f32[64,64]{1,0:T(8,128)S(1)} %shard_map.64.zeros_ref), custom_call_target="tpu_custom_call" | custom-call | flops 10000000000 | tf_op jit(solution)/shard_map/pallas_call | solution.py:93
  1.2 3.5 %collective-permute-start = (bf16[1,64,2,128]{3,2,1,0:T(2,128)(2,1)S(1)}, bf16[1,64,2,128]{3,2,1,0:T(2,128)(2,1)S(1)}, u32[]{:S(2)}, u32[]{:S(2)}) collective-permute-start(bf16[1,64,2,128]{3,2,1,0:T(2,128)(2,1)S(1)} %bitcast.7), channel_id=1, source_target_pairs={{0,9},{1,8},{2,11},{3,10},{4,13},{5,12},{6,15},{7,14},{8,1},{9,0},... | collective-permute-start | bytes 98312 | tf_op jit(solution)/shard_map/ppermute | solution.py:162
  4.7 0.3 shard_map.66.refs_6_
  5.0 1.5 %collective-permute-done = bf16[1,64,2,128]{3,2,1,0:T(2,128)(2,1)S(1)} collective-permute-done((bf16[1,64,2,128]{3,2,1,0:T(2,128)(2,1)S(1)}, bf16[1,64,2,128]{3,2,1,0:T(2,128)(2,1)S(1)}, u32[]{:S(2)}, u32[]{:S(2)}) %collective-permute-start) | collective-permute-done | bytes 32800 | tf_op jit(solution)/shard_map/ppermute | solution.py:162
  6.5 0.1 pad_maximum_fusion.refs_0_
  6.6 2.9 %collective-permute-start.1 = (bf16[2,64,2,128]{3,2,1,0:T(2,128)(2,1)S(1)}, bf16[2,64,2,128]{3,2,1,0:T(2,128)(2,1)S(1)}, u32[]{:S(2)}, u32[]{:S(2)}) collective-permute-start(bf16[2,64,2,128]{3,2,1,0:T(2,128)(2,1)S(1)} %pad_maximum_fusion.refs_0_), channel_id=1, source_target_pairs={{0,7},{1,6},{2,5},{3,4},{4,3},{5,2},{6,1},{7,0},{8,15},{9,14},{10,... | collective-permute-start | bytes 196616 | tf_op jit(solution)/shard_map/ppermute | solution.py:162
  9.5 0.5 %collective-permute-start.4 = (bf16[2,64,2,128]{3,2,1,0:T(2,128)(2,1)S(1)}, bf16[2,64,2,128]{3,2,1,0:T(2,128)(2,1)S(1)}, u32[]{:S(2)}, u32[]{:S(2)}) collective-permute-start(bf16[2,64,2,128]{3,2,1,0:T(2,128)(2,1)S(1)} %pad_maximum_fusion.refs_0_), channel_id=1, source_target_pairs={{0,5},{1,4},{2,7},{3,6},{4,1},{5,0},{6,3},{7,2},{8,13},{9,12},{10,... | collective-permute-start | bytes 196616 | tf_op jit(solution)/shard_map/ppermute | solution.py:162
  10.0 0.2 collective-permute-start.5
  10.2 1.1 %shard_map.67.refs_2_.refs_3_ = bf16[4,512,2,256]{3,2,1,0:T(2,128)(2,1)S(1)} custom-call(bf16[512,2,4096]{2,1,0:T(2,128)(2,1)S(1)} %bitcast.4), custom_call_target="tpu_custom_call" | custom-call | bytes 2097152 | tf_op jit(solution)/shard_map/pallas_call | solution.py:126
  11.3 0.7 %collective-permute-done.1.refs_2_ = bf16[2,64,2,128]{3,2,1,0:T(2,128)(2,1)S(1)} collective-permute-done((bf16[2,64,2,128]{3,2,1,0:T(2,128)(2,1)S(1)}, bf16[2,64,2,128]{3,2,1,0:T(2,128)(2,1)S(1)}, u32[]{:S(2)}, u32[]{:S(2)}) %collective-permute-start.1) | collective-permute-done | bytes 65568 | tf_op jit(solution)/shard_map/ppermute | solution.py:162
  12.0 0.5 %collective-permute-start.3 = (bf16[2,64,2,128]{3,2,1,0:T(2,128)(2,1)S(1)}, bf16[2,64,2,128]{3,2,1,0:T(2,128)(2,1)S(1)}, u32[]{:S(2)}, u32[]{:S(2)}) collective-permute-start(bf16[2,64,2,128]{3,2,1,0:T(2,128)(2,1)S(1)} %collective-permute-done.1.refs_2_), channel_id=1, source_target_pairs={{0,1},{1,0},{2,3},{3,2},{4,5},{5,4},{6,7},{7,6},{8,9},{9,8},{10,11... | collective-permute-start | bytes 196616 | tf_op jit(solution)/shard_map/ppermute | solution.py:162
  12.5 1.1 %collective-permute-done.4 = bf16[2,64,2,128]{3,2,1,0:T(2,128)(2,1)S(1)} collective-permute-done((bf16[2,64,2,128]{3,2,1,0:T(2,128)(2,1)S(1)}, bf16[2,64,2,128]{3,2,1,0:T(2,128)(2,1)S(1)}, u32[]{:S(2)}, u32[]{:S(2)}) %collective-permute-start.4) | collective-permute-done | bytes 65568 | tf_op jit(solution)/shard_map/ppermute | solution.py:162
  13.5 0.6 %collective-permute-done.5 = bf16[2,64,2,128]{3,2,1,0:T(2,128)(2,1)S(1)} collective-permute-done((bf16[2,64,2,128]{3,2,1,0:T(2,128)(2,1)S(1)}, bf16[2,64,2,128]{3,2,1,0:T(2,128)(2,1)S(1)}, u32[]{:S(2)}, u32[]{:S(2)}) %collective-permute-start.5) | collective-permute-done | bytes 65568 | tf_op jit(solution)/shard_map/ppermute | solution.py:162
  14.2 0.2 collective-permute-start.6
  14.4 1.1 %shard_map.68.refs_1_.refs_2_ = bf16[4,512,2,256]{3,2,1,0:T(2,128)(2,1)S(1)} custom-call(bf16[512,2,4096]{2,1,0:T(2,128)(2,1)S(1)} %bitcast.4), custom_call_target="tpu_custom_call" | custom-call | bytes 2097152 | tf_op jit(solution)/shard_map/pallas_call | solution.py:126
  15.5 0.1 collective-permute-done.6.refs_5_
  15.6 1.4 %shard_map.69 = bf16[128,128]{1,0:T(8,128)(2,1)S(1)} custom-call(bf16[2,64,2,128]{3,2,1,0:T(2,128)(2,1)S(1)} %pad_maximum_fusion.refs_0_, bf16[2,64,2,128]{3,2,1,0:T(2,128)(2,1)S(1)} %collective-permute-done.2.refs_1_, bf16[2,64,2,128]{3,2,1,0:T(2,128)(2,1)S(1)} %collective-permute-done.1.refs_2_, ...), custom_call_target="tpu_custom_call" | custom-call | tf_op jit(solution)/shard_map/pallas_call | solution.py:257
  17.0 2.7 %collective-permute-start.7 = (bf16[1,128,128]{2,1,0:T(8,128)(2,1)S(1)}, bf16[1,128,128]{2,1,0:T(8,128)(2,1)S(1)}, u32[]{:S(2)}, u32[]{:S(2)}) collective-permute-start(bf16[1,128,128]{2,1,0:T(8,128)(2,1)S(1)} %bitcast.5), channel_id=1, source_target_pairs={{0,9},{1,8},{2,11},{3,10},{4,13},{5,12},{6,15},{7,14},{8,1},{9,0},... | collective-permute-start | bytes 98312 | tf_op jit(solution)/shard_map/ppermute | solution.py:162
  19.7 1.1 %shard_map.70.refs_3_ = bf16[4,512,2,256]{3,2,1,0:T(2,128)(2,1)S(1)} custom-call(bf16[512,2,4096]{2,1,0:T(2,128)(2,1)S(1)} %bitcast.4), custom_call_target="tpu_custom_call" | custom-call | bytes 2097152 | tf_op jit(solution)/shard_map/pallas_call | solution.py:126
  20.8 0.5 %collective-permute-done.7 = bf16[1,128,128]{2,1,0:T(8,128)(2,1)S(1)} collective-permute-done((bf16[1,128,128]{2,1,0:T(8,128)(2,1)S(1)}, bf16[1,128,128]{2,1,0:T(8,128)(2,1)S(1)}, u32[]{:S(2)}, u32[]{:S(2)}) %collective-permute-start.7) | collective-permute-done | bytes 32800 | tf_op jit(solution)/shard_map/ppermute | solution.py:162
  21.3 0.4 %collective-permute-start.11 = (bf16[2,128,128]{2,1,0:T(8,128)(2,1)S(1)}, bf16[2,128,128]{2,1,0:T(8,128)(2,1)S(1)}, u32[]{:S(2)}, u32[]{:S(2)}) collective-permute-start(bf16[2,128,128]{2,1,0:T(8,128)(2,1)S(1)} %pad_maximum_fusion.1.refs_0_), channel_id=1, source_target_pairs={{0,1},{1,0},{2,3},{3,2},{4,5},{5,4},{6,7},{7,6},{8,9},{9,8},{10,11... | collective-permute-start | bytes 196616 | tf_op jit(solution)/shard_map/ppermute | solution.py:162
  21.7 2.8 %collective-permute-start.10 = (bf16[2,128,128]{2,1,0:T(8,128)(2,1)S(1)}, bf16[2,128,128]{2,1,0:T(8,128)(2,1)S(1)}, u32[]{:S(2)}, u32[]{:S(2)}) collective-permute-start(bf16[2,128,128]{2,1,0:T(8,128)(2,1)S(1)} %pad_maximum_fusion.1.refs_0_), channel_id=1, source_target_pairs={{0,7},{1,6},{2,5},{3,4},{4,3},{5,2},{6,1},{7,0},{8,15},{9,14},{10,... | collective-permute-start | bytes 196616 | tf_op jit(solution)/shard_map/ppermute | solution.py:162
  24.5 0.5 %collective-permute-start.9 = (bf16[2,128,128]{2,1,0:T(8,128)(2,1)S(1)}, bf16[2,128,128]{2,1,0:T(8,128)(2,1)S(1)}, u32[]{:S(2)}, u32[]{:S(2)}) collective-permute-start(bf16[2,128,128]{2,1,0:T(8,128)(2,1)S(1)} %pad_maximum_fusion.1.refs_0_), channel_id=1, source_target_pairs={{0,3},{1,2},{2,1},{3,0},{4,7},{5,6},{6,5},{7,4},{8,11},{9,10},{10,... | collective-permute-start | bytes 196616 | tf_op jit(solution)/shard_map/ppermute | solution.py:162
  25.0 1.1 %shard_map.72.refs_1_ = bf16[4,512,2,256]{3,2,1,0:T(2,128)(2,1)S(1)} custom-call(bf16[512,2,4096]{2,1,0:T(2,128)(2,1)S(1)} %bitcast.4), custom_call_target="tpu_custom_call" | custom-call | bytes 2097152 | tf_op jit(solution)/shard_map/pallas_call | solution.py:126
  26.1 0.8 %shard_map.71.refs_2_ = f32[1024,128]{1,0:T(8,128)S(1)} custom-call(bf16[2,128,128]{2,1,0:T(8,128)(2,1)S(1)} %pad_maximum_fusion.1.refs_0_, bf16[2,128,128]{2,1,0:T(8,128)(2,1)S(1)} %collective-permute-done.11.refs_1_, bf16[4,512,2,256]{3,2,1,0:T(2,128)(2,1)S(1)} %shard_map.67.refs_2_.refs_3_, bf16[4,512,2,256]{3,2,1,0:T(2,128)(2,1)S(1)} %shard_map.67.refs_2_.refs_3_), custom_call_target="tpu_custom_call" | custom-call | tf_op jit(solution)/shard_map/pallas_call | solution.py:302
  27.0 0.4 %collective-permute-start.12 = (bf16[2,128,128]{2,1,0:T(8,128)(2,1)S(1)}, bf16[2,128,128]{2,1,0:T(8,128)(2,1)S(1)}, u32[]{:S(2)}, u32[]{:S(2)}) collective-permute-start(bf16[2,128,128]{2,1,0:T(8,128)(2,1)S(1)} %collective-permute-done.10.refs_0_), channel_id=1, source_target_pairs={{0,1},{1,0},{2,3},{3,2},{4,5},{5,4},{6,7},{7,6},{8,9},{9,8},{10,11... | collective-permute-start | bytes 196616 | tf_op jit(solution)/shard_map/ppermute | solution.py:162
  27.3 0.5 %shard_map.73.refs_4_ = f32[1024,128]{1,0:T(8,128)S(1)} custom-call(bf16[2,128,128]{2,1,0:T(8,128)(2,1)S(1)} %collective-permute-done.10.refs_0_, bf16[4,512,2,256]{3,2,1,0:T(2,128)(2,1)S(1)} %shard_map.68.refs_1_.refs_2_, f32[1024,128]{1,0:T(8,128)S(1)} %shard_map.71.refs_2_), custom_call_target="tpu_custom_call" | custom-call | tf_op jit(solution)/shard_map/pallas_call | solution.py:302
  27.8 0.7 %collective-permute-done.8 = bf16[2,128,128]{2,1,0:T(8,128)(2,1)S(1)} collective-permute-done((bf16[2,128,128]{2,1,0:T(8,128)(2,1)S(1)}, bf16[2,128,128]{2,1,0:T(8,128)(2,1)S(1)}, u32[]{:S(2)}, u32[]{:S(2)}) %collective-permute-start.8) | collective-permute-done | bytes 65568 | tf_op jit(solution)/shard_map/ppermute | solution.py:162
  28.6 0.2 collective-permute-start.13
  28.9 1.1 %shard_map.74.refs_2_ = f32[1024,128]{1,0:T(8,128)S(1)} custom-call(bf16[2,128,128]{2,1,0:T(8,128)(2,1)S(1)} %collective-permute-done.12.refs_0_, bf16[4,128,128]{2,1,0:T(8,128)(2,1)S(1)} %constant_dynamic-update-slice_fusion.2.refs_1_, bf16[4,512,2,256]{3,2,1,0:T(2,128)(2,1)S(1)} %shard_map.68.refs_1_.refs_2_, ...), custom_call_target="tpu_custom_call" | custom-call | tf_op jit(solution)/shard_map/pallas_call | solution.py:302
  30.0 1.6 %shard_map.75 = f32[32,512]{1,0:T(8,128)} custom-call(bf16[4,128,128]{2,1,0:T(8,128)(2,1)S(1)} %collective-permute-done.13.refs_0_, bf16[4,512,2,256]{3,2,1,0:T(2,128)(2,1)S(1)} %shard_map.72.refs_1_, f32[1024,128]{1,0:T(8,128)S(1)} %shard_map.74.refs_2_, f32[1,512]{1,0:T(1,128)S(1)} %bitcast.9), custom_call_target="tpu_custom_call" | custom-call | tf_op jit(solution)/shard_map/pallas_call | solution.py:331
  (30 shorter events, 0.3 us)
Async XLA Ops:
  0.0 0.8 %copy-start.1 = (bf16[2,2,64,128]{3,2,1,0:T(8,128)(2,1)S(1)}, bf16[2,2,64,128]{3,2,1,0:T(8,128)(2,1)}, u32[]{:S(2)}) copy-start(bf16[2,2,64,128]{3,2,1,0:T(8,128)(2,1)} %factors_ref.1) | copy-start | bytes 196612
  0.0 0.8 %copy-start.2 = (s32[2,64]{1,0:T(2,128)S(1)}, s32[2,64]{1,0:T(2,128)}, u32[]{:S(2)}) copy-start(s32[2,64]{1,0:T(2,128)} %mask_ref.1) | copy-start | bytes 1540
  0.0 10.1 %slice-start = ((s8[8388608]{0:T(1024)(128)(4,1)}), s8[4194304]{0:T(1024)(128)(4,1)S(1)}, s32[]{:S(2)}) async-start(s8[8388608]{0:T(1024)(128)(4,1)} %bitcast.3), calls=%async_computation | async-start | bytes 8388608
  0.8 3.9 %copy-start = (bf16[2,256,4096]{2,1,0:T(8,128)(2,1)S(1)}, bf16[2,256,4096]{2,1,0:T(8,128)(2,1)}, u32[]{:S(2)}) copy-start(bf16[2,256,4096]{2,1,0:T(8,128)(2,1)} %source_ref) | copy-start | bytes 12582916
  0.8 9.3 %slice-start.1 = ((s8[8388608]{0:T(1024)(128)(4,1)}), s8[4194304]{0:T(1024)(128)(4,1)S(1)}, s32[]{:S(2)}) async-start(s8[8388608]{0:T(1024)(128)(4,1)} %bitcast.3), calls=%async_computation.1 | async-start | bytes 8388608
  1.2 5.3 %collective-permute-start = (bf16[1,64,2,128]{3,2,1,0:T(2,128)(2,1)S(1)}, bf16[1,64,2,128]{3,2,1,0:T(2,128)(2,1)S(1)}, u32[]{:S(2)}, u32[]{:S(2)}) collective-permute-start(bf16[1,64,2,128]{3,2,1,0:T(2,128)(2,1)S(1)} %bitcast.7), channel_id=1, source_target_pairs={{0,9},{1,8},{2,11},{3,10},{4,13},{5,12},{6,15},{7,14},{8,1},{9,0},... | collective-permute-start | bytes 98312 | tf_op jit(solution)/shard_map/ppermute | solution.py:162
  6.6 5.3 %collective-permute-start.1 = (bf16[2,64,2,128]{3,2,1,0:T(2,128)(2,1)S(1)}, bf16[2,64,2,128]{3,2,1,0:T(2,128)(2,1)S(1)}, u32[]{:S(2)}, u32[]{:S(2)}) collective-permute-start(bf16[2,64,2,128]{3,2,1,0:T(2,128)(2,1)S(1)} %pad_maximum_fusion.refs_0_), channel_id=1, source_target_pairs={{0,7},{1,6},{2,5},{3,4},{4,3},{5,2},{6,1},{7,0},{8,15},{9,14},{10,... | collective-permute-start | bytes 196616 | tf_op jit(solution)/shard_map/ppermute | solution.py:162
  9.5 4.1 %collective-permute-start.4 = (bf16[2,64,2,128]{3,2,1,0:T(2,128)(2,1)S(1)}, bf16[2,64,2,128]{3,2,1,0:T(2,128)(2,1)S(1)}, u32[]{:S(2)}, u32[]{:S(2)}) collective-permute-start(bf16[2,64,2,128]{3,2,1,0:T(2,128)(2,1)S(1)} %pad_maximum_fusion.refs_0_), channel_id=1, source_target_pairs={{0,5},{1,4},{2,7},{3,6},{4,1},{5,0},{6,3},{7,2},{8,13},{9,12},{10,... | collective-permute-start | bytes 196616 | tf_op jit(solution)/shard_map/ppermute | solution.py:162
  10.0 4.1 %collective-permute-start.5 = (bf16[2,64,2,128]{3,2,1,0:T(2,128)(2,1)S(1)}, bf16[2,64,2,128]{3,2,1,0:T(2,128)(2,1)S(1)}, u32[]{:S(2)}, u32[]{:S(2)}) collective-permute-start(bf16[2,64,2,128]{3,2,1,0:T(2,128)(2,1)S(1)} %pad_maximum_fusion.refs_0_), channel_id=1, source_target_pairs={{0,3},{1,2},{2,1},{3,0},{4,7},{5,6},{6,5},{7,4},{8,11},{9,10},{10,... | collective-permute-start | bytes 196616 | tf_op jit(solution)/shard_map/ppermute | solution.py:162
  12.0 2.1 %collective-permute-start.2 = (bf16[2,64,2,128]{3,2,1,0:T(2,128)(2,1)S(1)}, bf16[2,64,2,128]{3,2,1,0:T(2,128)(2,1)S(1)}, u32[]{:S(2)}, u32[]{:S(2)}) collective-permute-start(bf16[2,64,2,128]{3,2,1,0:T(2,128)(2,1)S(1)} %pad_maximum_fusion.refs_0_), channel_id=1, source_target_pairs={{0,1},{1,0},{2,3},{3,2},{4,5},{5,4},{6,7},{7,6},{8,9},{9,8},{10,11... | collective-permute-start | bytes 196616 | tf_op jit(solution)/shard_map/ppermute | solution.py:162
  12.0 2.1 %collective-permute-start.3 = (bf16[2,64,2,128]{3,2,1,0:T(2,128)(2,1)S(1)}, bf16[2,64,2,128]{3,2,1,0:T(2,128)(2,1)S(1)}, u32[]{:S(2)}, u32[]{:S(2)}) collective-permute-start(bf16[2,64,2,128]{3,2,1,0:T(2,128)(2,1)S(1)} %collective-permute-done.1.refs_2_), channel_id=1, source_target_pairs={{0,1},{1,0},{2,3},{3,2},{4,5},{5,4},{6,7},{7,6},{8,9},{9,8},{10,11... | collective-permute-start | bytes 196616 | tf_op jit(solution)/shard_map/ppermute | solution.py:162
  14.2 1.4 %collective-permute-start.6 = (bf16[4,64,2,128]{3,2,1,0:T(2,128)(2,1)S(1)}, bf16[4,64,2,128]{3,2,1,0:T(2,128)(2,1)S(1)}, u32[]{:S(2)}, u32[]{:S(2)}) collective-permute-start(bf16[4,64,2,128]{3,2,1,0:T(2,128)(2,1)S(1)} %constant_dynamic-update-slice_fusion.refs_4_), channel_id=1, source_target_pairs={{0,1},{1,0},{2,3},{3,2},{4,5},{5,4},{6,7},{7,6},{8,9},{9,8},{10,11... | collective-permute-start | bytes 393224 | tf_op jit(solution)/shard_map/ppermute | solution.py:162
  17.0 4.3 %collective-permute-start.7 = (bf16[1,128,128]{2,1,0:T(8,128)(2,1)S(1)}, bf16[1,128,128]{2,1,0:T(8,128)(2,1)S(1)}, u32[]{:S(2)}, u32[]{:S(2)}) collective-permute-start(bf16[1,128,128]{2,1,0:T(8,128)(2,1)S(1)} %bitcast.5), channel_id=1, source_target_pairs={{0,9},{1,8},{2,11},{3,10},{4,13},{5,12},{6,15},{7,14},{8,1},{9,0},... | collective-permute-start | bytes 98312 | tf_op jit(solution)/shard_map/ppermute | solution.py:162
  21.3 3.7 %collective-permute-start.11 = (bf16[2,128,128]{2,1,0:T(8,128)(2,1)S(1)}, bf16[2,128,128]{2,1,0:T(8,128)(2,1)S(1)}, u32[]{:S(2)}, u32[]{:S(2)}) collective-permute-start(bf16[2,128,128]{2,1,0:T(8,128)(2,1)S(1)} %pad_maximum_fusion.1.refs_0_), channel_id=1, source_target_pairs={{0,1},{1,0},{2,3},{3,2},{4,5},{5,4},{6,7},{7,6},{8,9},{9,8},{10,11... | collective-permute-start | bytes 196616 | tf_op jit(solution)/shard_map/ppermute | solution.py:162
  21.7 5.3 %collective-permute-start.10 = (bf16[2,128,128]{2,1,0:T(8,128)(2,1)S(1)}, bf16[2,128,128]{2,1,0:T(8,128)(2,1)S(1)}, u32[]{:S(2)}, u32[]{:S(2)}) collective-permute-start(bf16[2,128,128]{2,1,0:T(8,128)(2,1)S(1)} %pad_maximum_fusion.1.refs_0_), channel_id=1, source_target_pairs={{0,7},{1,6},{2,5},{3,4},{4,3},{5,2},{6,1},{7,0},{8,15},{9,14},{10,... | collective-permute-start | bytes 196616 | tf_op jit(solution)/shard_map/ppermute | solution.py:162
  24.5 4.1 %collective-permute-start.8 = (bf16[2,128,128]{2,1,0:T(8,128)(2,1)S(1)}, bf16[2,128,128]{2,1,0:T(8,128)(2,1)S(1)}, u32[]{:S(2)}, u32[]{:S(2)}) collective-permute-start(bf16[2,128,128]{2,1,0:T(8,128)(2,1)S(1)} %pad_maximum_fusion.1.refs_0_), channel_id=1, source_target_pairs={{0,5},{1,4},{2,7},{3,6},{4,1},{5,0},{6,3},{7,2},{8,13},{9,12},{10,... | collective-permute-start | bytes 196616 | tf_op jit(solution)/shard_map/ppermute | solution.py:162
  24.5 4.1 %collective-permute-start.9 = (bf16[2,128,128]{2,1,0:T(8,128)(2,1)S(1)}, bf16[2,128,128]{2,1,0:T(8,128)(2,1)S(1)}, u32[]{:S(2)}, u32[]{:S(2)}) collective-permute-start(bf16[2,128,128]{2,1,0:T(8,128)(2,1)S(1)} %pad_maximum_fusion.1.refs_0_), channel_id=1, source_target_pairs={{0,3},{1,2},{2,1},{3,0},{4,7},{5,6},{6,5},{7,4},{8,11},{9,10},{10,... | collective-permute-start | bytes 196616 | tf_op jit(solution)/shard_map/ppermute | solution.py:162
  27.0 1.9 %copy-start.3 = (s32[512]{0:T(512)S(1)}, s32[512]{0:T(512)}, u32[]{:S(2)}) copy-start(s32[512]{0:T(512)} %param.10) | copy-start | bytes 6148
  27.0 1.8 %copy-start.4 = (f32[16]{0:T(128)S(1)}, f32[16]{0:T(128)}, u32[]{:S(2)}) copy-start(f32[16]{0:T(128)} %param.11) | copy-start | bytes 196
  27.0 1.6 %collective-permute-start.12 = (bf16[2,128,128]{2,1,0:T(8,128)(2,1)S(1)}, bf16[2,128,128]{2,1,0:T(8,128)(2,1)S(1)}, u32[]{:S(2)}, u32[]{:S(2)}) collective-permute-start(bf16[2,128,128]{2,1,0:T(8,128)(2,1)S(1)} %collective-permute-done.10.refs_0_), channel_id=1, source_target_pairs={{0,1},{1,0},{2,3},{3,2},{4,5},{5,4},{6,7},{7,6},{8,9},{9,8},{10,11... | collective-permute-start | bytes 196616 | tf_op jit(solution)/shard_map/ppermute | solution.py:162
  28.6 1.4 %collective-permute-start.13 = (bf16[4,128,128]{2,1,0:T(8,128)(2,1)S(1)}, bf16[4,128,128]{2,1,0:T(8,128)(2,1)S(1)}, u32[]{:S(2)}, u32[]{:S(2)}) collective-permute-start(bf16[4,128,128]{2,1,0:T(8,128)(2,1)S(1)} %constant_dynamic-update-slice_fusion.2.refs_1_), channel_id=1, source_target_pairs={{0,1},{1,0},{2,3},{3,2},{4,5},{5,4},{6,7},{7,6},{8,9},{9,8},{10,11... | collective-permute-start | bytes 393224 | tf_op jit(solution)/shard_map/ppermute | solution.py:162
